TPU v7x, 32 devices: a whole 2x2x4 slice. The times are simulated.
32 devices in a mesh: seq: 8 (over z, y), batch: 4 (over x, core).
Axes of the slice: x: 2, y: 2, z: 4, core: 2. Of those that a mesh axis runs over, the one named last changes fastest.
Arguments:
- inputs: bfloat16 [16, 1024, 768], P('batch', 'seq'), may hold values from -6 to 6
- cotangent: bfloat16 [16, 1024, 768], P('batch', 'seq'), may hold values from -6 to 6
- doc_lengths: int32 [16, 8], P('batch'), may hold values from 1 to 512, 1024 in all within a row
- qkv_weight: float32 [896, 768], P('seq'), may hold values from -0.3125 to 0.3125
- out_weight: float32 [768, 768], P('seq'), may hold values from -0.625 to 0.625
- up_weight: float32 [3072, 768], P('seq'), may hold values from -0.21875 to 0.21875
- down_weight: float32 [768, 3072], P(None, 'seq'), may hold values from -0.109375 to 0.109375
- vectors: float32 [8576], P('seq'), may hold values from -0.9 to 1.6, as said below
- bases: float32 [4, 768, 768], replicated, may hold values from -1 to 1, as said below
- qkv_first: float32 [896, 768], P('seq'), may hold values from -64 to 64
- out_first: float32 [768, 768], P('seq'), may hold values from -20 to 20
- up_first: float32 [3072, 768], P('seq'), may hold values from -24 to 24
- down_first: float32 [768, 3072], P(None, 'seq'), may hold values from -40 to 40
- vector_first: float32 [8576], P('seq'), may hold values from -64 to 64
- qkv_second: float32 [896, 768], P('seq'), may hold values from 819.2 to 8192
- out_second: float32 [768, 768], P('seq'), may hold values from 81.92 to 1310.72
- up_second: float32 [3072, 768], P('seq'), may hold values from 131.072 to 1966.08
- down_second: float32 [768, 3072], P(None, 'seq'), may hold values from 409.6 to 6553.6
- vector_second: float32 [8576], P('seq'), may hold values from 327.68 to 16384
Outputs:
- outputs: bfloat16 [16, 1024, 768], P('batch', 'seq')
- input_grad: bfloat16 [16, 1024, 768], P('batch', 'seq')
- qkv_grad: float32 [896, 768], P('seq')
- out_grad: float32 [768, 768], P('seq')
- up_grad: float32 [3072, 768], P('seq')
- down_grad: float32 [768, 3072], P(None, 'seq')
- vector_grad: float32 [8576], P('seq')
- qkv_first_new: float32 [896, 768], P('seq')
- out_first_new: float32 [768, 768], P('seq')
- up_first_new: float32 [3072, 768], P('seq')
- down_first_new: float32 [768, 3072], P(None, 'seq')
- vector_first_new: float32 [8576], P('seq')
- qkv_second_new: float32 [896, 768], P('seq')
- out_second_new: float32 [768, 768], P('seq')
- up_second_new: float32 [3072, 768], P('seq')
- down_second_new: float32 [768, 3072], P(None, 'seq')
- vector_second_new: float32 [8576], P('seq')
- qkv_new: float32 [896, 768], P('seq')
- out_new: float32 [768, 768], P('seq')
- up_new: float32 [3072, 768], P('seq')
- down_new: float32 [768, 3072], P(None, 'seq')
- vector_new: float32 [8576], P('seq')
Inputs may be any that keep to these rules, and one draw needn't show every extreme that they name: `doc_lengths`: the 8 lengths of a row sum to 1024, and in every row the longest document has exactly half of 1024 positions. `vectors`: entries 0 to 767 and 1536 to 2303 are the two norms' gains, all others shifts and biases. `bases`: each of the four matrices is orthogonal.
All inputs are finite; a program needn't handle non-finite values.
Results may differ from a plain program's by a relative error of at most 0.006.
The roundings to bfloat16 on the way count: a program that leaves them out, or rounds other values in their place, can miss the bound.
Values may be sent and summed in bfloat16 or wider, within the bound.
No kernel may reach another device: no remote copies, remote signals or barrier semaphores. Data moves between devices by JAX's collectives and lax.ppermute only.
A program may use at most 192 MiB of HBM per device.

v0:
```python
import jax
import jax.numpy as jnp
from jax import lax
from jax.sharding import PartitionSpec as P

D = 768
HEADS = 12
HEAD = 64
ROT = 16
FF = 3072
STEP = 10


layer_eps = 1e-05
adam_eps = 1e-08
beta_first = 0.95
beta_second = 0.95
matrix_rate = 0.08
vector_rate = 0.3
rope_base = 10000.0
masked_score = -1e30


def spread_2(value, axis, root):
    mine = lax.axis_index(axis) == root
    return lax.psum(jnp.where(mine, value, jnp.zeros_like(value)), axis)


def matmul_exact(left, right):
    return jnp.dot(left, right, precision=lax.Precision.HIGHEST, preferred_element_type=jnp.float32)


def layer_norm(values, gain, shift):
    center = values - jnp.mean(values, axis=-1, keepdims=True)
    spread = jnp.mean(center * center, axis=-1, keepdims=True)
    return center * lax.rsqrt(spread + layer_eps) * gain + shift


def split_vectors(vectors):
    widths = [D, D, D, D, D + 2 * HEAD, D, FF, D]
    pieces = []
    offset = 0
    for piece_width in widths:
        pieces.append(vectors[offset : offset + piece_width])
        offset = offset + piece_width
    return pieces


def rotary_tables(offsets):
    freq_steps = jnp.arange(0, ROT, 2).astype(jnp.float32)
    inverse = 1.0 / rope_base ** (freq_steps / ROT)
    angles = offsets.astype(jnp.float32)[..., None] * inverse
    angles = jnp.concatenate([angles, angles], axis=-1)
    return (jnp.cos(angles), jnp.sin(angles))


def rotate(values, cosine, sine):
    turned = values[..., :ROT]
    half_rot = ROT // 2
    swapped = jnp.concatenate([-turned[..., half_rot:], turned[..., :half_rot]], axis=-1)
    return jnp.concatenate([turned * cosine + swapped * sine, values[..., ROT:]], axis=-1)


def doc_layout(lengths, positions):
    starts = jnp.cumsum(lengths) - lengths
    before = starts[None, :] <= positions[:, None]
    doc_ident = jnp.sum(before.astype(jnp.int32), axis=1) - 1
    doc_begin = jnp.max(jnp.where(before, starts[None, :], 0), axis=1)
    return (doc_ident, positions - doc_begin)


def masked_scores(query_rows, key_rows, allowed):
    scores = jnp.einsum(
        "hsd,kd->hsk", query_rows, key_rows, preferred_element_type=jnp.float32
    ) * HEAD ** (-0.5)
    return jnp.where(allowed[None], scores, masked_score)


def attend_forward(query_rows, key_vals, allowed):
    key_rows = key_vals[:, :HEAD]
    value_rows = key_vals[:, HEAD:]
    scores = masked_scores(query_rows, key_rows, allowed)
    row_max = jnp.max(scores, axis=-1, keepdims=True)
    weights = jnp.exp(scores - row_max)
    row_total = jnp.sum(weights, axis=-1, keepdims=True)
    weights_low = (weights / row_total).astype(jnp.bfloat16)
    context = jnp.einsum("hsk,kd->shd", weights_low, value_rows, preferred_element_type=jnp.float32)
    return (context, (row_max + jnp.log(row_total))[..., 0])


def attend_backward(query_rows, key_vals, allowed, log_total, d_context):
    key_rows = key_vals[:, :HEAD]
    value_rows = key_vals[:, HEAD:]
    scores = masked_scores(query_rows, key_rows, allowed)
    weights = jnp.exp(scores - log_total[..., None])
    weights_low = weights.astype(jnp.bfloat16)
    d_weights = jnp.einsum("shd,kd->hsk", d_context, value_rows, preferred_element_type=jnp.float32)
    inner_sum = jnp.sum(weights * d_weights, axis=-1, keepdims=True)
    d_scores = (weights * (d_weights - inner_sum)).astype(jnp.bfloat16)
    d_query = jnp.einsum(
        "hsk,kd->shd", d_scores, key_rows, preferred_element_type=jnp.float32
    ) * HEAD ** (-0.5)
    d_key = jnp.einsum(
        "hsk,hsd->kd", d_scores, query_rows, preferred_element_type=jnp.float32
    ) * HEAD ** (-0.5)
    d_value = jnp.einsum("hsk,shd->kd", weights_low, d_context, preferred_element_type=jnp.float32)
    return (d_query, jnp.concatenate([d_key, d_value], axis=-1))


def soap_step(weight, grad, first, second, basis, on_right):
    if on_right:
        rotated = matmul_exact(grad, basis)
    else:
        rotated = matmul_exact(basis.T, grad)
    new_first = beta_first * first + (1.0 - beta_first) * rotated
    new_second = beta_second * second + (1.0 - beta_second) * rotated * rotated
    ratio = (
        new_first
        / (1.0 - beta_first**STEP)
        / (jnp.sqrt(new_second / (1.0 - beta_second**STEP)) + adam_eps)
    )
    if on_right:
        unrotated = matmul_exact(ratio, basis.T)
    else:
        unrotated = matmul_exact(basis, ratio)
    return (weight - matrix_rate * unrotated, new_first, new_second)


def adam_step(weight, grad, first, second):
    new_first = beta_first * first + (1.0 - beta_first) * grad
    new_second = beta_second * second + (1.0 - beta_second) * grad * grad
    ratio = (
        new_first
        / (1.0 - beta_first**STEP)
        / (jnp.sqrt(new_second / (1.0 - beta_second**STEP)) + adam_eps)
    )
    return (weight - vector_rate * ratio, new_first, new_second)


def owned_update(matrix_slot, weight, grad, first, second, basis, on_right):
    owner_index = matrix_slot % lax.axis_size("batch")

    def compute():
        return soap_step(weight, grad, first, second, basis, on_right)

    def blank_states():
        return (jnp.zeros_like(weight), jnp.zeros_like(first), jnp.zeros_like(second))

    owned_states = lax.cond(lax.axis_index("batch") == owner_index, compute, blank_states)
    return (
        spread_2(owned_states[0], "batch", owner_index),
        spread_2(owned_states[1], "batch", owner_index),
        spread_2(owned_states[2], "batch", owner_index),
    )


def shards(
    inputs,
    cotangent,
    doc_lengths,
    qkv_weight,
    out_weight,
    up_weight,
    down_weight,
    vectors,
    bases,
    qkv_first,
    out_first,
    up_first,
    down_first,
    vector_first,
    qkv_second,
    out_second,
    up_second,
    down_second,
    vector_second,
):
    shard_count = lax.axis_size("seq")
    shard_index = lax.axis_index("seq")
    row_count = inputs.shape[0]
    shard_len = inputs.shape[1]
    total_len = shard_len * shard_count
    token_count = row_count * shard_len
    gathered = (
        lax.all_gather(qkv_weight.astype(jnp.bfloat16), "seq", axis=0, tiled=True),
        lax.all_gather(out_weight.astype(jnp.bfloat16), "seq", axis=0, tiled=True),
        lax.all_gather(up_weight.astype(jnp.bfloat16), "seq", axis=0, tiled=True),
        lax.all_gather(down_weight.astype(jnp.bfloat16), "seq", axis=1, tiled=True),
        lax.all_gather(vectors.astype(jnp.bfloat16), "seq", axis=0, tiled=True),
    )
    qkv_full, out_full, up_full, down_full, vector_full = gathered
    pieces = split_vectors(vector_full.astype(jnp.float32))
    gain_one, shift_one, gain_two, shift_two, qkv_bias, out_bias, up_bias, down_bias = pieces
    query_pos = shard_index * shard_len + jnp.arange(shard_len, dtype=jnp.int32)
    key_pos = jnp.arange(total_len, dtype=jnp.int32)
    query_doc, query_off = jax.vmap(lambda lengths: doc_layout(lengths, query_pos))(doc_lengths)
    key_doc = jax.vmap(lambda lengths: doc_layout(lengths, key_pos)[0])(doc_lengths)
    allowed = (query_doc[:, :, None] == key_doc[:, None, :]) & (
        key_pos[None, None, :] <= query_pos[None, :, None]
    )
    cosine, sine = rotary_tables(query_off)
    head_cos = cosine[:, :, None, :]
    head_sin = sine[:, :, None, :]
    flat_in = inputs.astype(jnp.float32).reshape(token_count, D)
    normed_one = layer_norm(flat_in, gain_one, shift_one)
    normed_two = layer_norm(flat_in, gain_two, shift_two)
    normed_one_low = normed_one.astype(jnp.bfloat16)
    normed_two_low = normed_two.astype(jnp.bfloat16)
    projected = jnp.dot(normed_one_low, qkv_full.T, preferred_element_type=jnp.float32) + qkv_bias
    projected = projected.reshape(row_count, shard_len, D + 2 * HEAD)
    query_raw = projected[..., :D].reshape(row_count, shard_len, HEADS, HEAD)
    key_raw = projected[..., D : D + HEAD]
    queries = rotate(query_raw, head_cos, head_sin)
    key_part = rotate(key_raw, cosine, sine)
    value_part = projected[..., D + HEAD :]
    query_low = jnp.transpose(queries, (0, 2, 1, 3)).astype(jnp.bfloat16)
    local_kv = jnp.concatenate([key_part, value_part], axis=-1).astype(jnp.bfloat16)
    key_vals = lax.all_gather(local_kv, "seq", axis=1, tiled=True)
    hidden = jnp.dot(normed_two_low, up_full.T, preferred_element_type=jnp.float32) + up_bias
    active_low = jax.nn.gelu(hidden, approximate=False).astype(jnp.bfloat16)
    mlp_out = jnp.dot(active_low, down_full.T, preferred_element_type=jnp.float32) + down_bias
    context, log_total = lax.map(
        lambda item_row: attend_forward(item_row[0], item_row[1], item_row[2]),
        (query_low, key_vals, allowed),
    )
    context_low = context.reshape(token_count, D).astype(jnp.bfloat16)
    attn_out = jnp.dot(context_low, out_full.T, preferred_element_type=jnp.float32) + out_bias
    outputs = (flat_in + attn_out + mlp_out).astype(jnp.bfloat16).reshape(row_count, shard_len, D)
    regathered = (
        lax.all_gather(qkv_weight.astype(jnp.bfloat16), "seq", axis=0, tiled=True),
        lax.all_gather(out_weight.astype(jnp.bfloat16), "seq", axis=0, tiled=True),
        lax.all_gather(up_weight.astype(jnp.bfloat16), "seq", axis=0, tiled=True),
        lax.all_gather(down_weight.astype(jnp.bfloat16), "seq", axis=1, tiled=True),
    )
    qkv_full = regathered[0]
    out_full = regathered[1]
    up_full = regathered[2]
    down_full = regathered[3]
    dy_low = cotangent.reshape(token_count, D)
    dy_full = dy_low.astype(jnp.float32)
    out_part = jnp.dot(dy_low.T, context_low, preferred_element_type=jnp.float32)
    down_part = jnp.dot(dy_low.T, active_low, preferred_element_type=jnp.float32)
    d_context = jnp.dot(dy_low, out_full, preferred_element_type=jnp.float32).astype(jnp.bfloat16)
    d_context = d_context.reshape(row_count, shard_len, HEADS, HEAD)
    d_query, d_kv = lax.map(
        lambda item_row: attend_backward(
            item_row[0], item_row[1], item_row[2], item_row[3], item_row[4]
        ),
        (query_low, key_vals, allowed, log_total, d_context),
    )
    key_sums = lax.psum_scatter(d_kv, "seq", scatter_dimension=1, tiled=True)
    d_active = jnp.dot(dy_low, down_full, preferred_element_type=jnp.float32)
    gelu_value, gelu_back = jax.vjp(
        lambda values_in: jax.nn.gelu(values_in, approximate=False), hidden
    )
    d_hidden = gelu_back(d_active)[0].astype(jnp.bfloat16)
    up_part = jnp.dot(d_hidden.T, normed_two_low, preferred_element_type=jnp.float32)
    d_normed_two = jnp.dot(d_hidden, up_full, preferred_element_type=jnp.float32)
    query_value, query_back = jax.vjp(
        lambda values_in: rotate(values_in, head_cos, head_sin), query_raw
    )
    d_query_raw = query_back(d_query)[0]
    key_value, key_back = jax.vjp(lambda values_in: rotate(values_in, cosine, sine), key_raw)
    d_key_raw = key_back(key_sums[..., :HEAD])[0]
    d_projected = jnp.concatenate(
        [d_query_raw.reshape(row_count, shard_len, D), d_key_raw, key_sums[..., HEAD:]], axis=-1
    )
    d_projected = d_projected.reshape(token_count, D + 2 * HEAD).astype(jnp.bfloat16)
    qkv_part = jnp.dot(d_projected.T, normed_one_low, preferred_element_type=jnp.float32)
    d_normed_one = jnp.dot(d_projected, qkv_full, preferred_element_type=jnp.float32)
    norm_value_one, norm_back_one = jax.vjp(layer_norm, flat_in, gain_one, shift_one)
    d_in_one, d_gain_one, d_shift_one = norm_back_one(d_normed_one)
    norm_value_two, norm_back_two = jax.vjp(layer_norm, flat_in, gain_two, shift_two)
    d_in_two, d_gain_two, d_shift_two = norm_back_two(d_normed_two)
    input_grad = (
        (dy_full + d_in_one + d_in_two).astype(jnp.bfloat16).reshape(row_count, shard_len, D)
    )
    dy_column = jnp.sum(dy_full, axis=0)
    vector_part = jnp.concatenate(
        [
            d_gain_one,
            d_shift_one,
            d_gain_two,
            d_shift_two,
            jnp.sum(d_projected.astype(jnp.float32), axis=0),
            dy_column,
            jnp.sum(d_hidden.astype(jnp.float32), axis=0),
            dy_column,
        ]
    )
    seq_sums = (
        lax.psum_scatter(qkv_part, "seq", scatter_dimension=0, tiled=True),
        lax.psum_scatter(out_part, "seq", scatter_dimension=0, tiled=True),
        lax.psum_scatter(up_part, "seq", scatter_dimension=0, tiled=True),
        lax.psum_scatter(down_part, "seq", scatter_dimension=1, tiled=True),
        lax.psum_scatter(vector_part, "seq", scatter_dimension=0, tiled=True),
    )
    all_sums = lax.psum((seq_sums[0], seq_sums[1], seq_sums[2], seq_sums[3], seq_sums[4]), "batch")
    qkv_grad, out_grad, up_grad, down_grad, vector_grad = all_sums
    qkv_states = owned_update(0, qkv_weight, qkv_grad, qkv_first, qkv_second, bases[0], True)
    out_states = owned_update(1, out_weight, out_grad, out_first, out_second, bases[1], True)
    up_states = owned_update(2, up_weight, up_grad, up_first, up_second, bases[2], True)
    down_states = owned_update(3, down_weight, down_grad, down_first, down_second, bases[3], False)
    vector_states = adam_step(vectors, vector_grad, vector_first, vector_second)
    return (
        outputs,
        input_grad,
        qkv_grad,
        out_grad,
        up_grad,
        down_grad,
        vector_grad,
        qkv_states[1],
        out_states[1],
        up_states[1],
        down_states[1],
        vector_states[1],
        qkv_states[2],
        out_states[2],
        up_states[2],
        down_states[2],
        vector_states[2],
        qkv_states[0],
        out_states[0],
        up_states[0],
        down_states[0],
        vector_states[0],
    )


def solution(mesh):
    return jax.shard_map(
        shards,
        mesh=mesh,
        in_specs=(
            P("batch", "seq", None),
            P("batch", "seq", None),
            P("batch", None),
            P("seq", None),
            P("seq", None),
            P("seq", None),
            P(None, "seq"),
            P("seq"),
            P(),
            P("seq", None),
            P("seq", None),
            P("seq", None),
            P(None, "seq"),
            P("seq"),
            P("seq", None),
            P("seq", None),
            P("seq", None),
            P(None, "seq"),
            P("seq"),
        ),
        out_specs=(
            P("batch", "seq", None),
            P("batch", "seq", None),
            P("seq", None),
            P("seq", None),
            P("seq", None),
            P(None, "seq"),
            P("seq"),
            P("seq", None),
            P("seq", None),
            P("seq", None),
            P(None, "seq"),
            P("seq"),
            P("seq", None),
            P("seq", None),
            P("seq", None),
            P(None, "seq"),
            P("seq"),
            P("seq", None),
            P("seq", None),
            P("seq", None),
            P(None, "seq"),
            P("seq"),
        ),
        check_vma=False,
    )
```

profile of v0, /device:TPU:0, one launch (start us, length us, event | category | flops | bytes accessed | tf_op | source)
XLA Modules:
  0.0 1219.9 jit_solution(3275850571437767421)
XLA Ops:
  7.3 1.7 convert_element_type.116
  13.5 39.2 %all-reduce.8 = bf16[8576]{0:T(1024)(128)(2,1)S(1)} all-reduce(bf16[8576]{0:T(1024)(128)(2,1)S(1)} %dynamic-update-slice), channel_id=1, replica_groups=mesh['seq'=8,'batch'=4] {'seq'}, use_global_device_ids=true, to_apply=%add.8 | all-reduce | flops 8576 | bytes 34304
  56.2 2.6 convolution_add_fusion
  63.2 35.4 %all-gather.10.cloned.1.call-done = bf16[768,768]{1,0:T(8,128)(2,1)} async-done(((bf16[96,768]{1,0:T(8,128)(2,1)}), bf16[768,768]{1,0:T(8,128)(2,1)}) %all-gather.10.cloned.1.call-update) | async-done | bytes 1179664 | tf_op jit(solution)/shard_map/all_gather | solution.py:186
  98.6 2.0 convolution_convert_fusion
  109.1 30.5 %all-gather.8.cloned.1.call-done = bf16[4,1024,128]{1,2,0:T(8,128)(2,1)} async-done(((bf16[4,128,128]{1,2,0:T(8,128)(2,1)}), bf16[4,1024,128]{1,2,0:T(8,128)(2,1)}) %all-gather.8.cloned.1.call-update) | async-done | bytes 1048592 | tf_op jit(solution)/shard_map/all_gather | solution.py:218
  139.6 27.1 %while.26 = (s32[]{:T(128)}, bf16[4,128,12,64]{1,3,2,0:T(8,128)(2,1)}, f32[4,12,128]{2,1,0:T(8,128)S(1)}, bf16[4,1024,128]{1,2,0:T(8,128)(2,1)}, pred[4,128,1024...) while((s32[]{:T(128)}, bf16[4,128,12,64]{1,3,2,0:T(8,128)(2,1)}, ...), condition=%wide.region_9.10_spmd.clone, body=%wide.region_6.9_spmd.sunk.clone | while | flops 421526016 | bytes 27256984 | solution.py:222
  142.0 1.7 fusion.255
  143.7 1.9 fusion.256
  148.7 1.7 fusion.255
  150.4 1.9 fusion.256
  155.5 1.7 fusion.255
  157.2 1.9 fusion.256
  162.2 1.7 fusion.255
  163.9 1.9 fusion.256
  166.7 44.7 %while.27 = (s32[]{:T(128)}, f32[4,128,12,64]{1,3,2,0:T(8,128)}, f32[4,1024,128]{1,2,0:T(8,128)}, bf16[4,1024,128]{1,2,0:T(8,128)(2,1)}, pred[4,128,1024]{2,1,0:...) while((s32[]{:T(128)}, f32[4,128,12,64]{1,3,2,0:T(8,128)}, ...), condition=%wide.region_12.13_spmd.clone, body=%wide.region_10.12_spmd.sunk.clone | while | flops 1030519296 | bytes 51558528 | solution.py:245
  168.7 2.3 fusion.264
  171.0 1.8 fusion.265
  172.8 1.8 fusion.266
  174.6 1.7 fusion.267
  179.9 2.3 fusion.264
  182.2 1.8 fusion.265
  184.0 1.9 fusion.266
  185.8 1.7 fusion.267
  191.1 2.3 fusion.264
  193.4 1.8 fusion.265
  195.2 1.8 fusion.266
  197.0 1.7 fusion.267
  202.2 2.3 fusion.264
  204.5 1.8 fusion.265
  206.3 1.9 fusion.266
  208.2 1.7 fusion.267
  217.1 2.4 copy.127
  222.1 56.2 %reduce-scatter.8.cloned.1.call-done = f32[4,128,128]{1,2,0:T(8,128)} async-done(((f32[4,1024,128]{1,2,0:T(8,128)}), f32[4,128,128]{1,2,0:T(8,128)}) %reduce-scatter.8.cloned.1.call-update) | async-done | bytes 262160 | tf_op jit(solution)/shard_map/reduce_scatter | solution.py:251
  281.9 2.5 fusion.190
  284.4 75.6 %all-gather.12.cloned.1.call-done = bf16[3072,768]{1,0:T(8,128)(2,1)} async-done(((bf16[384,768]{1,0:T(8,128)(2,1)}), bf16[3072,768]{1,0:T(8,128)(2,1)}) %all-gather.12.cloned.1.call-update) | async-done | bytes 4718608 | tf_op jit(solution)/shard_map/all_gather | solution.py:187
  360.0 6.8 fusion.187
  366.8 74.9 %all-gather.14.cloned.1.call-done = bf16[768,3072]{1,0:T(8,128)(2,1)} async-done(((bf16[768,384]{1,0:T(8,128)(2,1)}), bf16[768,3072]{1,0:T(8,128)(2,1)}) %all-gather.14.cloned.1.call-update) | async-done | bytes 4718608 | tf_op jit(solution)/shard_map/all_gather | solution.py:188
  441.7 19.7 %convert_reduce_fusion = (f32[3072]{0:T(1024)S(1)}, bf16[512,3072]{1,0:T(8,128)(2,1)S(1)}, f32[512,3072]{1,0:T(8,128)}) fusion(f32[512,3072]{1,0:T(8,128)} %fusion.187, f32[3072]{0:T(1024)S(1)} %slice.134, bf16[512,768]{1,0:T(8,128)(2,1)S(1)} %bitcast.340, bf16[768,3072]{1,0:T(8,128)(2,1)} %all-gather.14.cloned.1.call-done), kind=kOutput, calls=%fused_computation.140 | convolution fusion | flops 2533880832 | bytes 21258240 | tf_op jit(solution)/shard_map/dot_general | solution.py:252
  463.0 5.1 fusion.191
  468.2 6.2 multiply_convert_fusion
  474.4 1.7 copy-done.17
  476.1 5.3 convolution_bitcast_fusion.1
  481.5 30.9 %reduce-scatter.16.cloned.1.call-done = f32[96,768]{1,0:T(8,128)} async-done(((f32[768,768]{1,0:T(8,128)}), f32[96,768]{1,0:T(8,128)}) %reduce-scatter.16.cloned.1.call-update) | async-done | bytes 294928
  512.4 1.9 copy.128
  514.3 71.7 %reduce-scatter.10.cloned.1.call-done = f32[112,768]{1,0:T(8,128)} async-done(((f32[896,768]{1,0:T(8,128)}), f32[112,768]{1,0:T(8,128)}) %reduce-scatter.10.cloned.1.call-update) | async-done | bytes 344080 | tf_op jit(solution)/shard_map/reduce_scatter | solution.py:292
  586.0 166.3 %reduce-scatter.12.cloned.1.call-done = f32[384,768]{1,0:T(8,128)} async-done(((f32[3072,768]{1,0:T(8,128)}), f32[384,768]{1,0:T(8,128)}) %reduce-scatter.12.cloned.1.call-update) | async-done | bytes 1179664 | tf_op jit(solution)/shard_map/reduce_scatter | solution.py:294
  752.3 165.9 %reduce-scatter.14.cloned.1.call-done = f32[768,384]{0,1:T(8,128)} async-done(((f32[768,3072]{0,1:T(8,128)}), f32[768,384]{0,1:T(8,128)}) %reduce-scatter.14.cloned.1.call-update) | async-done | bytes 1179664 | tf_op jit(solution)/shard_map/reduce_scatter | solution.py:295
  919.1 69.8 %all-reduce.17.cloned.1.call-done = (f32[112,768]{1,0:T(8,128)}, f32[96,768]{0,1:T(8,128)}, f32[384,768]{1,0:T(8,128)}, f32[768,384]{0,1:T(8,128)}) async-done(((f32[112,768]{1,0:T(8,128)}, f32[96,768]{0,1:T(8,128)}, f32[384,768]{1,0:T(8,128)}, f32[768,384]{0,1:T(8,128)}), (f32[112,768]{1,0:T(8,128)}, f32[96,768]{0,1:T(8,128)}, f32[384,768]{1,0:T(8,128)}, ...) | async-done | bytes 2998288 | tf_op jit(solution)/shard_map/psum | solution.py:298
  988.9 8.6 conditional.4
  988.9 4.2 multiply_add_fusion
  993.1 4.4 fusion.50
  997.4 1.9 broadcast_select_fusion.8
  1001.6 2.6 conditional.6
  1006.3 5.1 conditional.7
  1012.6 1.9 broadcast_select_fusion.6
  1018.5 6.1 fusion.188
  1024.7 1.8 fusion.158
  1026.6 5.1 fusion.189
  1035.1 37.5 %all-reduce.9 = f32[8576]{0:T(1024)S(1)} all-reduce(f32[8576]{0:T(1024)S(1)} %constant_dynamic-update-slice_fusion.2), channel_id=7, replica_groups=mesh['seq'=8,'batch'=4] {'seq'}, use_global_device_ids=true, to_apply=%region_33.34.clone | all-reduce | flops 8576 | bytes 68608
  1072.7 15.4 %psum.123 = f32[1072]{0:T(1024)S(1)} all-reduce(f32[1072]{0:T(1024)S(1)} %dynamic-slice.2), channel_id=1, replica_groups=mesh['seq'=8,'batch'=4] {'batch'}, use_global_device_ids=true, to_apply=%region_34.35 | all-reduce | flops 1072 | bytes 8576 | tf_op jit(solution)/shard_map/psum | solution.py:298
  1088.8 3.2 add_convert_fusion.1
  1092.9 2.7 copy.123
  1095.6 105.1 %all-reduce.15.cloned.1.call-done = (f32[112,768]{1,0:T(8,128)}, f32[96,768]{1,0:T(8,128)}, f32[384,768]{1,0:T(8,128)}, f32[768,384]{1,0:T(8,128)}, f32[112,768]...) async-done(((f32[112,768]{1,0:T(8,128)}, ...) | async-done | bytes 8994832 | tf_op jit(solution)/shard_map/psum | solution.py:26
  (327 shorter events, 93.7 us)
Async XLA Ops:
  7.2 4.7 copy-start.65
  7.2 4.7 copy-start.53
  7.2 45.4 %copy-start = (bf16[4,128,768]{2,1,0:T(8,128)(2,1)S(1)}, bf16[4,128,768]{2,1,0:T(8,128)(2,1)}, u32[]{:S(2)}) copy-start(bf16[4,128,768]{2,1,0:T(8,128)(2,1)} %param.31) | copy-start | bytes 2359300
  7.2 46.0 %copy-start.61 = (s32[4,8]{1,0:T(4,128)S(1)}, s32[4,8]{1,0:T(4,128)}, u32[]{:S(2)}) copy-start(s32[4,8]{1,0:T(4,128)} %param.33) | copy-start | bytes 388
  7.2 49.0 %all-gather.6.cloned.1.call-start = ((), (), s32[]{:S(2)}) async-start(), calls=%async_computation.5 | async-start | bytes 1548288 | tf_op jit(solution)/shard_map/all_gather | solution.py:185
  9.0 89.6 %all-gather.10.cloned.1.call-start = ((), (), s32[]{:S(2)}) async-start(), calls=%async_computation.7 | async-start | bytes 1327104 | tf_op jit(solution)/shard_map/all_gather | solution.py:186
  10.8 128.9 %all-gather.8.cloned.1.call-start = ((), (), s32[]{:S(2)}) async-start(), calls=%async_computation.6 | async-start | bytes 1179648 | tf_op jit(solution)/shard_map/all_gather | solution.py:218
  52.6 3.6 copy-start.43
  52.8 6.0 copy-start.49
  53.2 3.0 copy-start.56
  53.3 2.9 copy-start.62
  53.5 2.8 copy-start.58
  54.1 4.7 copy-start.51
  54.8 4.1 copy-start.45
  54.8 4.1 copy-start.47
  56.2 2.7 copy-start.15
  58.9 3.1 copy-start.9
  59.1 39.6 %copy-start.2 = (bf16[4,128,768]{2,1,0:T(8,128)(2,1)S(1)}, bf16[4,128,768]{2,1,0:T(8,128)(2,1)}, u32[]{:S(2)}) copy-start(bf16[4,128,768]{2,1,0:T(8,128)(2,1)} %param.32) | copy-start | bytes 2359300
  60.4 217.9 %reduce-scatter.8.cloned.1.call-start = ((), (), s32[]{:S(2)}) async-start(), calls=%async_computation.10 | async-start | bytes 2359296 | tf_op jit(solution)/shard_map/reduce_scatter | solution.py:251
  139.6 27.1 %copy-start.8 = (bf16[4,128,12,64]{1,3,2,0:T(8,128)(2,1)S(1)}, bf16[4,128,12,64]{1,3,2,0:T(8,128)(2,1)}, u32[]{:S(2)}) copy-start(bf16[4,128,12,64]{1,3,2,0:T(8,128)(2,1)} %copy.114) | copy-start | bytes 2359300
  211.4 2.2 copy-start.5
  211.4 148.6 %all-gather.12.cloned.1.call-start = ((), (), s32[]{:S(2)}) async-start(), calls=%async_computation.8 | async-start | bytes 5308416 | tf_op jit(solution)/shard_map/all_gather | solution.py:187
  213.6 228.1 %all-gather.14.cloned.1.call-start = ((), (), s32[]{:S(2)}) async-start(), calls=%async_computation.9 | async-start | bytes 5308416 | tf_op jit(solution)/shard_map/all_gather | solution.py:188
  214.5 297.9 %reduce-scatter.16.cloned.1.call-start = ((), (), s32[]{:S(2)}) async-start(), calls=%async_computation.14 | async-start | bytes 2654208
  219.5 366.5 %reduce-scatter.10.cloned.1.call-start = ((), (), s32[]{:S(2)}) async-start(), calls=%async_computation.11 | async-start | bytes 3096576 | tf_op jit(solution)/shard_map/reduce_scatter | solution.py:292
  221.4 60.5 %copy-start.16 = (bf16[512,768]{1,0:T(8,128)(2,1)S(1)}, bf16[512,768]{1,0:T(8,128)(2,1)}, u32[]{:S(2)}) copy-start(bf16[512,768]{1,0:T(8,128)(2,1)} %copy-done.15) | copy-start | bytes 2359300
  284.4 75.7 %copy-start.36 = (bf16[512,768]{1,0:T(8,128)(2,1)S(1)}, bf16[512,768]{1,0:T(8,128)(2,1)}, u32[]{:S(2)}) copy-start(bf16[512,768]{1,0:T(8,128)(2,1)} %get-tuple-element.462) | copy-start | bytes 2359300
  284.4 467.9 %reduce-scatter.12.cloned.1.call-start = ((), (), s32[]{:S(2)}) async-start(), calls=%async_computation.12 | async-start | bytes 10616832 | tf_op jit(solution)/shard_map/reduce_scatter | solution.py:294
  468.2 450.0 %reduce-scatter.14.cloned.1.call-start = ((), (), s32[]{:S(2)}) async-start(), calls=%async_computation.13 | async-start | bytes 10616832 | tf_op jit(solution)/shard_map/reduce_scatter | solution.py:295
  481.4 507.4 %all-reduce.17.cloned.1.call-start = ((), (), s32[]{:S(2)}) async-start(), calls=%async_computation.16 | async-start | bytes 6193152 | tf_op jit(solution)/shard_map/psum | solution.py:298
  918.2 70.7 %copy-start.20 = (f32[112,768]{1,0:T(8,128)S(1)}, f32[112,768]{1,0:T(8,128)}, u32[]{:S(2)}) copy-start(f32[112,768]{1,0:T(8,128)} %param.34) | copy-start | bytes 1032196
  918.2 282.5 %all-reduce.15.cloned.1.call-start = ((), (), s32[]{:S(2)}) async-start(), calls=%async_computation.15 | async-start | bytes 17989632 | tf_op jit(solution)/shard_map/psum | solution.py:26
  988.8 10.5 copy-start.19
  988.9 10.5 copy-start.24
  997.4 1.9 copy-start.21
  1004.3 2.0 copy-start.35
  1011.5 3.0 copy-start.34
  1018.5 6.1 copy-start.1
  1018.5 6.1 copy-start.14
  1018.5 6.1 copy-start.63
  1018.5 6.1 copy-start.64
  1018.5 6.1 copy-start.67
  1024.7 1.9 copy-start.69
  1026.6 5.1 copy-start.46
  1026.6 5.1 copy-start.48
  1026.6 5.1 copy-start.50
  1026.6 5.1 copy-start.66
  1033.3 54.8 %copy-start.54 = (f32[1072]{0:T(1024)S(1)}, f32[1072]{0:T(1024)}, u32[]{:S(2)}) copy-start(f32[1072]{0:T(1024)} %param.38) | copy-start | bytes 12868
  1033.3 54.8 %copy-start.59 = (f32[1072]{0:T(1024)S(1)}, f32[1072]{0:T(1024)}, u32[]{:S(2)}) copy-start(f32[1072]{0:T(1024)} %param.49) | copy-start | bytes 12868
  1033.3 54.8 %copy-start.60 = (f32[1072]{0:T(1024)S(1)}, f32[1072]{0:T(1024)}, u32[]{:S(2)}) copy-start(f32[1072]{0:T(1024)} %param.44) | copy-start | bytes 12868
  1088.1 3.9 copy-start.55
  1092.0 108.6 %copy-start.23 = (f32[112,768]{1,0:T(8,128)S(1)}, f32[112,768]{1,0:T(8,128)}, u32[]{:S(2)}) copy-start(f32[112,768]{1,0:T(8,128)} %get-tuple-element.693) | copy-start | bytes 1032196
  1092.0 109.4 %copy-start.6 = (f32[384,768]{1,0:T(8,128)S(1)}, f32[384,768]{1,0:T(8,128)}, u32[]{:S(2)}) copy-start(f32[384,768]{1,0:T(8,128)} %get-tuple-element.695) | copy-start | bytes 3538948
  1200.7 1.8 copy-start.39
  1200.7 2.5 copy-start.42
  1201.4 2.5 copy-start.32
  1202.4 2.5 copy-start.31
  1203.9 2.0 copy-start.38
  1204.9 1.8 copy-start.41
  1204.9 2.5 copy-start.30
  1205.9 2.5 copy-start.29
  1207.4 2.0 copy-start.37
  1208.4 2.5 copy-start.28
  1209.4 2.5 copy-start.27
  (23 other events, 30.9 us)
Sparse Core Ops, SparseCore 0:
  10.8 45.2 all-gather.5
  58.9 39.6 all-gather.9
  101.3 38.2 all-gather.7
  211.5 66.8 reduce-scatter.7
  281.0 78.9 all-gather.11
  362.5 79.1 all-gather.13
  445.2 67.1 reduce-scatter.15
  515.9 70.0 reduce-scatter.9
  589.6 162.6 reduce-scatter.11
  755.7 162.3 reduce-scatter.13
  921.4 67.4 all-reduce.16
  1018.6 182.0 all-reduce.14
where the time goes:
time: 1230 us; the launch traced here: 1220 us
  waiting for transfers between devices  882 us (72%)
  matrix products  110 us (9%)
  blocking collectives  92.1 us (7%)
  local copies, waits for them, and re-layouts  58.3 us (5%)
  other arithmetic  56.7 us (5%)
  between operations  16.7 us (1%)
    reduce_scatter x1, waiting for transfers between devices, shards(): lax.psum_scatter(up_part, 'seq', scatter_dimension=0, tiled=True)  166 us
    reduce_scatter x1, waiting for transfers between devices, shards(): lax.psum_scatter(down_part, 'seq', scatter_dimension=1, tiled=True)  166 us
    psum x1, waiting for transfers between devices, spread_2(): return lax.psum(jnp.where(mine, value, jnp.zeros_like(value)), axis)  105 us
    unnamed x2, blocking collectives  76.6 us
    all_gather x1, waiting for transfers between devices, shards(): lax.all_gather(up_weight.astype(jnp.bfloat16), 'seq', axis=0, tiled=True)  75.6 us
    all_gather x1, waiting for transfers between devices, shards(): lax.all_gather(down_weight.astype(jnp.bfloat16), 'seq', axis=1, tiled=True)  74.9 us
    reduce_scatter x1, waiting for transfers between devices, shards(): lax.psum_scatter(qkv_part, 'seq', scatter_dimension=0, tiled=True)  71.7 us
    psum x1, waiting for transfers between devices, shards(): lax.psum((seq_sums[0], seq_sums[1], seq_sums[2], seq_sums[3], seq_sums[4]...  69.8 us
  transfers between devices with their start and end apart: 12, of which 11 were waited for; matrix products, arithmetic and copies ran while one was open for 9% of the time, Pallas kernels for 0%

commit v1 on v0

v1 whole, which is shorter than its diff:
```python
import functools

import jax
import jax.numpy as jnp
from jax import lax
from jax.experimental import pallas as pl
from jax.experimental.pallas import tpu as pltpu
from jax.sharding import PartitionSpec as P

D = 768
HEADS = 12
HEAD = 64
ROT = 16
FF = 3072
STEP = 10

layer_eps = 1e-05
adam_eps = 1e-08
beta_first = 0.95
beta_second = 0.95
matrix_rate = 0.08
vector_rate = 0.3
rope_base = 10000.0
masked_score = -1e30
low = jnp.bfloat16
f32 = jnp.float32
VMEM_LIMIT = 56 * 1024 * 1024


def swap(value, bit):
    axis, step = bit
    return lax.ppermute(value, axis, [(i, i ^ step) for i in range(lax.axis_size(axis))])


def mine(bit):
    axis, step = bit
    return lax.rem(lax.axis_index(axis) // step, 2)


def place(have, bit, canon):
    return sum(1 for other in have if canon.index(other) < canon.index(bit))


def gather_bits(piece, order, canon, absolute):
    have = []
    value = piece
    for bit in order:
        got = swap(value, bit)
        if absolute:
            upper = mine(bit) == 1
            pair = [jnp.where(upper, got, value), jnp.where(upper, value, got)]
        else:
            pair = [value, got]
        value = jnp.stack(pair, axis=place(have, bit, canon))
        have.append(bit)
    return value


def sum_bits(value, order, canon, absolute):
    left = list(order)
    for bit in order:
        axis = place([b for b in left if b != bit], bit, canon)
        if absolute:
            own = mine(bit)
            kept = lax.dynamic_index_in_dim(value, own, axis, keepdims=False)
            sent = lax.dynamic_index_in_dim(value, 1 - own, axis, keepdims=False)
        else:
            kept = lax.index_in_dim(value, 0, axis, keepdims=False)
            sent = lax.index_in_dim(value, 1, axis, keepdims=False)
        value = kept.astype(f32) + swap(sent.astype(low), bit).astype(f32)
        left.remove(bit)
    return value


def bit_names(axis, size):
    return [(axis, 1 << k) for k in range(size.bit_length() - 1)]


def matmul_exact(left, right):
    return jnp.dot(left, right, precision=lax.Precision.HIGHEST, preferred_element_type=f32)


def split_vectors(vectors):
    widths = [D, D, D, D, D + 2 * HEAD, D, FF, D]
    pieces = []
    offset = 0
    for piece_width in widths:
        pieces.append(vectors[offset : offset + piece_width])
        offset = offset + piece_width
    return pieces


def moments(rotated, first, second):
    new_first = beta_first * first + (1.0 - beta_first) * rotated
    new_second = beta_second * second + (1.0 - beta_second) * rotated * rotated
    ratio = (
        new_first
        / (1.0 - beta_first**STEP)
        / (jnp.sqrt(new_second / (1.0 - beta_second**STEP)) + adam_eps)
    )
    return ratio, new_first, new_second


def soap_step(weight, grad, first, second, basis, on_right):
    rotated = matmul_exact(grad, basis) if on_right else matmul_exact(basis.T, grad)
    ratio, new_first, new_second = moments(rotated, first, second)
    unrotated = matmul_exact(ratio, basis.T) if on_right else matmul_exact(basis, ratio)
    return (weight - matrix_rate * unrotated, new_first, new_second)


def adam_step(weight, grad, first, second):
    ratio, new_first, new_second = moments(grad, first, second)
    return (weight - vector_rate * ratio, new_first, new_second)


def turn(values, cosine, sine, back):
    half = ROT // 2
    heads = values.reshape(-1, HEAD, values.shape[-1])
    a, b = heads[:, :half], heads[:, half:ROT]
    if back:
        pair = [a * cosine + b * sine, b * cosine - a * sine]
    else:
        pair = [a * cosine - b * sine, b * cosine + a * sine]
    return jnp.concatenate(pair + [heads[:, ROT:]], axis=1).reshape(values.shape)


def attention_kernel(blocks, width, q_ref, do_ref, start_ref, cos_ref, sin_ref, *refs):
    kv_refs = refs[:blocks]
    context_ref, dq_ref, dkv_own_ref, dkv_ref = refs[blocks:]
    length = q_ref.shape[1]
    keys = blocks * length
    key_t = jnp.concatenate([ref[:HEAD, :] for ref in reversed(kv_refs)], axis=1)
    value_t = jnp.concatenate([ref[HEAD:, :] for ref in reversed(kv_refs)], axis=1)
    key = key_t.astype(f32).T.astype(low)
    value = value_t.astype(f32).T.astype(low)
    key_pos = lax.broadcasted_iota(jnp.int32, (keys, length), 0) - (blocks - 1) * length
    query_pos = lax.broadcasted_iota(jnp.int32, (keys, length), 1)
    allowed = (key_pos >= start_ref[0]) & (key_pos <= query_pos)
    bias = jnp.where(allowed, 0.0, masked_score)
    cosine, sine = cos_ref[...], sin_ref[...]
    d_key = jnp.zeros((keys, HEAD), f32)
    d_value = jnp.zeros((keys, HEAD), f32)
    last = (((1,), (1,)), ((), ()))
    for first in range(0, HEADS, width):
        heads = range(first, first + width)
        query = jnp.concatenate([q_ref[h * HEAD : (h + 1) * HEAD, :] for h in heads], axis=1)
        d_out = jnp.concatenate([do_ref[h * HEAD : (h + 1) * HEAD, :] for h in heads], axis=1)
        scores = jnp.dot(key, query, preferred_element_type=f32)
        scores = scores + jnp.concatenate([bias] * width, axis=1)
        weights = jnp.exp(scores - jnp.max(scores, axis=0, keepdims=True))
        probs = weights * (1.0 / jnp.sum(weights, axis=0, keepdims=True))
        probs_low = probs.astype(low)
        context_t = jnp.dot(value_t, probs_low, preferred_element_type=f32)
        d_probs = jnp.dot(value, d_out, preferred_element_type=f32)
        inner = jnp.sum(probs * d_probs, axis=0, keepdims=True)
        d_scores = (probs * (d_probs - inner)).astype(low)
        d_query = jnp.dot(key_t, d_scores, preferred_element_type=f32) * HEAD ** (-0.5)
        d_value = d_value + lax.dot_general(probs_low, d_out, last, preferred_element_type=f32)
        d_key = d_key + lax.dot_general(d_scores, query, last, preferred_element_type=f32)
        for k, h in enumerate(heads):
            lanes = slice(k * length, (k + 1) * length)
            part = d_query[:, lanes]
            a, b = part[: ROT // 2], part[ROT // 2 : ROT]
            turned = jnp.concatenate([a * cosine + b * sine, b * cosine - a * sine, part[ROT:]], axis=0)
            dq_ref[h * HEAD : (h + 1) * HEAD, :] = turned.astype(low)
        for k in range(0, width, 2):
            h = first + k
            two = jnp.concatenate(
                [context_t[:, k * length : (k + 1) * length], context_t[:, (k + 1) * length : (k + 2) * length]], axis=0
            )
            context_ref[:, h * HEAD : (h + 2) * HEAD] = two.T.astype(low)
    d_kv = jnp.concatenate([d_key, d_value], axis=1).T
    for k in range(blocks):
        part = d_kv[:, (blocks - 1 - k) * length : (blocks - k) * length]
        if k == 0:
            dkv_own_ref[...] = part
        else:
            dkv_ref[k - 1] = part.astype(low)


def attention(q_t, do_t, start, cosine, sine, kv):
    rows, _, length = start.shape
    blocks = len(kv)
    tokens = q_t.shape[1]
    by_row = lambda height: pl.BlockSpec((height, length), lambda r: (0, r))
    return pl.pallas_call(
        functools.partial(attention_kernel, blocks, 4),
        grid=(rows,),
        in_specs=[by_row(D), by_row(D), pl.BlockSpec((1, 1, length), lambda r: (r, 0, 0)), by_row(ROT // 2), by_row(ROT // 2)]
        + [by_row(2 * HEAD)] * blocks,
        out_specs=[
            pl.BlockSpec((length, D), lambda r: (r, 0)),
            by_row(D),
            by_row(2 * HEAD),
            pl.BlockSpec((blocks - 1, 2 * HEAD, length), lambda r: (0, 0, r)),
        ],
        out_shape=[
            jax.ShapeDtypeStruct((tokens, D), low),
            jax.ShapeDtypeStruct((D, tokens), low),
            jax.ShapeDtypeStruct((2 * HEAD, tokens), f32),
            jax.ShapeDtypeStruct((blocks - 1, 2 * HEAD, tokens), low),
        ],
        compiler_params=pltpu.CompilerParams(vmem_limit_bytes=VMEM_LIMIT),
        cost_estimate=pl.CostEstimate(
            flops=4 * 7 * tokens * HEADS * blocks * length * HEAD * 2, bytes_accessed=8 << 20, transcendentals=0
        ),
        name="attention",
    )(q_t, do_t, start, cosine, sine, *kv)


def feed_kernel(n_ref, dy_ref, up_ref, down_ref, bias_ref, out_ref, dn_ref, up_grad_ref, down_grad_ref, bias_grad_ref):
    last = (((1,), (1,)), ((), ()))
    first = (((0,), (0,)), ((), ()))
    normed, d_out = n_ref[...], dy_ref[...]
    up, down = up_ref[...], down_ref[...]
    hidden = lax.dot_general(normed, up, last, preferred_element_type=f32) + bias_ref[...]
    share = 0.5 * (1.0 + lax.erf(hidden * (0.5**0.5)))
    slope = share + hidden * (jnp.exp(-0.5 * hidden * hidden) * (0.5 / 3.141592653589793) ** 0.5)
    active = (hidden * share).astype(low)
    d_active = lax.dot_general(d_out, down, last, preferred_element_type=f32)
    d_hidden = (d_active * slope).astype(low)
    out = jnp.dot(active, down, preferred_element_type=f32)
    d_normed = jnp.dot(d_hidden, up, preferred_element_type=f32)

    @pl.when(pl.program_id(0) == 0)
    def _():
        out_ref[...] = out
        dn_ref[...] = d_normed

    @pl.when(pl.program_id(0) > 0)
    def _():
        out_ref[...] += out
        dn_ref[...] += d_normed

    up_grad_ref[...] = lax.dot_general(d_hidden, normed, first, preferred_element_type=f32).astype(up_grad_ref.dtype)
    down_grad_ref[...] = lax.dot_general(active, d_out, first, preferred_element_type=f32).astype(down_grad_ref.dtype)
    bias_grad_ref[...] = jnp.sum(d_hidden.astype(f32), axis=0, keepdims=True)


def feed(normed, d_out, up, down, bias, grad_type):
    tokens = normed.shape[0]
    units = up.shape[0]
    step = 512 if units % 512 == 0 else units
    whole = pl.BlockSpec((tokens, D), lambda i: (0, 0))
    part = pl.BlockSpec((step, D), lambda i: (i, 0))
    row = pl.BlockSpec((1, step), lambda i: (0, i))
    return pl.pallas_call(
        feed_kernel,
        grid=(units // step,),
        in_specs=[whole, whole, part, part, row],
        out_specs=[whole, whole, part, part, row],
        out_shape=[
            jax.ShapeDtypeStruct((tokens, D), f32),
            jax.ShapeDtypeStruct((tokens, D), f32),
            jax.ShapeDtypeStruct((units, D), grad_type),
            jax.ShapeDtypeStruct((units, D), grad_type),
            jax.ShapeDtypeStruct((1, units), f32),
        ],
        compiler_params=pltpu.CompilerParams(vmem_limit_bytes=VMEM_LIMIT),
        cost_estimate=pl.CostEstimate(flops=12 * tokens * units * D, bytes_accessed=8 << 20, transcendentals=0),
        name="feed",
    )(normed, d_out, up, down, bias)


def shards(
    inputs,
    cotangent,
    doc_lengths,
    qkv_weight,
    out_weight,
    up_weight,
    down_weight,
    vectors,
    bases,
    qkv_first,
    out_first,
    up_first,
    down_first,
    vector_first,
    qkv_second,
    out_second,
    up_second,
    down_second,
    vector_second,
):
    seq_count, batch_count = lax.axis_size("seq"), lax.axis_size("batch")
    seq_index, batch_index = lax.axis_index("seq"), lax.axis_index("batch")
    row_count, shard_len = inputs.shape[:2]
    tokens = row_count * shard_len
    y_bit, *z_bits = bit_names("seq", seq_count)
    core_bit, *x_bits = bit_names("batch", batch_count)
    canon = z_bits[::-1] + [y_bit] + x_bits[::-1] + [core_bit]
    near = [core_bit] + x_bits[::-1] + [y_bit] + z_bits[::-1]
    y_then_x = z_bits + [y_bit] + x_bits
    x_then_y = z_bits + x_bits + [y_bit]

    qkv_rows, out_rows, up_rows, vec_len = qkv_weight.shape[0], out_weight.shape[0], up_weight.shape[0], vectors.shape[0]
    vec_rows = -(-vec_len // D)
    used = qkv_rows + vec_rows
    head_rows = -(-used // (8 * batch_count)) * 8 * batch_count
    vec_pad = vec_rows * D - vec_len

    def own_part(rows):
        size = rows.shape[0] // batch_count
        return lax.dynamic_slice_in_dim(rows, batch_index * size, size, axis=0)

    head_shard = jnp.concatenate(
        [qkv_weight, jnp.pad(vectors, (0, vec_pad)).reshape(vec_rows, D), jnp.zeros((head_rows - used, D), f32)], axis=0
    ).astype(low)
    head_full = gather_bits(own_part(head_shard), y_then_x + [core_bit], canon, True).reshape(seq_count, head_rows, D)
    out_full = gather_bits(own_part(out_weight.astype(low)), x_then_y + [core_bit], canon, True).reshape(D, D)
    up_near = gather_bits(own_part(up_weight.astype(low)), y_then_x, near, False).reshape(-1, D)
    down_near = gather_bits(own_part(down_weight.T.astype(low)), x_then_y, near, False).reshape(-1, D)
    up_far = swap(up_near, core_bit)
    down_far = swap(down_near, core_bit)

    qkv_full = head_full[:, :qkv_rows].reshape(D + 2 * HEAD, D)
    vector_full = head_full[:, qkv_rows:used].reshape(seq_count, vec_rows * D)[:, :vec_len].reshape(-1)
    pieces = split_vectors(vector_full.astype(f32))
    gain_one, shift_one, gain_two, shift_two, qkv_bias, out_bias, up_bias, down_bias = pieces
    unit_count = up_rows // batch_count
    device = jnp.arange(seq_count * batch_count)
    entry = jnp.zeros_like(device)
    for axis_name, index, number in (("seq", seq_index, device // batch_count), ("batch", batch_index, device % batch_count)):
        differs = number ^ index
        for place_from_end, bit in enumerate(near[::-1]):
            if bit[0] == axis_name:
                entry = entry + ((differs // bit[1]) % 2) * (1 << place_from_end)
    is_entry = entry[None, :] == device[:, None]
    bias_near = lax.dot_general(
        is_entry.astype(f32), up_bias.reshape(-1, unit_count), (((1,), (0,)), ((), ())), preferred_element_type=f32
    ).reshape(2, 1, FF // 2)

    first_pos = seq_index * shard_len
    query_pos = first_pos + jnp.arange(shard_len, dtype=jnp.int32)
    docs = doc_lengths.shape[1]
    earlier = jnp.arange(docs)[:, None] < jnp.arange(docs)[None, :]
    doc_starts = jnp.sum(jnp.where(earlier[None], doc_lengths[:, :, None], 0), axis=1)
    start = jnp.max(
        jnp.where(doc_starts[:, None, :] <= query_pos[None, :, None], doc_starts[:, None, :], 0), axis=-1
    )
    offsets = (query_pos[None, :] - start).reshape(tokens)
    inverse = 1.0 / rope_base ** (jnp.arange(0, ROT, 2).astype(f32) / ROT)
    angles = offsets.astype(f32)[None, :] * inverse[:, None]
    cosine, sine = jnp.cos(angles), jnp.sin(angles)
    start_here = (start - first_pos).astype(jnp.int32)[:, None, :]

    flat_in = inputs.astype(f32).reshape(tokens, D)
    center = flat_in - jnp.mean(flat_in, axis=-1, keepdims=True)
    inv_sigma = lax.rsqrt(jnp.mean(center * center, axis=-1, keepdims=True) + layer_eps)
    xhat = center * inv_sigma
    normed_one = (xhat * gain_one + shift_one).astype(low)
    normed_two = (xhat * gain_two + shift_two).astype(low)
    dy = cotangent.reshape(tokens, D)
    last = (((1,), (1,)), ((), ()))
    projected = lax.dot_general(qkv_full, normed_one, last, preferred_element_type=f32) + qkv_bias[:, None]
    turned = turn(projected[: D + HEAD], cosine, sine, False).astype(low)
    q_t = turned[:D] * jnp.asarray(HEAD ** (-0.5), low)
    kv_own = jnp.concatenate([turned[D:], projected[D + HEAD :].astype(low)], axis=0)
    reach = seq_count // 2
    kv = [kv_own] + [
        lax.ppermute(kv_own, "seq", [(j, j + i) for j in range(seq_count - i)]) for i in range(1, reach + 1)
    ]
    do_t = lax.dot_general(out_full, dy, (((0,), (1,)), ((), ())), preferred_element_type=f32).astype(low)
    context, dq_t, dkv_own, dkv_sent = attention(q_t, do_t, start_here, cosine, sine, kv)
    dkv = dkv_own
    for i in range(1, reach + 1):
        dkv = dkv + lax.ppermute(dkv_sent[i - 1], "seq", [(j + i, j) for j in range(seq_count - i)]).astype(f32)

    out_one, dn_one, up_grad_far, down_grad_far, bias_grad_far = feed(normed_two, dy, up_far, down_far, bias_near[1], low)
    out_two, dn_two, up_grad_near, down_grad_near, bias_grad_near = feed(
        normed_two, dy, up_near, down_near, bias_near[0], f32
    )

    attn_out = lax.dot_general(context, out_full, last, preferred_element_type=f32)
    outputs = (flat_in + attn_out + (out_one + out_two) + (out_bias + down_bias)).astype(low)

    def reduce_near(near_half, far_half, order):
        value = near_half + swap(far_half, core_bit).astype(f32)
        bits = near[1:]
        value = value.reshape((2,) * len(bits) + (-1, D))
        return sum_bits(value, order[::-1], bits, False)

    up_sum = reduce_near(up_grad_near, up_grad_far, y_then_x)
    down_sum = reduce_near(down_grad_near, down_grad_far, x_then_y)

    out_grad_part = lax.dot_general(dy, context, (((0,), (0,)), ((), ())), preferred_element_type=f32)
    bit_shape = (2,) * len(canon)
    out_sum = sum_bits(
        out_grad_part.reshape(bit_shape + (-1, D)), [core_bit] + x_then_y[::-1], canon, True
    )

    d_proj = jnp.concatenate([dq_t, turn(dkv[:HEAD], cosine, sine, True).astype(low), dkv[HEAD:].astype(low)], axis=0)
    qkv_grad_part = jnp.dot(d_proj, normed_one, preferred_element_type=f32)
    d_normed_one = lax.dot_general(d_proj, qkv_full, (((0,), (0,)), ((), ())), preferred_element_type=f32)
    d_normed_two = dn_one + dn_two
    d_hat = d_normed_one * gain_one + d_normed_two * gain_two
    d_in = (
        d_hat - jnp.mean(d_hat, axis=-1, keepdims=True) - xhat * jnp.mean(d_hat * xhat, axis=-1, keepdims=True)
    ) * inv_sigma
    input_grad = (dy.astype(f32) + d_in).astype(low)
    dy_column = jnp.sum(dy.astype(f32), axis=0)
    bias_grad = jnp.concatenate([bias_grad_near, bias_grad_far], axis=0).reshape(-1, unit_count)
    bias_grad = lax.dot_general(
        is_entry.astype(f32), bias_grad, (((0,), (0,)), ((), ())), precision=lax.Precision.HIGHEST, preferred_element_type=f32
    ).reshape(FF)
    vector_part = jnp.concatenate(
        [
            jnp.sum(d_normed_one * xhat, axis=0),
            jnp.sum(d_normed_one, axis=0),
            jnp.sum(d_normed_two * xhat, axis=0),
            jnp.sum(d_normed_two, axis=0),
            jnp.sum(d_proj.astype(f32), axis=1),
            dy_column,
            bias_grad,
            dy_column,
        ]
    )
    head_part = jnp.concatenate(
        [
            qkv_grad_part.reshape(seq_count, qkv_rows, D),
            jnp.pad(vector_part.reshape(seq_count, vec_len), ((0, 0), (0, vec_pad))).reshape(seq_count, vec_rows, D),
            jnp.zeros((seq_count, head_rows - used, D), f32),
        ],
        axis=1,
    )
    head_sum = sum_bits(head_part.reshape(bit_shape + (-1, D)), [core_bit] + y_then_x[::-1], canon, True)

    batch_canon = x_bits[::-1] + [core_bit]

    def spread(part):
        return gather_bits(part.astype(low), x_bits + [core_bit], batch_canon, True).reshape(-1, D).astype(f32)

    head_grad, out_grad, up_grad, down_grad = spread(head_sum), spread(out_sum), spread(up_sum), spread(down_sum).T
    qkv_grad = head_grad[:qkv_rows]
    vector_grad = head_grad[qkv_rows:used].reshape(-1)[:vec_len]
    qkv_states = soap_step(qkv_weight, qkv_grad, qkv_first, qkv_second, bases[0], True)
    out_states = soap_step(out_weight, out_grad, out_first, out_second, bases[1], True)
    up_states = soap_step(up_weight, up_grad, up_first, up_second, bases[2], True)
    down_states = soap_step(down_weight, down_grad, down_first, down_second, bases[3], False)
    vector_states = adam_step(vectors, vector_grad, vector_first, vector_second)
    states = (qkv_states, out_states, up_states, down_states, vector_states)
    return (
        outputs.reshape(inputs.shape),
        input_grad.reshape(inputs.shape),
        qkv_grad,
        out_grad,
        up_grad,
        down_grad,
        vector_grad,
        *(state[1] for state in states),
        *(state[2] for state in states),
        *(state[0] for state in states),
    )


def solution(mesh):
    tokens = P("batch", "seq", None)
    rows, columns, flat = P("seq", None), P(None, "seq"), P("seq")
    params = (rows, rows, rows, columns, flat)
    return jax.shard_map(
        shards,
        mesh=mesh,
        in_specs=(tokens, tokens, P("batch", None)) + params + (P(),) + params + params,
        out_specs=(tokens, tokens) + params * 4,
        check_vma=False,
    )
```

time: 1230 us -> 401 us (0.33)
  waiting for transfers between devices: 882 us -> 147 us
  blocking collectives: 92.1 us -> 0 us
  matrix products: 110 us -> 42.8 us
  starting transfers between devices: 0.5 us -> 67.6 us
  Pallas kernels: 0 us -> 47.4 us
  other arithmetic: 56.7 us -> 39.8 us
  between operations: 16.7 us -> 2.67 us
    reduce_scatter x4 -> x0, waiting for transfers between devices: 460 us -> none  [the longest x1 166 us: shards(): lax.psum_scatter(up_part, 'seq', scatter_dimension=0, tiled=True)]
    all_gather x5 -> x0, waiting for transfers between devices: 216 us -> none  [the longest x1 75.6 us: shards(): lax.all_gather(up_weight.astype(jnp.bfloat16), 'seq', axis=0, tiled=True)]
    psum x2 -> x0, waiting for transfers between devices: 175 us -> none  [the longest x1 105 us: spread_2(): return lax.psum(jnp.where(mine, value, jnp.zeros_like(value)), axis)]
    ppermute x0 -> x56, waiting for transfers between devices: none -> 147 us  [the longest x48 129 us: swap(): lax.ppermute(value, axis, [(i, i ^ step) for i in range(lax.axis_size(axi...]
    dot_general x40 -> x8, matrix products: 102 us -> 11.3 us  [the longest x1 2.26 us: shards(): lax.dot_general(d_proj, qkv_full, (((0,), (0,)), ((), ())), preferred_ele...]
    unnamed x2 -> x0, blocking collectives: 76.6 us -> none
    ppermute x0 -> x56, starting transfers between devices: none -> 67.6 us  [the longest x48 51.3 us: swap(): lax.ppermute(value, axis, [(i, i ^ step) for i in range(lax.axis_size(axi...]
    pallas_call x0 -> x3, Pallas kernels: none -> 47.4 us  [the longest x2 26.1 us: feed(): pl.pallas_call(feed_kernel, grid=(units // step,), in_specs=[whole, whole...]
  transfers between devices with their start and end apart: 12 -> 56, of which waited for: 11 -> 30; matrix products, arithmetic and copies ran while one was open for 9% -> 27% of each run, Pallas kernels for 0% -> 12%
where the time goes in v1:
time: 401 us; the launch traced here: 393 us
  waiting for transfers between devices  147 us (37%)
  starting transfers between devices  67.6 us (17%)
  Pallas kernels  47.4 us (12%)
  local copies, waits for them, and re-layouts  46 us (11%)
  matrix products  42.8 us (11%)
  other arithmetic  39.8 us (10%)
    ppermute x48, waiting for transfers between devices, swap(): lax.ppermute(value, axis, [(i, i ^ step) for i in range(lax.axis_size(axi...  129 us
    ppermute x48, starting transfers between devices, swap(): lax.ppermute(value, axis, [(i, i ^ step) for i in range(lax.axis_size(axi...  51.3 us
    dot_general x8, matrix products, matmul_exact(): jnp.dot(left, right, precision=lax.Precision.HIGHEST, preferred_element_t...  31.5 us
    unnamed x172, local copies, waits for them, and re-layouts  28.9 us
    pallas_call x2, Pallas kernels, feed(): pl.pallas_call(feed_kernel, grid=(units // step,), in_specs=[whole, whole...  26.1 us
    pallas_call x1, Pallas kernels, attention(): pl.pallas_call(functools.partial(attention_kernel, blocks, 4), grid=(rows...  21.3 us
    ppermute x4, waiting for transfers between devices, shards(): lax.ppermute(dkv_sent[i - 1], 'seq', [(j + i, j) for j in range(seq_count...  15.3 us
    another operation x43, other arithmetic, gather_bits(): value = jnp.stack(pair, axis=place(have, bit, canon))  11.3 us
  transfers between devices with their start and end apart: 56, of which 30 were waited for; matrix products, arithmetic and copies ran while one was open for 27% of the time, Pallas kernels for 12%

profile of v1, /device:TPU:0, one launch (start us, length us, event | category | flops | bytes accessed | tf_op | source)
XLA Modules:
  0.0 392.9 jit_solution(13848326763098083624)
XLA Ops:
  2.6 3.1 collective-permute-start
  5.6 1.7 copy.119
  9.1 2.1 collective-permute-start.14
  20.1 2.7 copy.127
  22.7 2.7 copy.128
  26.9 3.1 collective-permute-start.6
  32.3 1.9 collective-permute-start.7
  34.2 3.6 collective-permute-done.1
  37.9 1.6 collective-permute-start.2
  39.6 3.0 collective-permute-start.15
  44.5 1.6 collective-permute-start.3
  46.1 15.4 %collective-permute-done.20 = bf16[2,96,768]{2,1,0:T(8,128)(2,1)S(1)} collective-permute-done((bf16[2,96,768]{2,1,0:T(8,128)(2,1)S(1)}, bf16[2,96,768]{2,1,0:T(8,128)(2,1)S(1)}, u32[]{:S(2)}, u32[]{:S(2)}) %collective-permute-start.20) | collective-permute-done | bytes 294944 | tf_op jit(solution)/shard_map/ppermute | solution.py:32
  61.6 1.6 collective-permute-start.21
  63.2 3.2 collective-permute-done.15
  67.9 6.1 %collective-permute-done.21 = bf16[2,2,96,768]{3,2,1,0:T(8,128)(2,1)S(1)} collective-permute-done((bf16[2,2,96,768]{3,2,1,0:T(8,128)(2,1)S(1)}, bf16[2,2,96,768]{3,2,1,0:T(8,128)(2,1)S(1)}, u32[]{:S(2)}, u32[]{:S(2)}) %collective-permute-start.21) | collective-permute-done | bytes 589856 | tf_op jit(solution)/shard_map/ppermute | solution.py:32
  74.0 1.6 fusion.183
  76.1 6.7 %collective-permute-done.16 = bf16[2,2,96,768]{3,2,1,0:T(8,128)(2,1)S(1)} collective-permute-done((bf16[2,2,96,768]{3,2,1,0:T(8,128)(2,1)S(1)}, bf16[2,2,96,768]{3,2,1,0:T(8,128)(2,1)S(1)}, u32[]{:S(2)}, u32[]{:S(2)}) %collective-permute-start.16) | collective-permute-done | bytes 589856 | tf_op jit(solution)/shard_map/ppermute | solution.py:32
  82.8 1.6 fusion.184
  84.5 1.7 convolution_convert_fusion.do_ref
  89.4 2.6 collective-permute-start.10
  93.3 5.1 %collective-permute-start.12 = (bf16[128,512]{1,0:T(8,128)(2,1)S(1)}, bf16[128,512]{1,0:T(8,128)(2,1)S(1)}, u32[]{:S(2)}, u32[]{:S(2)}) collective-permute-start(bf16[128,512]{1,0:T(8,128)(2,1)S(1)} %pad_maximum_fusion.24.refs_0_), channel_id=1, source_target_pairs={{0,12},{4,16},{8,20},{12,24},{16,28},{1,13},{5,17},{9,21},{13,25},... | collective-permute-start | bytes 393224 | tf_op jit(solution)/shard_map/ppermute | solution.py:362
  98.4 1.6 collective-permute-start.13
  104.5 2.0 collective-permute-done.10.refs_1_
  107.2 21.3 %attention.1 = (bf16[512,768]{1,0:T(8,128)(2,1)}, bf16[768,512]{1,0:T(8,128)(2,1)}, f32[128,512]{1,0:T(8,128)}, bf16[4,128,512]{2,1,0:T(8,128)(2,1)}) custom-call(bf16[768,512]{1,0:T(8,128)(2,1)} %bitcast.407, bf16[768,512]{1,0:T(8,128)(2,1)} %convolution_convert_fusion.do_ref, s32[4,1,128]{2,1,0:T(1,128)} %bitcast.416, f32[8,512]{1,0:T(8,128)} %copy-done.40, ...), custom_call_target="tpu_custom_call" | custom-call | flops 14092861440 | bytes 8388608 | tf_op jit(solution)/shard_map/attention/pallas_call | solution.py:186
  133.5 1.8 collective-permute-start.27
  135.4 2.1 fusion.192
  137.6 1.6 collective-permute-start.17
  140.4 4.2 %collective-permute-done.26 = bf16[128,512]{1,0:T(8,128)(2,1)S(1)} collective-permute-done((bf16[128,512]{1,0:T(8,128)(2,1)S(1)}, bf16[128,512]{1,0:T(8,128)(2,1)S(1)}, u32[]{:S(2)}, u32[]{:S(2)}) %collective-permute-start.26) | collective-permute-done | bytes 131104 | tf_op jit(solution)/shard_map/ppermute | solution.py:368
  144.6 10.0 %collective-permute-done.27 = bf16[128,512]{1,0:T(8,128)(2,1)S(1)} collective-permute-done((bf16[128,512]{1,0:T(8,128)(2,1)S(1)}, bf16[128,512]{1,0:T(8,128)(2,1)S(1)}, u32[]{:S(2)}, u32[]{:S(2)}) %collective-permute-start.27) | collective-permute-done | bytes 131104 | tf_op jit(solution)/shard_map/ppermute | solution.py:368
  158.7 4.5 %collective-permute-done.17 = bf16[2,2,2,96,768]{4,3,2,1,0:T(8,128)(2,1)S(1)} collective-permute-done((bf16[2,2,2,96,768]{4,3,2,1,0:T(8,128)(2,1)S(1)}, bf16[2,2,2,96,768]{4,3,2,1,0:T(8,128)(2,1)S(1)}, u32[]{:S(2)}, u32[]{:S(2)}) %collective-permute-start.17) | collective-permute-done | bytes 1179680 | tf_op jit(solution)/shard_map/ppermute | solution.py:32
  163.8 1.5 collective-permute-start.37
  166.2 3.8 collective-permute-done.37
  170.0 9.1 %collective-permute-start.38 = (bf16[2,24,768]{2,1,0:T(8,128)(2,1)S(1)}, bf16[2,24,768]{2,1,0:T(8,128)(2,1)S(1)}, u32[]{:S(2)}, u32[]{:S(2)}) collective-permute-start(bf16[2,24,768]{2,1,0:T(8,128)(2,1)S(1)} %fusion.135), channel_id=1, source_target_pairs={{0,16},{4,20},{8,24},{12,28},{16,0},{20,4},{24,8},{28,12},{1,17},{... | collective-permute-start | bytes 221192 | tf_op jit(solution)/shard_map/ppermute | solution.py:32
  179.2 2.3 fusion.190
  181.4 1.6 collective-permute-done.38
  184.3 13.3 %feed.3 = (f32[512,768]{1,0:T(8,128)}, f32[512,768]{1,0:T(8,128)}, f32[1536,768]{1,0:T(8,128)}, f32[1536,768]{1,0:T(8,128)}, f32[1,1536]{1,0:T(1,128)}) custom-call(bf16[512,768]{1,0:T(8,128)(2,1)} %fusion.41.n_ref, bf16[512,768]{1,0:T(8,128)(2,1)} %bitcast.378, bf16[1536,768]{1,0:T(8,128)(2,1)} %bitcast.398, bf16[1536,768]{1,0:T(8,128)(2,1)} %bitcast.396, ...), custom_call_target="tpu_custom_call" | custom-call | flops 7247757312 | bytes 8388608 | tf_op jit(solution)/shard_map/feed/pallas_call | solution.py:247
  197.6 1.5 fusion.136
  200.6 12.8 %feed.2 = (f32[512,768]{1,0:T(8,128)}, f32[512,768]{1,0:T(8,128)}, bf16[1536,768]{1,0:T(8,128)(2,1)}, bf16[1536,768]{1,0:T(8,128)(2,1)}, f32[1,1536]{1,0:T(1,128)}) custom-call(bf16[512,768]{1,0:T(8,128)(2,1)} %fusion.41.n_ref, bf16[512,768]{1,0:T(8,128)(2,1)} %bitcast.379, bf16[1536,768]{1,0:T(8,128)(2,1)} %collective-permute-done.18.up_ref, ...), custom_call_target="tpu_custom_call" | custom-call | flops 7247757312 | bytes 8388608 | tf_op jit(solution)/shard_map/feed/pallas_call | solution.py:247
  217.8 5.2 %add_reduce_fusion = (f32[768]{0:T(1024)S(1)}, f32[768]{0:T(1024)S(1)}, f32[512]{0:T(512)S(1)}, f32[512]{0:T(512)}, f32[512,768]{1,0:T(8,128)}, /*index=5*/f32[768]{0:T(1024)S(1)}, f32[768]{0:T(1024)S(1)}) fusion(f32[512,768]{1,0:T(8,128)} %get-tuple-element.42, f32[512,768]{1,0:T(8,128)} %get-tuple-element.43, f32[512]{0:T(512)} %get-tuple-element.255, ...), kind=kLoop, calls=%fused_computation.364 | loop fusion | flops 6287360 | bytes 7104512 | tf_op jit(solution)/shard_map/reduce_sum | solution.py:412
  239.3 1.5 select_bitcast_fusion.33
  243.3 2.8 fusion.111
  246.1 3.2 fusion.91
  249.6 4.2 %collective-permute-done.29 = bf16[2,2,2,32,768]{4,3,2,1,0:T(8,128)(2,1)S(1)} collective-permute-done((bf16[2,2,2,32,768]{4,3,2,1,0:T(8,128)(2,1)S(1)}, bf16[2,2,2,32,768]{4,3,2,1,0:T(8,128)(2,1)S(1)}, u32[]{:S(2)}, u32[]{:S(2)}) %collective-permute-start.29) | collective-permute-done | bytes 393248 | tf_op jit(solution)/shard_map/ppermute | solution.py:32
  255.8 4.3 %collective-permute-done.30 = bf16[2,2,32,768]{3,2,1,0:T(8,128)(2,1)S(1)} collective-permute-done((bf16[2,2,32,768]{3,2,1,0:T(8,128)(2,1)S(1)}, bf16[2,2,32,768]{3,2,1,0:T(8,128)(2,1)S(1)}, u32[]{:S(2)}, u32[]{:S(2)}) %collective-permute-start.30) | collective-permute-done | bytes 196640 | tf_op jit(solution)/shard_map/ppermute | solution.py:32
  260.2 3.4 collective-permute-start.31
  263.7 1.8 fusion.33
  265.5 1.8 collective-permute-done.31
  267.4 4.1 %collective-permute-done.32 = bf16[32,768]{1,0:T(8,128)(2,1)S(1)} collective-permute-done((bf16[32,768]{1,0:T(8,128)(2,1)S(1)}, bf16[32,768]{1,0:T(8,128)(2,1)S(1)}, u32[]{:S(2)}, u32[]{:S(2)}) %collective-permute-start.32) | collective-permute-done | bytes 49184 | tf_op jit(solution)/shard_map/ppermute | solution.py:32
  273.6 2.1 collective-permute-done.33
  280.8 24.0 %collective-permute-done.43 = bf16[2,2,2,96,768]{4,3,2,1,0:T(8,128)(2,1)S(1)} collective-permute-done((bf16[2,2,2,96,768]{4,3,2,1,0:T(8,128)(2,1)S(1)}, bf16[2,2,2,96,768]{4,3,2,1,0:T(8,128)(2,1)S(1)}, u32[]{:S(2)}, u32[]{:S(2)}) %collective-permute-start.43) | collective-permute-done | bytes 1179680 | tf_op jit(solution)/shard_map/ppermute | solution.py:32
  308.1 3.4 fusion.70
  311.5 8.6 %collective-permute-done.44 = bf16[2,2,96,768]{3,2,1,0:T(8,128)(2,1)S(1)} collective-permute-done((bf16[2,2,96,768]{3,2,1,0:T(8,128)(2,1)S(1)}, bf16[2,2,96,768]{3,2,1,0:T(8,128)(2,1)S(1)}, u32[]{:S(2)}, u32[]{:S(2)}) %collective-permute-start.44) | collective-permute-done | bytes 589856 | tf_op jit(solution)/shard_map/ppermute | solution.py:32
  320.3 2.4 collective-permute-start.45
  322.9 2.2 collective-permute-start.52
  325.0 16.1 %collective-permute-done.45 = bf16[2,96,768]{2,1,0:T(8,128)(2,1)S(1)} collective-permute-done((bf16[2,96,768]{2,1,0:T(8,128)(2,1)S(1)}, bf16[2,96,768]{2,1,0:T(8,128)(2,1)S(1)}, u32[]{:S(2)}, u32[]{:S(2)}) %collective-permute-start.45) | collective-permute-done | bytes 294944 | tf_op jit(solution)/shard_map/ppermute | solution.py:32
  342.3 5.1 %collective-permute-done.52 = bf16[2,96,768]{2,1,0:T(8,128)(2,1)S(1)} collective-permute-done((bf16[2,96,768]{2,1,0:T(8,128)(2,1)S(1)}, bf16[2,96,768]{2,1,0:T(8,128)(2,1)S(1)}, u32[]{:S(2)}, u32[]{:S(2)}) %collective-permute-start.52) | collective-permute-done | bytes 294944 | tf_op jit(solution)/shard_map/ppermute | solution.py:32
  347.6 3.0 collective-permute-done.46
  351.2 2.4 collective-permute-done.53
  355.2 1.8 collective-permute-done.47
  356.9 2.6 collective-permute-done.54
  362.7 3.6 fusion.74
  366.4 6.4 %fusion.61 = f32[768,384]{0,1:T(8,128)} fusion(f32[768,384]{0,1:T(8,128)S(1)} %copy-done.14, f32[4,768,768]{2,1,0:T(8,128)} %param.27, f32[768,384]{0,1:T(8,128)S(1)} %get-tuple-element.182, f32[768,384]{0,1:T(8,128)S(1)} %get-tuple-element.183), kind=kOutput, calls=%fused_computation.78 | convolution fusion | flops 2719678464 | bytes 7077888 | tf_op jit(solution)/shard_map/dot_general | solution.py:80
  381.5 3.7 fusion.73
  385.2 7.5 %fusion.52 = f32[384,768]{1,0:T(8,128)} fusion(f32[384,768]{1,0:T(8,128)S(1)} %copy-done.39, f32[4,768,768]{2,1,0:T(8,128)} %param.27, f32[384,768]{1,0:T(8,128)S(1)} %get-tuple-element.184, f32[384,768]{1,0:T(8,128)S(1)} %get-tuple-element.185), kind=kOutput, calls=%fused_computation.74 | convolution fusion | flops 2719678464 | bytes 7077888 | tf_op jit(solution)/shard_map/dot_general | solution.py:80
  (404 shorter events, 96.1 us)
Async XLA Ops:
  2.6 27.4 %collective-permute-start = (bf16[32,768]{1,0:T(8,128)(2,1)S(1)}, bf16[32,768]{1,0:T(8,128)(2,1)}, u32[]{:S(2)}, u32[]{:S(2)}) collective-permute-start(bf16[32,768]{1,0:T(8,128)(2,1)S(1)} %fusion.141), channel_id=1, source_target_pairs={{0,8},{4,12},{8,0},{12,4},{16,24},{20,28},{24,16},{28,20},{1,9},{5... | collective-permute-start | bytes 147464 | tf_op jit(solution)/shard_map/ppermute | solution.py:32
  8.1 31.4 %collective-permute-start.19 = (bf16[96,768]{1,0:T(8,128)(2,1)}, bf16[96,768]{1,0:T(8,128)(2,1)S(1)}, u32[]{:S(2)}, u32[]{:S(2)}) collective-permute-start(bf16[96,768]{1,0:T(8,128)(2,1)} %get-tuple-element.191), channel_id=1, source_target_pairs={{0,8},{4,12},{8,0},{12,4},{16,24},{20,28},{24,16},{28,20},{1,9},{5... | collective-permute-start | bytes 442376 | tf_op jit(solution)/shard_map/ppermute | solution.py:32
  9.1 30.5 %collective-permute-start.14 = (bf16[96,768]{1,0:T(8,128)(2,1)S(1)}, bf16[96,768]{1,0:T(8,128)(2,1)S(1)}, u32[]{:S(2)}, u32[]{:S(2)}) collective-permute-start(bf16[96,768]{1,0:T(8,128)(2,1)S(1)} %dynamic-slice_convert_fusion.6), channel_id=1, source_target_pairs={{0,8},{4,12},{8,0},{12,4},{16,24},{20,28},{24,16},{28,20},{1,9},{5... | collective-permute-start | bytes 442376 | tf_op jit(solution)/shard_map/ppermute | solution.py:32
  12.6 13.3 %collective-permute-start.5 = (bf16[24,768]{1,0:T(8,128)(2,1)}, bf16[24,768]{1,0:T(8,128)(2,1)}, u32[]{:S(2)}, u32[]{:S(2)}) collective-permute-start(bf16[24,768]{1,0:T(8,128)(2,1)} %dynamic-slice_convert_fusion.11), channel_id=1, source_target_pairs={{0,8},{4,12},{8,0},{12,4},{16,24},{20,28},{24,16},{28,20},{1,9},{5... | collective-permute-start | bytes 110600 | tf_op jit(solution)/shard_map/ppermute | solution.py:32
  19.4 69.4 %copy-start.40 = (f32[8,512]{1,0:T(8,128)}, f32[8,512]{1,0:T(8,128)S(1)}, u32[]{:S(2)}) copy-start(f32[8,512]{1,0:T(8,128)S(1)} %get-tuple-element.250.cos_ref) | copy-start | bytes 49156
  26.9 5.4 %collective-permute-start.6 = (bf16[2,24,768]{2,1,0:T(8,128)(2,1)S(1)}, bf16[2,24,768]{2,1,0:T(8,128)(2,1)S(1)}, u32[]{:S(2)}, u32[]{:S(2)}) collective-permute-start(bf16[2,24,768]{2,1,0:T(8,128)(2,1)S(1)} %pad_maximum_fusion.27), channel_id=1, source_target_pairs={{0,16},{4,20},{8,24},{12,28},{16,0},{20,4},{24,8},{28,12},{1,17},{... | collective-permute-start | bytes 221192 | tf_op jit(solution)/shard_map/ppermute | solution.py:32
  30.8 7.0 %collective-permute-start.1 = (bf16[2,32,768]{2,1,0:T(8,128)(2,1)S(1)}, bf16[2,32,768]{2,1,0:T(8,128)(2,1)S(1)}, u32[]{:S(2)}, u32[]{:S(2)}) collective-permute-start(bf16[2,32,768]{2,1,0:T(8,128)(2,1)S(1)} %pad_maximum_fusion.25), channel_id=1, source_target_pairs={{0,16},{4,20},{8,24},{12,28},{16,0},{20,4},{24,8},{28,12},{1,17},{... | collective-permute-start | bytes 294920 | tf_op jit(solution)/shard_map/ppermute | solution.py:32
  32.3 10.2 %collective-permute-start.7 = (bf16[2,2,24,768]{3,2,1,0:T(8,128)(2,1)S(1)}, bf16[2,2,24,768]{3,2,1,0:T(8,128)(2,1)S(1)}, u32[]{:S(2)}, u32[]{:S(2)}) collective-permute-start(bf16[2,2,24,768]{3,2,1,0:T(8,128)(2,1)S(1)} %pad_maximum_fusion.22), channel_id=1, source_target_pairs={{0,2},{1,3},{2,0},{3,1},{4,6},{5,7},{6,4},{7,5},{8,10},{9,11},{10,... | collective-permute-start | bytes 442376 | tf_op jit(solution)/shard_map/ppermute | solution.py:32
  37.9 6.6 %collective-permute-start.2 = (bf16[2,2,32,768]{3,2,1,0:T(8,128)(2,1)S(1)}, bf16[2,2,32,768]{3,2,1,0:T(8,128)(2,1)S(1)}, u32[]{:S(2)}, u32[]{:S(2)}) collective-permute-start(bf16[2,2,32,768]{3,2,1,0:T(8,128)(2,1)S(1)} %pad_maximum_fusion.20), channel_id=1, source_target_pairs={{0,4},{4,0},{8,12},{12,8},{16,20},{20,16},{24,28},{28,24},{1,5},{5... | collective-permute-start | bytes 589832 | tf_op jit(solution)/shard_map/ppermute | solution.py:32
  39.5 22.0 %collective-permute-start.20 = (bf16[2,96,768]{2,1,0:T(8,128)(2,1)S(1)}, bf16[2,96,768]{2,1,0:T(8,128)(2,1)S(1)}, u32[]{:S(2)}, u32[]{:S(2)}) collective-permute-start(bf16[2,96,768]{2,1,0:T(8,128)(2,1)S(1)} %get-tuple-element.223), channel_id=1, source_target_pairs={{0,16},{4,20},{8,24},{12,28},{16,0},{20,4},{24,8},{28,12},{1,17},{... | collective-permute-start | bytes 884744 | tf_op jit(solution)/shard_map/ppermute | solution.py:32
  39.6 26.7 %collective-permute-start.15 = (bf16[2,96,768]{2,1,0:T(8,128)(2,1)S(1)}, bf16[2,96,768]{2,1,0:T(8,128)(2,1)S(1)}, u32[]{:S(2)}, u32[]{:S(2)}) collective-permute-start(bf16[2,96,768]{2,1,0:T(8,128)(2,1)S(1)} %get-tuple-element.225), channel_id=1, source_target_pairs={{0,16},{4,20},{8,24},{12,28},{16,0},{20,4},{24,8},{28,12},{1,17},{... | collective-permute-start | bytes 884744 | tf_op jit(solution)/shard_map/ppermute | solution.py:32
  42.7 24.3 %collective-permute-start.8 = (bf16[2,2,2,24,768]{4,3,2,1,0:T(8,128)(2,1)S(1)}, bf16[2,2,2,24,768]{4,3,2,1,0:T(8,128)(2,1)S(1)}, u32[]{:S(2)}, u32[]{:S(2)}) collective-permute-start(bf16[2,2,2,24,768]{4,3,2,1,0:T(8,128)(2,1)S(1)} %pad_maximum_fusion.15), channel_id=1, source_target_pairs={{0,4},{4,0},{8,12},{12,8},{16,20},{20,16},{24,28},{28,24},{1,5},{5... | collective-permute-start | bytes 884744 | tf_op jit(solution)/shard_map/ppermute | solution.py:32
  44.5 22.7 %collective-permute-start.3 = (bf16[2,2,2,32,768]{4,3,2,1,0:T(8,128)(2,1)S(1)}, bf16[2,2,2,32,768]{4,3,2,1,0:T(8,128)(2,1)S(1)}, u32[]{:S(2)}, u32[]{:S(2)}) collective-permute-start(bf16[2,2,2,32,768]{4,3,2,1,0:T(8,128)(2,1)S(1)} %pad_maximum_fusion.14), channel_id=1, source_target_pairs={{0,2},{1,3},{2,0},{3,1},{4,6},{5,7},{6,4},{7,5},{8,10},{9,11},{10,... | collective-permute-start | bytes 1179656 | tf_op jit(solution)/shard_map/ppermute | solution.py:32
  61.6 12.4 %collective-permute-start.21 = (bf16[2,2,96,768]{3,2,1,0:T(8,128)(2,1)S(1)}, bf16[2,2,96,768]{3,2,1,0:T(8,128)(2,1)S(1)}, u32[]{:S(2)}, u32[]{:S(2)}) collective-permute-start(bf16[2,2,96,768]{3,2,1,0:T(8,128)(2,1)S(1)} %get-tuple-element.203), channel_id=1, source_target_pairs={{0,2},{1,3},{2,0},{3,1},{4,6},{5,7},{6,4},{7,5},{8,10},{9,11},{10,... | collective-permute-start | bytes 1769480 | tf_op jit(solution)/shard_map/ppermute | solution.py:32
  66.4 16.3 %collective-permute-start.16 = (bf16[2,2,96,768]{3,2,1,0:T(8,128)(2,1)S(1)}, bf16[2,2,96,768]{3,2,1,0:T(8,128)(2,1)S(1)}, u32[]{:S(2)}, u32[]{:S(2)}) collective-permute-start(bf16[2,2,96,768]{3,2,1,0:T(8,128)(2,1)S(1)} %get-tuple-element.205), channel_id=1, source_target_pairs={{0,4},{4,0},{8,12},{12,8},{16,20},{20,16},{24,28},{28,24},{1,5},{5... | collective-permute-start | bytes 1769480 | tf_op jit(solution)/shard_map/ppermute | solution.py:32
  67.1 17.2 %collective-permute-start.9 = (bf16[2,2,2,2,24,768]{5,4,3,2,1,0:T(8,128)(2,1)S(1)}, bf16[2,2,2,2,24,768]{5,4,3,2,1,0:T(8,128)(2,1)S(1)}, u32[]{:S(2)}, u32[]{:S(2)}) collective-permute-start(bf16[2,2,2,2,24,768]{5,4,3,2,1,0:T(8,128)(2,1)S(1)} %pad_maximum_fusion.9), channel_id=1, source_target_pairs={{0,1},{1,0},{2,3},{3,2},{4,5},{5,4},{6,7},{7,6},{8,9},{9,8},{10,11... | collective-permute-start | bytes 1769480 | tf_op jit(solution)/shard_map/ppermute | solution.py:32
  67.4 18.9 %collective-permute-start.4 = (bf16[2,2,2,2,32,768]{5,4,3,2,1,0:T(8,128)(2,1)S(1)}, bf16[2,2,2,2,32,768]{5,4,3,2,1,0:T(8,128)(2,1)S(1)}, u32[]{:S(2)}, u32[]{:S(2)}) collective-permute-start(bf16[2,2,2,2,32,768]{5,4,3,2,1,0:T(8,128)(2,1)S(1)} %pad_maximum_fusion.8), channel_id=1, source_target_pairs={{0,1},{1,0},{2,3},{3,2},{4,5},{5,4},{6,7},{7,6},{8,9},{9,8},{10,11... | collective-permute-start | bytes 2359304 | tf_op jit(solution)/shard_map/ppermute | solution.py:32
  75.6 80.4 %collective-permute-start.22 = (bf16[2,2,2,96,768]{4,3,2,1,0:T(8,128)(2,1)}, bf16[2,2,2,96,768]{4,3,2,1,0:T(8,128)(2,1)}, u32[]{:S(2)}, u32[]{:S(2)}) collective-permute-start(bf16[2,2,2,96,768]{4,3,2,1,0:T(8,128)(2,1)} %get-tuple-element.189), channel_id=1, source_target_pairs={{0,4},{4,0},{8,12},{12,8},{16,20},{20,16},{24,28},{28,24},{1,5},{5... | collective-permute-start | bytes 3538952 | tf_op jit(solution)/shard_map/ppermute | solution.py:32
  89.4 17.0 %collective-permute-start.10 = (bf16[128,512]{1,0:T(8,128)(2,1)S(1)}, bf16[128,512]{1,0:T(8,128)(2,1)S(1)}, u32[]{:S(2)}, u32[]{:S(2)}) collective-permute-start(bf16[128,512]{1,0:T(8,128)(2,1)S(1)} %pad_maximum_fusion.24.refs_0_), channel_id=1, source_target_pairs={{0,4},{4,8},{8,12},{12,16},{16,20},{20,24},{24,28},{1,5},{5,9},{9,... | collective-permute-start | bytes 393224 | tf_op jit(solution)/shard_map/ppermute | solution.py:362
  92.0 14.5 %collective-permute-start.11 = (bf16[128,512]{1,0:T(8,128)(2,1)S(1)}, bf16[128,512]{1,0:T(8,128)(2,1)S(1)}, u32[]{:S(2)}, u32[]{:S(2)}) collective-permute-start(bf16[128,512]{1,0:T(8,128)(2,1)S(1)} %pad_maximum_fusion.24.refs_0_), channel_id=1, source_target_pairs={{0,8},{4,12},{8,16},{12,20},{16,24},{20,28},{1,9},{5,13},{9,17},{1... | collective-permute-start | bytes 393224 | tf_op jit(solution)/shard_map/ppermute | solution.py:362
  93.3 13.2 %collective-permute-start.12 = (bf16[128,512]{1,0:T(8,128)(2,1)S(1)}, bf16[128,512]{1,0:T(8,128)(2,1)S(1)}, u32[]{:S(2)}, u32[]{:S(2)}) collective-permute-start(bf16[128,512]{1,0:T(8,128)(2,1)S(1)} %pad_maximum_fusion.24.refs_0_), channel_id=1, source_target_pairs={{0,12},{4,16},{8,20},{12,24},{16,28},{1,13},{5,17},{9,21},{13,25},... | collective-permute-start | bytes 393224 | tf_op jit(solution)/shard_map/ppermute | solution.py:362
  98.4 8.1 %collective-permute-start.13 = (bf16[128,512]{1,0:T(8,128)(2,1)S(1)}, bf16[128,512]{1,0:T(8,128)(2,1)S(1)}, u32[]{:S(2)}, u32[]{:S(2)}) collective-permute-start(bf16[128,512]{1,0:T(8,128)(2,1)S(1)} %pad_maximum_fusion.24.refs_0_), channel_id=1, source_target_pairs={{0,16},{4,20},{8,24},{12,28},{1,17},{5,21},{9,25},{13,29},{2,18},{... | collective-permute-start | bytes 393224 | tf_op jit(solution)/shard_map/ppermute | solution.py:362
  129.6 7.9 %collective-permute-start.24 = (bf16[128,512]{1,0:T(8,128)(2,1)S(1)}, bf16[128,512]{1,0:T(8,128)(2,1)S(1)}, u32[]{:S(2)}, u32[]{:S(2)}) collective-permute-start(bf16[128,512]{1,0:T(8,128)(2,1)S(1)} %get-tuple-element.206), channel_id=1, source_target_pairs={{4,0},{8,4},{12,8},{16,12},{20,16},{24,20},{28,24},{5,1},{9,5},{13... | collective-permute-start | bytes 393224 | tf_op jit(solution)/shard_map/ppermute | solution.py:368
  130.9 9.4 %collective-permute-start.25 = (bf16[128,512]{1,0:T(8,128)(2,1)S(1)}, bf16[128,512]{1,0:T(8,128)(2,1)S(1)}, u32[]{:S(2)}, u32[]{:S(2)}) collective-permute-start(bf16[128,512]{1,0:T(8,128)(2,1)S(1)} %get-tuple-element.209), channel_id=1, source_target_pairs={{8,0},{12,4},{16,8},{20,12},{24,16},{28,20},{9,1},{13,5},{17,9},{2... | collective-permute-start | bytes 393224 | tf_op jit(solution)/shard_map/ppermute | solution.py:368
  132.2 12.3 %collective-permute-start.26 = (bf16[128,512]{1,0:T(8,128)(2,1)S(1)}, bf16[128,512]{1,0:T(8,128)(2,1)S(1)}, u32[]{:S(2)}, u32[]{:S(2)}) collective-permute-start(bf16[128,512]{1,0:T(8,128)(2,1)S(1)} %get-tuple-element.208), channel_id=1, source_target_pairs={{12,0},{16,4},{20,8},{24,12},{28,16},{13,1},{17,5},{21,9},{25,13},... | collective-permute-start | bytes 393224 | tf_op jit(solution)/shard_map/ppermute | solution.py:368
  133.5 21.0 %collective-permute-start.27 = (bf16[128,512]{1,0:T(8,128)(2,1)S(1)}, bf16[128,512]{1,0:T(8,128)(2,1)S(1)}, u32[]{:S(2)}, u32[]{:S(2)}) collective-permute-start(bf16[128,512]{1,0:T(8,128)(2,1)S(1)} %get-tuple-element.207), channel_id=1, source_target_pairs={{16,0},{20,4},{24,8},{28,12},{17,1},{21,5},{25,9},{29,13},{18,2},{... | collective-permute-start | bytes 393224 | tf_op jit(solution)/shard_map/ppermute | solution.py:368
  135.4 19.1 %copy-start.37 = (f32[128,512]{1,0:T(8,128)S(1)}, f32[128,512]{1,0:T(8,128)}, u32[]{:S(2)}) copy-start(f32[128,512]{1,0:T(8,128)} %get-tuple-element.40) | copy-start | bytes 786436
  137.5 17.2 %copy-start.53 = (f32[512]{0:T(512)S(1)}, f32[512]{0:T(512)}, u32[]{:S(2)}) copy-start(f32[512]{0:T(512)} %copy-done.52) | copy-start | bytes 6148
  137.5 17.3 %copy-start.30 = (bf16[768,512]{1,0:T(8,128)(2,1)S(1)}, bf16[768,512]{1,0:T(8,128)(2,1)}, u32[]{:S(2)}) copy-start(bf16[768,512]{1,0:T(8,128)(2,1)} %get-tuple-element.39) | copy-start | bytes 2359300
  137.6 25.6 %collective-permute-start.17 = (bf16[2,2,2,96,768]{4,3,2,1,0:T(8,128)(2,1)S(1)}, bf16[2,2,2,96,768]{4,3,2,1,0:T(8,128)(2,1)S(1)}, u32[]{:S(2)}, u32[]{:S(2)}) collective-permute-start(bf16[2,2,2,96,768]{4,3,2,1,0:T(8,128)(2,1)S(1)} %copy-done.22), channel_id=1, source_target_pairs={{0,2},{1,3},{2,0},{3,1},{4,6},{5,7},{6,4},{7,5},{8,10},{9,11},{10,... | collective-permute-start | bytes 3538952 | tf_op jit(solution)/shard_map/ppermute | solution.py:32
  140.4 15.3 %collective-permute-start.35 = (bf16[2,2,2,2,24,768]{5,4,3,2,1,0:T(8,128)(2,1)S(1)}, bf16[2,2,2,2,24,768]{5,4,3,2,1,0:T(8,128)(2,1)S(1)}, u32[]{:S(2)}, u32[]{:S(2)}) collective-permute-start(bf16[2,2,2,2,24,768]{5,4,3,2,1,0:T(8,128)(2,1)S(1)} %fusion.95), channel_id=1, source_target_pairs={{0,1},{1,0},{2,3},{3,2},{4,5},{5,4},{6,7},{7,6},{8,9},{9,8},{10,11... | collective-permute-start | bytes 1769480 | tf_op jit(solution)/shard_map/ppermute | solution.py:32
  155.8 7.8 %collective-permute-start.36 = (bf16[2,2,2,24,768]{4,3,2,1,0:T(8,128)(2,1)S(1)}, bf16[2,2,2,24,768]{4,3,2,1,0:T(8,128)(2,1)S(1)}, u32[]{:S(2)}, u32[]{:S(2)}) collective-permute-start(bf16[2,2,2,24,768]{4,3,2,1,0:T(8,128)(2,1)S(1)} %fusion.112), channel_id=1, source_target_pairs={{0,4},{4,0},{8,12},{12,8},{16,20},{20,16},{24,28},{28,24},{1,5},{5... | collective-permute-start | bytes 884744 | tf_op jit(solution)/shard_map/ppermute | solution.py:32
  158.6 42.0 %collective-permute-start.23 = (bf16[1536,768]{1,0:T(8,128)(2,1)S(1)}, bf16[1536,768]{1,0:T(8,128)(2,1)}, u32[]{:S(2)}, u32[]{:S(2)}) collective-permute-start(bf16[1536,768]{1,0:T(8,128)(2,1)S(1)} %bitcast.395), channel_id=1, source_target_pairs={{0,1},{1,0},{2,3},{3,2},{4,5},{5,4},{6,7},{7,6},{8,9},{9,8},{10,11... | collective-permute-start | bytes 7077896 | tf_op jit(solution)/shard_map/ppermute | solution.py:32
  163.5 37.1 %collective-permute-start.18 = (bf16[1536,768]{1,0:T(8,128)(2,1)S(1)}, bf16[1536,768]{1,0:T(8,128)(2,1)}, u32[]{:S(2)}, u32[]{:S(2)}) collective-permute-start(bf16[1536,768]{1,0:T(8,128)(2,1)S(1)} %bitcast.397), channel_id=1, source_target_pairs={{0,1},{1,0},{2,3},{3,2},{4,5},{5,4},{6,7},{7,6},{8,9},{9,8},{10,11... | collective-permute-start | bytes 7077896 | tf_op jit(solution)/shard_map/ppermute | solution.py:32
  163.8 6.2 %collective-permute-start.37 = (bf16[2,2,24,768]{3,2,1,0:T(8,128)(2,1)S(1)}, bf16[2,2,24,768]{3,2,1,0:T(8,128)(2,1)S(1)}, u32[]{:S(2)}, u32[]{:S(2)}) collective-permute-start(bf16[2,2,24,768]{3,2,1,0:T(8,128)(2,1)S(1)} %fusion.128), channel_id=1, source_target_pairs={{0,2},{1,3},{2,0},{3,1},{4,6},{5,7},{6,4},{7,5},{8,10},{9,11},{10,... | collective-permute-start | bytes 442376 | tf_op jit(solution)/shard_map/ppermute | solution.py:32
  170.0 13.0 %collective-permute-start.38 = (bf16[2,24,768]{2,1,0:T(8,128)(2,1)S(1)}, bf16[2,24,768]{2,1,0:T(8,128)(2,1)S(1)}, u32[]{:S(2)}, u32[]{:S(2)}) collective-permute-start(bf16[2,24,768]{2,1,0:T(8,128)(2,1)S(1)} %fusion.135), channel_id=1, source_target_pairs={{0,16},{4,20},{8,24},{12,28},{16,0},{20,4},{24,8},{28,12},{1,17},{... | collective-permute-start | bytes 221192 | tf_op jit(solution)/shard_map/ppermute | solution.py:32
  183.7 13.9 %collective-permute-start.39 = (bf16[24,768]{1,0:T(8,128)(2,1)S(1)}, bf16[24,768]{1,0:T(8,128)(2,1)}, u32[]{:S(2)}, u32[]{:S(2)}) collective-permute-start(bf16[24,768]{1,0:T(8,128)(2,1)S(1)} %fusion.142), channel_id=1, source_target_pairs={{0,8},{4,12},{8,0},{12,4},{16,24},{20,28},{24,16},{28,20},{1,9},{5... | collective-permute-start | bytes 110600 | tf_op jit(solution)/shard_map/ppermute | solution.py:32
  199.1 40.2 %collective-permute-start.40 = (bf16[24,768]{1,0:T(8,128)(2,1)}, bf16[24,768]{1,0:T(8,128)(2,1)}, u32[]{:S(2)}, u32[]{:S(2)}) collective-permute-start(bf16[24,768]{1,0:T(8,128)(2,1)} %fusion.136), channel_id=1, source_target_pairs={{0,2},{1,3},{2,0},{3,1},{4,6},{5,7},{6,4},{7,5},{8,10},{9,11},{10,... | collective-permute-start | bytes 110600 | tf_op jit(solution)/shard_map/ppermute | solution.py:32
  239.2 3.1 collective-permute-start.28
  240.8 1.3 collective-permute-start.41
  242.5 11.2 %collective-permute-start.29 = (bf16[2,2,2,32,768]{4,3,2,1,0:T(8,128)(2,1)S(1)}, bf16[2,2,2,32,768]{4,3,2,1,0:T(8,128)(2,1)S(1)}, u32[]{:S(2)}, u32[]{:S(2)}) collective-permute-start(bf16[2,2,2,32,768]{4,3,2,1,0:T(8,128)(2,1)S(1)} %fusion.104), channel_id=1, source_target_pairs={{0,2},{1,3},{2,0},{3,1},{4,6},{5,7},{6,4},{7,5},{8,10},{9,11},{10,... | collective-permute-start | bytes 1179656 | tf_op jit(solution)/shard_map/ppermute | solution.py:32
  246.1 17.5 %copy-start.70 = (f32[512,768]{1,0:T(8,128)S(1)}, f32[512,768]{1,0:T(8,128)}, u32[]{:S(2)}) copy-start(f32[512,768]{1,0:T(8,128)} %get-tuple-element.37) | copy-start | bytes 4718596
  249.3 26.4 %collective-permute-start.42 = (bf16[1536,768]{1,0:T(8,128)(2,1)S(1)}, bf16[1536,768]{1,0:T(8,128)(2,1)S(1)}, u32[]{:S(2)}, u32[]{:S(2)}) collective-permute-start(bf16[1536,768]{1,0:T(8,128)(2,1)S(1)} %copy-done.64), channel_id=1, source_target_pairs={{0,1},{1,0},{2,3},{3,2},{4,5},{5,4},{6,7},{7,6},{8,9},{9,8},{10,11... | collective-permute-start | bytes 7077896 | tf_op jit(solution)/shard_map/ppermute | solution.py:32
  253.8 22.0 %slice-start.5 = ((s8[4718592]{0:T(1024)(128)(4,1)}), s8[4194304]{0:T(1024)(128)(4,1)S(1)}, s32[]{:S(2)}) async-start(s8[4718592]{0:T(1024)(128)(4,1)} %bitcast.388), calls=%async_computation.5 | async-start | bytes 8388608
  253.9 6.2 %collective-permute-start.30 = (bf16[2,2,32,768]{3,2,1,0:T(8,128)(2,1)S(1)}, bf16[2,2,32,768]{3,2,1,0:T(8,128)(2,1)S(1)}, u32[]{:S(2)}, u32[]{:S(2)}) collective-permute-start(bf16[2,2,32,768]{3,2,1,0:T(8,128)(2,1)S(1)} %fusion.124), channel_id=1, source_target_pairs={{0,4},{4,0},{8,12},{12,8},{16,20},{20,16},{24,28},{28,24},{1,5},{5... | collective-permute-start | bytes 589832 | tf_op jit(solution)/shard_map/ppermute | solution.py:32
  255.8 21.2 %collective-permute-start.49 = (bf16[1536,768]{1,0:T(8,128)(2,1)S(1)}, bf16[1536,768]{1,0:T(8,128)(2,1)S(1)}, u32[]{:S(2)}, u32[]{:S(2)}) collective-permute-start(bf16[1536,768]{1,0:T(8,128)(2,1)S(1)} %copy-done.63), channel_id=1, source_target_pairs={{0,1},{1,0},{2,3},{3,2},{4,5},{5,4},{6,7},{7,6},{8,9},{9,8},{10,11... | collective-permute-start | bytes 7077896 | tf_op jit(solution)/shard_map/ppermute | solution.py:32
  260.2 7.1 %collective-permute-start.31 = (bf16[2,32,768]{2,1,0:T(8,128)(2,1)S(1)}, bf16[2,32,768]{2,1,0:T(8,128)(2,1)S(1)}, u32[]{:S(2)}, u32[]{:S(2)}) collective-permute-start(bf16[2,32,768]{2,1,0:T(8,128)(2,1)S(1)} %fusion.133), channel_id=1, source_target_pairs={{0,16},{4,20},{8,24},{12,28},{16,0},{20,4},{24,8},{28,12},{1,17},{... | collective-permute-start | bytes 294920 | tf_op jit(solution)/shard_map/ppermute | solution.py:32
  267.3 4.2 %collective-permute-start.32 = (bf16[32,768]{1,0:T(8,128)(2,1)S(1)}, bf16[32,768]{1,0:T(8,128)(2,1)S(1)}, u32[]{:S(2)}, u32[]{:S(2)}) collective-permute-start(bf16[32,768]{1,0:T(8,128)(2,1)S(1)} %fusion.139), channel_id=1, source_target_pairs={{0,8},{4,12},{8,0},{12,4},{16,24},{20,28},{24,16},{28,20},{1,9},{5... | collective-permute-start | bytes 147464 | tf_op jit(solution)/shard_map/ppermute | solution.py:32
  271.5 4.2 %collective-permute-start.33 = (bf16[32,768]{1,0:T(8,128)(2,1)S(1)}, bf16[32,768]{1,0:T(8,128)(2,1)S(1)}, u32[]{:S(2)}, u32[]{:S(2)}) collective-permute-start(bf16[32,768]{1,0:T(8,128)(2,1)S(1)} %fusion.134), channel_id=1, source_target_pairs={{0,2},{1,3},{2,0},{3,1},{4,6},{5,7},{6,4},{7,5},{8,10},{9,11},{10,... | collective-permute-start | bytes 147464 | tf_op jit(solution)/shard_map/ppermute | solution.py:32
  275.7 3.7 collective-permute-start.34
  276.4 28.4 %collective-permute-start.43 = (bf16[2,2,2,96,768]{4,3,2,1,0:T(8,128)(2,1)S(1)}, bf16[2,2,2,96,768]{4,3,2,1,0:T(8,128)(2,1)S(1)}, u32[]{:S(2)}, u32[]{:S(2)}) collective-permute-start(bf16[2,2,2,96,768]{4,3,2,1,0:T(8,128)(2,1)S(1)} %bitcast.405), channel_id=1, source_target_pairs={{0,2},{1,3},{2,0},{3,1},{4,6},{5,7},{6,4},{7,5},{8,10},{9,11},{10,... | collective-permute-start | bytes 3538952 | tf_op jit(solution)/shard_map/ppermute | solution.py:32
  278.7 28.4 %collective-permute-start.50 = (bf16[2,2,2,96,768]{4,3,2,1,0:T(8,128)(2,1)S(1)}, bf16[2,2,2,96,768]{4,3,2,1,0:T(8,128)(2,1)S(1)}, u32[]{:S(2)}, u32[]{:S(2)}) collective-permute-start(bf16[2,2,2,96,768]{4,3,2,1,0:T(8,128)(2,1)S(1)} %fusion.75), channel_id=1, source_target_pairs={{0,4},{4,0},{8,12},{12,8},{16,20},{20,16},{24,28},{28,24},{1,5},{5... | collective-permute-start | bytes 3538952 | tf_op jit(solution)/shard_map/ppermute | solution.py:32
  280.6 27.4 %copy-start.18 = (f32[112,768]{1,0:T(8,128)}, f32[112,768]{1,0:T(8,128)S(1)}, u32[]{:S(2)}) copy-start(f32[112,768]{1,0:T(8,128)S(1)} %get-tuple-element.212) | copy-start | bytes 1032196
  280.6 27.4 %copy-start.19 = (f32[112,768]{1,0:T(8,128)}, f32[112,768]{1,0:T(8,128)S(1)}, u32[]{:S(2)}) copy-start(f32[112,768]{1,0:T(8,128)S(1)} %get-tuple-element.213) | copy-start | bytes 1032196
  305.1 15.0 %collective-permute-start.44 = (bf16[2,2,96,768]{3,2,1,0:T(8,128)(2,1)S(1)}, bf16[2,2,96,768]{3,2,1,0:T(8,128)(2,1)S(1)}, u32[]{:S(2)}, u32[]{:S(2)}) collective-permute-start(bf16[2,2,96,768]{3,2,1,0:T(8,128)(2,1)S(1)} %fusion.96), channel_id=1, source_target_pairs={{0,4},{4,0},{8,12},{12,8},{16,20},{20,16},{24,28},{28,24},{1,5},{5... | collective-permute-start | bytes 1769480 | tf_op jit(solution)/shard_map/ppermute | solution.py:32
  307.4 15.3 %collective-permute-start.51 = (bf16[2,2,96,768]{3,2,1,0:T(8,128)(2,1)S(1)}, bf16[2,2,96,768]{3,2,1,0:T(8,128)(2,1)S(1)}, u32[]{:S(2)}, u32[]{:S(2)}) collective-permute-start(bf16[2,2,96,768]{3,2,1,0:T(8,128)(2,1)S(1)} %fusion.97), channel_id=1, source_target_pairs={{0,2},{1,3},{2,0},{3,1},{4,6},{5,7},{6,4},{7,5},{8,10},{9,11},{10,... | collective-permute-start | bytes 1769480 | tf_op jit(solution)/shard_map/ppermute | solution.py:32
  320.3 20.8 %collective-permute-start.45 = (bf16[2,96,768]{2,1,0:T(8,128)(2,1)S(1)}, bf16[2,96,768]{2,1,0:T(8,128)(2,1)S(1)}, u32[]{:S(2)}, u32[]{:S(2)}) collective-permute-start(bf16[2,96,768]{2,1,0:T(8,128)(2,1)S(1)} %fusion.113), channel_id=1, source_target_pairs={{0,16},{4,20},{8,24},{12,28},{16,0},{20,4},{24,8},{28,12},{1,17},{... | collective-permute-start | bytes 884744 | tf_op jit(solution)/shard_map/ppermute | solution.py:32
  322.9 24.6 %collective-permute-start.52 = (bf16[2,96,768]{2,1,0:T(8,128)(2,1)S(1)}, bf16[2,96,768]{2,1,0:T(8,128)(2,1)S(1)}, u32[]{:S(2)}, u32[]{:S(2)}) collective-permute-start(bf16[2,96,768]{2,1,0:T(8,128)(2,1)S(1)} %fusion.114), channel_id=1, source_target_pairs={{0,16},{4,20},{8,24},{12,28},{16,0},{20,4},{24,8},{28,12},{1,17},{... | collective-permute-start | bytes 884744 | tf_op jit(solution)/shard_map/ppermute | solution.py:32
  341.2 9.4 %collective-permute-start.46 = (bf16[96,768]{1,0:T(8,128)(2,1)S(1)}, bf16[96,768]{1,0:T(8,128)(2,1)S(1)}, u32[]{:S(2)}, u32[]{:S(2)}) collective-permute-start(bf16[96,768]{1,0:T(8,128)(2,1)S(1)} %fusion.129), channel_id=1, source_target_pairs={{0,8},{4,12},{8,0},{12,4},{16,24},{20,28},{24,16},{28,20},{1,9},{5... | collective-permute-start | bytes 442376 | tf_op jit(solution)/shard_map/ppermute | solution.py:32
  347.5 6.1 %collective-permute-start.53 = (bf16[96,768]{1,0:T(8,128)(2,1)S(1)}, bf16[96,768]{1,0:T(8,128)(2,1)S(1)}, u32[]{:S(2)}, u32[]{:S(2)}) collective-permute-start(bf16[96,768]{1,0:T(8,128)(2,1)S(1)} %fusion.130), channel_id=1, source_target_pairs={{0,8},{4,12},{8,0},{12,4},{16,24},{20,28},{24,16},{28,20},{1,9},{5... | collective-permute-start | bytes 442376 | tf_op jit(solution)/shard_map/ppermute | solution.py:32
  350.6 6.3 %collective-permute-start.47 = (bf16[96,768]{1,0:T(8,128)(2,1)S(1)}, bf16[96,768]{1,0:T(8,128)(2,1)S(1)}, u32[]{:S(2)}, u32[]{:S(2)}) collective-permute-start(bf16[96,768]{1,0:T(8,128)(2,1)S(1)} %fusion.118), channel_id=1, source_target_pairs={{0,2},{1,3},{2,0},{3,1},{4,6},{5,7},{6,4},{7,5},{8,10},{9,11},{10,... | collective-permute-start | bytes 442376 | tf_op jit(solution)/shard_map/ppermute | solution.py:32
  353.7 5.8 %collective-permute-start.54 = (bf16[96,768]{1,0:T(8,128)(2,1)S(1)}, bf16[96,768]{1,0:T(8,128)(2,1)S(1)}, u32[]{:S(2)}, u32[]{:S(2)}) collective-permute-start(bf16[96,768]{1,0:T(8,128)(2,1)S(1)} %fusion.116), channel_id=1, source_target_pairs={{0,2},{1,3},{2,0},{3,1},{4,6},{5,7},{6,4},{7,5},{8,10},{9,11},{10,... | collective-permute-start | bytes 442376 | tf_op jit(solution)/shard_map/ppermute | solution.py:32
  359.6 2.0 collective-permute-start.55
  361.1 17.3 %collective-permute-start.48 = (bf16[2,96,768]{2,1,0:T(8,128)(2,1)}, bf16[2,96,768]{2,1,0:T(8,128)(2,1)}, u32[]{:S(2)}, u32[]{:S(2)}) collective-permute-start(bf16[2,96,768]{2,1,0:T(8,128)(2,1)} %pad_maximum_fusion.18), channel_id=1, source_target_pairs={{0,1},{1,0},{2,3},{3,2},{4,5},{5,4},{6,7},{7,6},{8,9},{9,8},{10,11... | collective-permute-start | bytes 884744 | tf_op jit(solution)/shard_map/ppermute | solution.py:32
  (70 other events, 398.7 us)

commit v2 on v1

--- a/solution.py
+++ b/solution.py
@@ -25,6 +25,7 @@
 low = jnp.bfloat16
 f32 = jnp.float32
 VMEM_LIMIT = 56 * 1024 * 1024
+GROUPS = 2
 
 
 def swap(value, bit):
@@ -37,47 +38,68 @@
     return lax.rem(lax.axis_index(axis) // step, 2)
 
 
-def place(have, bit, canon):
-    return sum(1 for other in have if canon.index(other) < canon.index(bit))
-
-
-def gather_bits(piece, order, canon, absolute):
-    have = []
-    value = piece
-    for bit in order:
-        got = swap(value, bit)
-        if absolute:
-            upper = mine(bit) == 1
-            pair = [jnp.where(upper, got, value), jnp.where(upper, value, got)]
-        else:
-            pair = [value, got]
-        value = jnp.stack(pair, axis=place(have, bit, canon))
-        have.append(bit)
-    return value
-
-
-def sum_bits(value, order, canon, absolute):
-    left = list(order)
-    for bit in order:
-        axis = place([b for b in left if b != bit], bit, canon)
-        if absolute:
-            own = mine(bit)
-            kept = lax.dynamic_index_in_dim(value, own, axis, keepdims=False)
-            sent = lax.dynamic_index_in_dim(value, 1 - own, axis, keepdims=False)
-        else:
-            kept = lax.index_in_dim(value, 0, axis, keepdims=False)
-            sent = lax.index_in_dim(value, 1, axis, keepdims=False)
-        value = kept.astype(f32) + swap(sent.astype(low), bit).astype(f32)
-        left.remove(bit)
-    return value
+def flow(first, *others):
+    return lax.optimization_barrier((first, *others))[0]
+
+
+def swap_z(value, step):
+    size = lax.axis_size("seq")
+    return lax.ppermute(value, "seq", [(i, i ^ (2 * step)) for i in range(size)])
+
+
+def z_index():
+    return lax.axis_index("seq") // 2
+
+
+def gather_z(piece):
+    return [piece] + [swap_z(piece, k) for k in range(1, lax.axis_size("seq") // 2)]
+
+
+def by_z(parts):
+    count = len(parts)
+    step = 1
+    while step < count:
+        upper = lax.rem(z_index() // step, 2) == 1
+        parts = [jnp.where(upper, parts[k ^ step], parts[k]) for k in range(count)]
+        step *= 2
+    return jnp.stack(parts)
+
+
+def gather_bit(value, bit, axis, absolute=False):
+    got = swap(value, bit)
+    if absolute:
+        upper = mine(bit) == 1
+        return jnp.stack([jnp.where(upper, got, value), jnp.where(upper, value, got)], axis=axis)
+    return jnp.stack([value, got], axis=axis)
+
+
+def split_bit(value, bit, axis, absolute=False):
+    if absolute:
+        own = mine(bit)
+        return (
+            lax.dynamic_index_in_dim(value, own, axis, keepdims=False),
+            lax.dynamic_index_in_dim(value, 1 - own, axis, keepdims=False).astype(low),
+        )
+    return lax.index_in_dim(value, 0, axis, keepdims=False), lax.index_in_dim(value, 1, axis, keepdims=False).astype(low)
+
+
+def sum_bit(value, bit, axis, absolute=False):
+    kept, sent = split_bit(value, bit, axis, absolute)
+    return kept.astype(f32) + swap(sent, bit).astype(f32)
+
+
+def sum_z(value, absolute=False):
+    count = value.shape[0]
+    own = z_index() if absolute else 0
+    pick = lambda k: lax.dynamic_index_in_dim(value, own ^ k, 0, keepdims=False) if absolute else value[k]
+    total = pick(0).astype(f32)
+    for k in range(1, count):
+        total = total + swap_z(pick(k).astype(low), k).astype(f32)
+    return total
 
 
 def bit_names(axis, size):
     return [(axis, 1 << k) for k in range(size.bit_length() - 1)]
-
-
-def matmul_exact(left, right):
-    return jnp.dot(left, right, precision=lax.Precision.HIGHEST, preferred_element_type=f32)
 
 
 def split_vectors(vectors):
@@ -99,13 +121,6 @@
         / (jnp.sqrt(new_second / (1.0 - beta_second**STEP)) + adam_eps)
     )
     return ratio, new_first, new_second
-
-
-def soap_step(weight, grad, first, second, basis, on_right):
-    rotated = matmul_exact(grad, basis) if on_right else matmul_exact(basis.T, grad)
-    ratio, new_first, new_second = moments(rotated, first, second)
-    unrotated = matmul_exact(ratio, basis.T) if on_right else matmul_exact(basis, ratio)
-    return (weight - matrix_rate * unrotated, new_first, new_second)
 
 
 def adam_step(weight, grad, first, second):
@@ -208,7 +223,9 @@
     )(q_t, do_t, start, cosine, sine, *kv)
 
 
-def feed_kernel(n_ref, dy_ref, up_ref, down_ref, bias_ref, out_ref, dn_ref, up_grad_ref, down_grad_ref, bias_grad_ref):
+def feed_kernel(n_ref, dy_ref, up_ref, down_ref, bias_ref, *refs):
+    out_ref, dn_ref, up_grad_ref, down_grad_ref, bias_grad_ref = refs[-5:]
+    before = refs[:-5]
     last = (((1,), (1,)), ((), ()))
     first = (((0,), (0,)), ((), ()))
     normed, d_out = n_ref[...], dy_ref[...]
@@ -224,8 +241,8 @@
 
     @pl.when(pl.program_id(0) == 0)
     def _():
-        out_ref[...] = out
-        dn_ref[...] = d_normed
+        out_ref[...] = before[0][...] + out if before else out
+        dn_ref[...] = before[1][...] + d_normed if before else d_normed
 
     @pl.when(pl.program_id(0) > 0)
     def _():
@@ -237,17 +254,18 @@
     bias_grad_ref[...] = jnp.sum(d_hidden.astype(f32), axis=0, keepdims=True)
 
 
-def feed(normed, d_out, up, down, bias, grad_type):
+def feed(normed, d_out, up, down, bias, before, grad_type):
     tokens = normed.shape[0]
     units = up.shape[0]
-    step = 512 if units % 512 == 0 else units
+    step = 256 if units % 256 == 0 else units
     whole = pl.BlockSpec((tokens, D), lambda i: (0, 0))
     part = pl.BlockSpec((step, D), lambda i: (i, 0))
     row = pl.BlockSpec((1, step), lambda i: (0, i))
+    before = before or []
     return pl.pallas_call(
         feed_kernel,
         grid=(units // step,),
-        in_specs=[whole, whole, part, part, row],
+        in_specs=[whole, whole, part, part, row] + [whole] * len(before),
         out_specs=[whole, whole, part, part, row],
         out_shape=[
             jax.ShapeDtypeStruct((tokens, D), f32),
@@ -259,7 +277,122 @@
         compiler_params=pltpu.CompilerParams(vmem_limit_bytes=VMEM_LIMIT),
         cost_estimate=pl.CostEstimate(flops=12 * tokens * units * D, bytes_accessed=8 << 20, transcendentals=0),
         name="feed",
-    )(normed, d_out, up, down, bias)
+    )(normed, d_out, up, down, bias, *before)
+
+
+def tail_kernel(
+    vec_len, x_ref, dy_ref, dq_ref, dkv_ref, cos_ref, sin_ref, w_ref, n_ref, dn_ref, gain_ref, bias_ref,
+    in_grad_ref, part_ref, flat,
+):
+    shards_of, rows = w_ref.shape[:2]
+    d_kv = dkv_ref[...]
+    a, b = d_kv[: ROT // 2], d_kv[ROT // 2 : ROT]
+    cosine, sine = cos_ref[...], sin_ref[...]
+    d_kv = jnp.concatenate([a * cosine + b * sine, b * cosine - a * sine, d_kv[ROT:]], axis=0).astype(low)
+    d_proj = jnp.concatenate([dq_ref[...], d_kv], axis=0)
+    first = (((0,), (0,)), ((), ()))
+    weight = w_ref[...].reshape(shards_of * rows, D)
+    qkv_grad = jnp.dot(d_proj, n_ref[...], preferred_element_type=f32)
+    d_one = lax.dot_general(d_proj, weight, first, preferred_element_type=f32)
+    d_two = dn_ref[...]
+    x = x_ref[...].astype(f32)
+    dy = dy_ref[...].astype(f32)
+    center = x - jnp.mean(x, axis=-1, keepdims=True)
+    inv_sigma = lax.rsqrt(jnp.mean(center * center, axis=-1, keepdims=True) + layer_eps)
+    xhat = center * inv_sigma
+    d_hat = d_one * gain_ref[0:1] + d_two * gain_ref[1:2]
+    d_in = (
+        d_hat - jnp.mean(d_hat, axis=-1, keepdims=True) - xhat * jnp.mean(d_hat * xhat, axis=-1, keepdims=True)
+    ) * inv_sigma
+    in_grad_ref[...] = (dy + d_in).astype(low)
+    columns = lambda v: jnp.sum(v, axis=0, keepdims=True)
+    dy_column = columns(dy)
+    ones = jnp.ones((8, d_proj.shape[1]), low)
+    proj_sum = lax.dot_general(ones, d_proj, (((1,), (1,)), ((), ())), preferred_element_type=f32)[0:1]
+    pieces = [columns(d_one * xhat), columns(d_one), columns(d_two * xhat), columns(d_two)]
+    pieces += [proj_sum, dy_column, bias_ref[...], dy_column]
+    offset = 0
+    for piece in pieces:
+        flat[:, offset : offset + piece.shape[1]] = piece
+        offset += piece.shape[1]
+    part_ref[...] = jnp.zeros_like(part_ref)
+    for s in range(shards_of):
+        part_ref[s, :rows, :] = qkv_grad[s * rows : (s + 1) * rows]
+        left = vec_len
+        row = rows
+        while left > 0:
+            size = min(left, D)
+            begin = s * vec_len + (row - rows) * D
+            part_ref[s, row : row + 1, :size] = flat[:, begin : begin + size]
+            left -= size
+            row += 1
+
+
+def tail(x, dy, dq_t, dkv, cosine, sine, weight, normed, d_normed, gains, bias_grad, head_rows, vec_len):
+    tokens = x.shape[0]
+    shards_of = weight.shape[0]
+    total = shards_of * vec_len
+    return pl.pallas_call(
+        functools.partial(tail_kernel, vec_len),
+        out_shape=[
+            jax.ShapeDtypeStruct((tokens, D), low),
+            jax.ShapeDtypeStruct((shards_of, head_rows, D), f32),
+        ],
+        scratch_shapes=[pltpu.VMEM((1, total), f32)],
+        compiler_params=pltpu.CompilerParams(vmem_limit_bytes=VMEM_LIMIT),
+        cost_estimate=pl.CostEstimate(flops=4 * tokens * 896 * D, bytes_accessed=8 << 20, transcendentals=0),
+        name="tail",
+    )(x, dy, dq_t, dkv, cosine, sine, weight, normed, d_normed, gains, bias_grad)
+
+
+def split_low(value):
+    high = value.astype(low)
+    return high, (value - high.astype(f32)).astype(low)
+
+
+def update_kernel(
+    across, g_ref, basis_ref, w_ref, first_ref, second_ref, grad_ref, first_new_ref, second_new_ref, w_new_ref, b_high, b_low
+):
+    @pl.when(pl.program_id(0) == 0)
+    def _():
+        high, rest = split_low(basis_ref[...])
+        b_high[...] = high
+        b_low[...] = rest
+
+    high, rest = b_high[...], b_low[...]
+    grad = g_ref[...]
+    rotated = jnp.dot(grad, high, preferred_element_type=f32) + jnp.dot(grad, rest, preferred_element_type=f32)
+    grad = grad.astype(f32)
+    if across:
+        rotated, grad = rotated.T, grad.T
+    grad_ref[...] = grad
+    ratio, first_new, second_new = moments(rotated, first_ref[...], second_ref[...])
+    first_new_ref[...] = first_new
+    second_new_ref[...] = second_new
+    r_high, r_rest = split_low(ratio)
+    if across:
+        product = lambda r, b: jnp.dot(b, r, preferred_element_type=f32)
+    else:
+        product = lambda r, b: lax.dot_general(r, b, (((1,), (1,)), ((), ())), preferred_element_type=f32)
+    unrotated = product(r_high, high) + (product(r_high, rest) + product(r_rest, high))
+    w_new_ref[...] = w_ref[...] - matrix_rate * unrotated
+
+
+def update(grad, bases, number, weight, first, second, across=False):
+    count = grad.shape[0]
+    step = 128 if count % 128 == 0 else count
+    block = pl.BlockSpec((D, step), lambda i: (0, i)) if across else pl.BlockSpec((step, D), lambda i: (i, 0))
+    return pl.pallas_call(
+        functools.partial(update_kernel, across),
+        grid=(count // step,),
+        in_specs=[pl.BlockSpec((step, D), lambda i: (i, 0)), pl.BlockSpec((None, D, D), lambda i: (number, 0, 0)), block, block, block],
+        out_specs=[block] * 4,
+        out_shape=[jax.ShapeDtypeStruct(weight.shape, f32)] * 4,
+        scratch_shapes=[pltpu.VMEM((D, D), low), pltpu.VMEM((D, D), low)],
+        compiler_params=pltpu.CompilerParams(vmem_limit_bytes=VMEM_LIMIT),
+        cost_estimate=pl.CostEstimate(flops=10 * count * D * D, bytes_accessed=8 << 20, transcendentals=0),
+        name="update",
+    )(grad, bases, weight, first, second)
 
 
 def shards(
@@ -289,10 +422,7 @@
     tokens = row_count * shard_len
     y_bit, *z_bits = bit_names("seq", seq_count)
     core_bit, *x_bits = bit_names("batch", batch_count)
-    canon = z_bits[::-1] + [y_bit] + x_bits[::-1] + [core_bit]
     near = [core_bit] + x_bits[::-1] + [y_bit] + z_bits[::-1]
-    y_then_x = z_bits + [y_bit] + x_bits
-    x_then_y = z_bits + x_bits + [y_bit]
 
     qkv_rows, out_rows, up_rows, vec_len = qkv_weight.shape[0], out_weight.shape[0], up_weight.shape[0], vectors.shape[0]
     vec_rows = -(-vec_len // D)
@@ -307,14 +437,43 @@
     head_shard = jnp.concatenate(
         [qkv_weight, jnp.pad(vectors, (0, vec_pad)).reshape(vec_rows, D), jnp.zeros((head_rows - used, D), f32)], axis=0
     ).astype(low)
-    head_full = gather_bits(own_part(head_shard), y_then_x + [core_bit], canon, True).reshape(seq_count, head_rows, D)
-    out_full = gather_bits(own_part(out_weight.astype(low)), x_then_y + [core_bit], canon, True).reshape(D, D)
-    up_near = gather_bits(own_part(up_weight.astype(low)), y_then_x, near, False).reshape(-1, D)
-    down_near = gather_bits(own_part(down_weight.T.astype(low)), x_then_y, near, False).reshape(-1, D)
-    up_far = swap(up_near, core_bit)
-    down_far = swap(down_near, core_bit)
-
-    qkv_full = head_full[:, :qkv_rows].reshape(D + 2 * HEAD, D)
+    out_part = own_part(out_weight.astype(low))
+    head_part_rows = head_rows // batch_count
+    first_group = gather_z(jnp.concatenate([own_part(head_shard), out_part], axis=0))
+    by_depth = by_z(first_group)
+    head_full, out_full = by_depth[:, :head_part_rows], by_depth[:, head_part_rows:]
+    head_full = gather_bit(head_full, y_bit, 1, True)
+    for bit in x_bits:
+        out_full = gather_bit(out_full, bit, 1, True)
+    for bit in x_bits:
+        head_full = gather_bit(head_full, bit, 2, True)
+    out_full = gather_bit(out_full, y_bit, 1, True)
+    order = 2 + len(x_bits)
+    head_full = gather_bit(head_full, core_bit, order, True).reshape(seq_count, head_rows, D)
+    out_full = gather_bit(out_full, core_bit, order, True).reshape(D, D)
+
+    up_part, down_part = own_part(up_weight.astype(low)), own_part(down_weight.T.astype(low))
+    unit_rows = up_part.shape[0] // GROUPS
+    earlier_z = first_group[1]
+    feed_weights = []
+    for g in range(GROUPS):
+        rows = slice(g * unit_rows, (g + 1) * unit_rows)
+        both = flow(jnp.concatenate([up_part[rows], down_part[rows]], axis=0), earlier_z)
+        parts = gather_z(both)
+        earlier_z = parts[1]
+        parts = jnp.stack(parts)
+        up_near, down_near = parts[:, :unit_rows], parts[:, unit_rows:]
+        up_near = gather_bit(up_near, y_bit, 0)
+        for bit in x_bits:
+            down_near = gather_bit(down_near, bit, 0)
+        for bit in x_bits:
+            up_near = gather_bit(up_near, bit, 0)
+        down_near = gather_bit(down_near, y_bit, len(x_bits))
+        up_near, down_near = up_near.reshape(-1, D), down_near.reshape(-1, D)
+        feed_weights.append((up_near, down_near, swap(up_near, core_bit), swap(down_near, core_bit)))
+
+    qkv_rows_full = head_full[:, :qkv_rows]
+    qkv_full = qkv_rows_full.reshape(D + 2 * HEAD, D)
     vector_full = head_full[:, qkv_rows:used].reshape(seq_count, vec_rows * D)[:, :vec_len].reshape(-1)
     pieces = split_vectors(vector_full.astype(f32))
     gain_one, shift_one, gain_two, shift_two, qkv_bias, out_bias, up_bias, down_bias = pieces
@@ -329,7 +488,8 @@
     is_entry = entry[None, :] == device[:, None]
     bias_near = lax.dot_general(
         is_entry.astype(f32), up_bias.reshape(-1, unit_count), (((1,), (0,)), ((), ())), preferred_element_type=f32
-    ).reshape(2, 1, FF // 2)
+    )
+    bias_near = bias_near.reshape(2, -1, GROUPS, unit_rows).transpose(0, 2, 1, 3).reshape(2, GROUPS, 1, -1)
 
     first_pos = seq_index * shard_len
     query_pos = first_pos + jnp.arange(shard_len, dtype=jnp.int32)
@@ -367,79 +527,73 @@
     for i in range(1, reach + 1):
         dkv = dkv + lax.ppermute(dkv_sent[i - 1], "seq", [(j + i, j) for j in range(seq_count - i)]).astype(f32)
 
-    out_one, dn_one, up_grad_far, down_grad_far, bias_grad_far = feed(normed_two, dy, up_far, down_far, bias_near[1], low)
-    out_two, dn_two, up_grad_near, down_grad_near, bias_grad_near = feed(
-        normed_two, dy, up_near, down_near, bias_near[0], f32
-    )
+    d_hidden_sums, up_sums, down_sums = [[], []], [], []
+    sums = None
+    for g, (up_near, down_near, up_far, down_far) in enumerate(feed_weights):
+        *sums, up_grad_far, down_grad_far, bias_far = feed(normed_two, dy, up_far, down_far, bias_near[1, g], sums, low)
+        up_got, down_got = swap(up_grad_far, core_bit), swap(down_grad_far, core_bit)
+        *sums, up_grad, down_grad, bias_here = feed(normed_two, dy, up_near, down_near, bias_near[0, g], sums, f32)
+        d_hidden_sums[0].append(bias_here)
+        d_hidden_sums[1].append(bias_far)
+        shape = (2,) * len(x_bits) + (2, seq_count // 2, unit_rows, D)
+        up_sum = (up_grad + up_got.astype(f32)).reshape(shape)
+        down_sum = (down_grad + down_got.astype(f32)).reshape(shape)
+        for bit in x_bits[::-1]:
+            up_sum = sum_bit(up_sum, bit, 0)
+        down_sum = sum_bit(down_sum, y_bit, len(x_bits))
+        up_sum = sum_bit(up_sum, y_bit, 0)
+        for bit in x_bits[::-1]:
+            down_sum = sum_bit(down_sum, bit, 0)
+        both = sum_z(jnp.concatenate([up_sum, down_sum], axis=1))
+        up_sums.append(both[:unit_rows])
+        down_sums.append(both[unit_rows:])
+    mlp_out, d_normed_two = sums
 
     attn_out = lax.dot_general(context, out_full, last, preferred_element_type=f32)
-    outputs = (flat_in + attn_out + (out_one + out_two) + (out_bias + down_bias)).astype(low)
-
-    def reduce_near(near_half, far_half, order):
-        value = near_half + swap(far_half, core_bit).astype(f32)
-        bits = near[1:]
-        value = value.reshape((2,) * len(bits) + (-1, D))
-        return sum_bits(value, order[::-1], bits, False)
-
-    up_sum = reduce_near(up_grad_near, up_grad_far, y_then_x)
-    down_sum = reduce_near(down_grad_near, down_grad_far, x_then_y)
+    outputs = (flat_in + attn_out + mlp_out + (out_bias + down_bias)).astype(low)
 
     out_grad_part = lax.dot_general(dy, context, (((0,), (0,)), ((), ())), preferred_element_type=f32)
-    bit_shape = (2,) * len(canon)
-    out_sum = sum_bits(
-        out_grad_part.reshape(bit_shape + (-1, D)), [core_bit] + x_then_y[::-1], canon, True
-    )
-
-    d_proj = jnp.concatenate([dq_t, turn(dkv[:HEAD], cosine, sine, True).astype(low), dkv[HEAD:].astype(low)], axis=0)
-    qkv_grad_part = jnp.dot(d_proj, normed_one, preferred_element_type=f32)
-    d_normed_one = lax.dot_general(d_proj, qkv_full, (((0,), (0,)), ((), ())), preferred_element_type=f32)
-    d_normed_two = dn_one + dn_two
-    d_hat = d_normed_one * gain_one + d_normed_two * gain_two
-    d_in = (
-        d_hat - jnp.mean(d_hat, axis=-1, keepdims=True) - xhat * jnp.mean(d_hat * xhat, axis=-1, keepdims=True)
-    ) * inv_sigma
-    input_grad = (dy.astype(f32) + d_in).astype(low)
-    dy_column = jnp.sum(dy.astype(f32), axis=0)
-    bias_grad = jnp.concatenate([bias_grad_near, bias_grad_far], axis=0).reshape(-1, unit_count)
+    bias_grad = jnp.stack([jnp.concatenate(side, axis=0) for side in d_hidden_sums])
+    bias_grad = bias_grad.reshape(2, GROUPS, -1, unit_rows).transpose(0, 2, 1, 3).reshape(-1, unit_count)
     bias_grad = lax.dot_general(
         is_entry.astype(f32), bias_grad, (((0,), (0,)), ((), ())), precision=lax.Precision.HIGHEST, preferred_element_type=f32
-    ).reshape(FF)
-    vector_part = jnp.concatenate(
-        [
-            jnp.sum(d_normed_one * xhat, axis=0),
-            jnp.sum(d_normed_one, axis=0),
-            jnp.sum(d_normed_two * xhat, axis=0),
-            jnp.sum(d_normed_two, axis=0),
-            jnp.sum(d_proj.astype(f32), axis=1),
-            dy_column,
-            bias_grad,
-            dy_column,
-        ]
+    ).reshape(1, FF)
+    input_grad, head_part = tail(
+        inputs.reshape(tokens, D), dy, dq_t, dkv, cosine, sine, qkv_rows_full, normed_one, d_normed_two,
+        jnp.stack([gain_one, gain_two]), bias_grad, head_rows, vec_len,
     )
-    head_part = jnp.concatenate(
-        [
-            qkv_grad_part.reshape(seq_count, qkv_rows, D),
-            jnp.pad(vector_part.reshape(seq_count, vec_len), ((0, 0), (0, vec_pad))).reshape(seq_count, vec_rows, D),
-            jnp.zeros((seq_count, head_rows - used, D), f32),
-        ],
-        axis=1,
-    )
-    head_sum = sum_bits(head_part.reshape(bit_shape + (-1, D)), [core_bit] + y_then_x[::-1], canon, True)
-
-    batch_canon = x_bits[::-1] + [core_bit]
+    shape = (seq_count // 2, 2) + (2,) * len(x_bits) + (2, -1, D)
+    both = jnp.concatenate([head_part.reshape(shape), out_grad_part.reshape(shape)], axis=len(shape) - 2)
+    both = sum_bit(both, core_bit, len(shape) - 3, True)
+    head_sum, out_sum = both[..., :head_part_rows, :], both[..., head_part_rows:, :]
+    for bit in x_bits[::-1]:
+        head_sum = sum_bit(head_sum, bit, 2, True)
+    out_sum = sum_bit(out_sum, y_bit, 1, True)
+    head_sum = sum_bit(head_sum, y_bit, 1, True)
+    for bit in x_bits[::-1]:
+        out_sum = sum_bit(out_sum, bit, 1, True)
+    both = sum_z(jnp.concatenate([head_sum, out_sum], axis=1), True)
 
     def spread(part):
-        return gather_bits(part.astype(low), x_bits + [core_bit], batch_canon, True).reshape(-1, D).astype(f32)
-
-    head_grad, out_grad, up_grad, down_grad = spread(head_sum), spread(out_sum), spread(up_sum), spread(down_sum).T
-    qkv_grad = head_grad[:qkv_rows]
-    vector_grad = head_grad[qkv_rows:used].reshape(-1)[:vec_len]
-    qkv_states = soap_step(qkv_weight, qkv_grad, qkv_first, qkv_second, bases[0], True)
-    out_states = soap_step(out_weight, out_grad, out_first, out_second, bases[1], True)
-    up_states = soap_step(up_weight, up_grad, up_first, up_second, bases[2], True)
-    down_states = soap_step(down_weight, down_grad, down_first, down_second, bases[3], False)
-    vector_states = adam_step(vectors, vector_grad, vector_first, vector_second)
-    states = (qkv_states, out_states, up_states, down_states, vector_states)
+        value = part.astype(low)
+        for k, bit in enumerate(x_bits):
+            value = gather_bit(value, bit, 0, True)
+        value = gather_bit(value, core_bit, len(x_bits), True)
+        return value.reshape(batch_count, -1, D)
+
+    feed_grads = spread(jnp.concatenate(up_sums + down_sums, axis=0))
+    up_low = feed_grads[:, : GROUPS * unit_rows].reshape(-1, D)
+    down_low = feed_grads[:, GROUPS * unit_rows :].reshape(-1, D)
+    others = spread(both)
+    head_low = others[:, :head_part_rows].reshape(-1, D)
+    out_low = others[:, head_part_rows:].reshape(-1, D)
+    up_grad, *up_states = update(up_low, bases, 2, up_weight, up_first, up_second)
+    down_grad, *down_states = update(down_low, bases, 3, down_weight, down_first, down_second, True)
+    out_grad, *out_states = update(out_low, bases, 1, out_weight, out_first, out_second)
+    qkv_grad, *qkv_states = update(head_low[:qkv_rows], bases, 0, qkv_weight, qkv_first, qkv_second)
+    vector_grad = head_low[qkv_rows:used].astype(f32).reshape(-1)[:vec_len]
+    vector_new, *vector_states = adam_step(vectors, vector_grad, vector_first, vector_second)
+    states = (qkv_states, out_states, up_states, down_states, (*vector_states, vector_new))
     return (
         outputs.reshape(inputs.shape),
         input_grad.reshape(inputs.shape),
@@ -448,9 +602,9 @@
         up_grad,
         down_grad,
         vector_grad,
+        *(state[0] for state in states),
         *(state[1] for state in states),
         *(state[2] for state in states),
-        *(state[0] for state in states),
     )
 
 

time: 401 us -> 357 us (0.89)
  the two profiles are of different devices: /device:TPU:0 before, /device:TPU:9 now
where the time goes in v2:
time: 357 us; the launch traced here: 350 us
  starting transfers between devices  109 us (31%)
  Pallas kernels  96.6 us (27%)
  waiting for transfers between devices  83.5 us (23%)
  other arithmetic  29.6 us (8%)
  local copies, waits for them, and re-layouts  20.8 us (6%)
  matrix products  8.32 us (2%)
    ppermute x39, starting transfers between devices, swap(): lax.ppermute(value, axis, [(i, i ^ step) for i in range(lax.axis_size(axi...  63.3 us
    ppermute x39, waiting for transfers between devices, swap(): lax.ppermute(value, axis, [(i, i ^ step) for i in range(lax.axis_size(axi...  44.9 us
    pallas_call x4, Pallas kernels, feed(): pl.pallas_call(feed_kernel, grid=(units // step,), in_specs=[whole, whole...  40.8 us
    ppermute x18, waiting for transfers between devices, swap_z(): return lax.ppermute(value, 'seq', [(i, i ^ 2 * step) for i in range(size)])  33.8 us
    ppermute x18, starting transfers between devices, swap_z(): return lax.ppermute(value, 'seq', [(i, i ^ 2 * step) for i in range(size)])  28.4 us
    pallas_call x4, Pallas kernels, update(): pl.pallas_call(functools.partial(update_kernel, across), grid=(count // s...  26.9 us
    pallas_call x1, Pallas kernels, attention(): pl.pallas_call(functools.partial(attention_kernel, blocks, 4), grid=(rows...  21.3 us
    ppermute x4, starting transfers between devices, shards(): lax.ppermute(kv_own, 'seq', [(j, j + i) for j in range(seq_count - i)])  8.81 us
  transfers between devices with their start and end apart: 65, of which 23 were waited for; matrix products, arithmetic and copies ran while one was open for 14% of the time, Pallas kernels for 22%

profile of v2, /device:TPU:9, one launch (start us, length us, event | category | flops | bytes accessed | tf_op | source)
XLA Modules:
  0.0 350.4 jit_solution(7885913919634956512)
XLA Ops:
  3.6 2.6 collective-permute-start
  11.6 2.2 collective-permute-start.23
  14.2 1.3 collective-permute-start.3
  16.7 1.9 collective-permute-done.13
  18.5 3.1 collective-permute-start.14
  21.7 3.8 %collective-permute-start.15 = (bf16[96,768]{1,0:T(8,128)(2,1)S(1)}, bf16[96,768]{1,0:T(8,128)(2,1)S(1)}, u32[]{:S(2)}, u32[]{:S(2)}) collective-permute-start(bf16[96,768]{1,0:T(8,128)(2,1)S(1)} %pad_maximum_fusion.26), channel_id=1, source_target_pairs={{0,16},{4,20},{8,24},{12,28},{16,0},{20,4},{24,8},{28,12},{1,17},{... | collective-permute-start | bytes 442376 | tf_op jit(solution)/shard_map/ppermute | solution.py:47
  26.2 8.2 %collective-permute-start.16 = (bf16[96,768]{1,0:T(8,128)(2,1)S(1)}, bf16[96,768]{1,0:T(8,128)(2,1)S(1)}, u32[]{:S(2)}, u32[]{:S(2)}) collective-permute-start(bf16[96,768]{1,0:T(8,128)(2,1)S(1)} %pad_maximum_fusion.26), channel_id=1, source_target_pairs={{0,24},{4,28},{8,16},{12,20},{16,8},{20,12},{24,0},{28,4},{1,25},{... | collective-permute-start | bytes 442376 | tf_op jit(solution)/shard_map/ppermute | solution.py:47
  34.8 1.3 collective-permute-start.25
  36.5 1.4 collective-permute-start.4
  42.2 3.2 collective-permute-done.7
  45.4 2.5 collective-permute-start.26
  48.7 7.5 %collective-permute-start.8 = (bf16[4,2,2,24,768]{4,3,2,1,0:T(8,128)(2,1)S(1)}, bf16[4,2,2,24,768]{4,3,2,1,0:T(8,128)(2,1)S(1)}, u32[]{:S(2)}, u32[]{:S(2)}) collective-permute-start(bf16[4,2,2,24,768]{4,3,2,1,0:T(8,128)(2,1)S(1)} %pad_maximum_fusion.11), channel_id=1, source_target_pairs={{0,1},{1,0},{2,3},{3,2},{4,5},{5,4},{6,7},{7,6},{8,9},{9,8},{10,11... | collective-permute-start | bytes 1769480 | tf_op jit(solution)/shard_map/ppermute | solution.py:33
  56.4 5.9 %collective-permute-start.5 = (bf16[4,2,2,32,768]{4,3,0,1,2:T(8,128)(2,1)S(1)}, bf16[4,2,2,32,768]{4,3,0,1,2:T(8,128)(2,1)S(1)}, u32[]{:S(2)}, u32[]{:S(2)}) collective-permute-start(bf16[4,2,2,32,768]{4,3,0,1,2:T(8,128)(2,1)S(1)} %pad_maximum_fusion.10), channel_id=1, source_target_pairs={{0,1},{1,0},{2,3},{3,2},{4,5},{5,4},{6,7},{7,6},{8,9},{9,8},{10,11... | collective-permute-start | bytes 2359304 | tf_op jit(solution)/shard_map/ppermute | solution.py:33
  64.4 2.5 collective-permute-start.18
  68.0 8.1 %collective-permute-start.30 = (bf16[768,768]{1,0:T(8,128)(2,1)}, bf16[768,768]{1,0:T(8,128)(2,1)}, u32[]{:S(2)}, u32[]{:S(2)}) collective-permute-start(bf16[768,768]{1,0:T(8,128)(2,1)} %bitcast.71.down_ref), channel_id=1, source_target_pairs={{0,1},{1,0},{2,3},{3,2},{4,5},{5,4},{6,7},{7,6},{8,9},{9,8},{10,11... | collective-permute-start | bytes 3538952 | tf_op jit(solution)/shard_map/ppermute | solution.py:33
  78.7 1.7 convolution_convert_fusion.do_ref
  85.0 1.9 collective-permute-start.10
  87.0 2.8 collective-permute-start.11
  91.1 2.8 collective-permute-start.9
  96.0 1.6 fusion.20
  98.8 3.2 collective-permute-start.29
  102.8 21.3 %attention.1 = (bf16[512,768]{1,0:T(8,128)(2,1)}, bf16[768,512]{1,0:T(8,128)(2,1)}, f32[128,512]{1,0:T(8,128)}, bf16[4,128,512]{2,1,0:T(8,128)(2,1)}) custom-call(bf16[768,512]{1,0:T(8,128)(2,1)} %bitcast.348, bf16[768,512]{1,0:T(8,128)(2,1)} %convolution_convert_fusion.do_ref, s32[4,1,128]{2,1,0:T(1,128)} %bitcast.375, f32[8,512]{1,0:T(8,128)} %copy-done.21, ...), custom_call_target="tpu_custom_call" | custom-call | flops 14092861440 | bytes 8388608 | tf_op jit(solution)/shard_map/attention/pallas_call | solution.py:201
  125.3 4.0 %collective-permute-start.31 = (bf16[128,512]{1,0:T(8,128)(2,1)S(1)}, bf16[128,512]{1,0:T(8,128)(2,1)S(1)}, u32[]{:S(2)}, u32[]{:S(2)}) collective-permute-start(bf16[128,512]{1,0:T(8,128)(2,1)S(1)} %get-tuple-element.159), channel_id=1, source_target_pairs={{4,0},{8,4},{12,8},{16,12},{20,16},{24,20},{28,24},{5,1},{9,5},{13... | collective-permute-start | bytes 393224 | tf_op jit(solution)/shard_map/ppermute | solution.py:528
  129.3 1.9 collective-permute-start.32
  132.6 2.1 fusion.105
  135.5 7.3 %collective-permute-start.21 = (bf16[768,768]{1,0:T(8,128)(2,1)S(1)}, bf16[768,768]{1,0:T(8,128)(2,1)}, u32[]{:S(2)}, u32[]{:S(2)}) collective-permute-start(bf16[768,768]{1,0:T(8,128)(2,1)S(1)} %bitcast.343), channel_id=1, source_target_pairs={{0,1},{1,0},{2,3},{3,2},{4,5},{5,4},{6,7},{7,6},{8,9},{9,8},{10,11... | collective-permute-start | bytes 3538952 | tf_op jit(solution)/shard_map/ppermute | solution.py:33
  142.8 1.6 collective-permute-start.34
  144.4 2.0 fusion.104
  146.3 4.4 %collective-permute-done.34 = bf16[128,512]{1,0:T(8,128)(2,1)S(1)} collective-permute-done((bf16[128,512]{1,0:T(8,128)(2,1)S(1)}, bf16[128,512]{1,0:T(8,128)(2,1)S(1)}, u32[]{:S(2)}, u32[]{:S(2)}) %collective-permute-start.34) | collective-permute-done | bytes 131104 | tf_op jit(solution)/shard_map/ppermute | solution.py:528
  151.6 9.2 %feed.4 = (f32[512,768]{1,0:T(8,128)}, f32[512,768]{1,0:T(8,128)}, bf16[768,768]{1,0:T(8,128)(2,1)}, bf16[768,768]{1,0:T(8,128)(2,1)}, f32[1,768]{1,0:T(1,128)}) custom-call(bf16[512,768]{1,0:T(8,128)(2,1)} %get-tuple-element.125.n_ref, bf16[512,768]{1,0:T(8,128)(2,1)} %bitcast.329, bf16[768,768]{1,0:T(8,128)(2,1)} %collective-permute-done.29.up_ref, ...), custom_call_target="tpu_custom_call" | custom-call | flops 3623878656 | bytes 8388608 | tf_op jit(solution)/shard_map/feed/pallas_call | solution.py:265
  161.6 10.6 %feed.5 = (f32[512,768]{1,0:T(8,128)}, f32[512,768]{1,0:T(8,128)}, f32[768,768]{1,0:T(8,128)}, f32[768,768]{1,0:T(8,128)}, f32[1,768]{1,0:T(1,128)}) custom-call(bf16[512,768]{1,0:T(8,128)(2,1)} %get-tuple-element.125.n_ref, bf16[512,768]{1,0:T(8,128)(2,1)} %bitcast.330, bf16[768,768]{1,0:T(8,128)(2,1)} %bitcast.344, bf16[768,768]{1,0:T(8,128)(2,1)} %bitcast.71.down_ref, ...), custom_call_target="tpu_custom_call" | custom-call | flops 3623878656 | bytes 8388608 | tf_op jit(solution)/shard_map/feed/pallas_call | solution.py:265
  172.2 10.3 %feed.6 = (f32[512,768]{1,0:T(8,128)}, f32[512,768]{1,0:T(8,128)}, bf16[768,768]{1,0:T(8,128)(2,1)}, bf16[768,768]{1,0:T(8,128)(2,1)}, f32[1,768]{1,0:T(1,128)}) custom-call(bf16[512,768]{1,0:T(8,128)(2,1)} %get-tuple-element.125.n_ref, bf16[512,768]{1,0:T(8,128)(2,1)} %bitcast.331, bf16[768,768]{1,0:T(8,128)(2,1)} %collective-permute-done.21.up_ref, ...), custom_call_target="tpu_custom_call" | custom-call | flops 3623878656 | bytes 8388608 | tf_op jit(solution)/shard_map/feed/pallas_call | solution.py:265
  183.1 10.7 %feed.7 = (f32[512,768]{1,0:T(8,128)}, f32[512,768]{1,0:T(8,128)}, f32[768,768]{1,0:T(8,128)}, f32[768,768]{1,0:T(8,128)}, f32[1,768]{1,0:T(1,128)}) custom-call(bf16[512,768]{1,0:T(8,128)(2,1)} %get-tuple-element.125.n_ref, bf16[512,768]{1,0:T(8,128)(2,1)} %bitcast.332, bf16[768,768]{1,0:T(8,128)(2,1)} %bitcast.342, bf16[768,768]{1,0:T(8,128)(2,1)} %bitcast.340, ...), custom_call_target="tpu_custom_call" | custom-call | flops 3623878656 | bytes 8388608 | tf_op jit(solution)/shard_map/feed/pallas_call | solution.py:265
  198.6 1.4 maximum_bitcast_fusion.1
  200.8 1.4 fusion.71
  202.2 1.4 reshape.513.bias_ref
  203.6 7.5 %tail.1 = (bf16[512,768]{1,0:T(8,128)(2,1)}, f32[8,128,768]{2,1,0:T(8,128)}) custom-call(bf16[512,768]{1,0:T(8,128)(2,1)} %bitcast.314, bf16[512,768]{1,0:T(8,128)(2,1)} %bitcast.333, bf16[768,512]{1,0:T(8,128)(2,1)} %get-tuple-element.76.dq_ref, f32[128,512]{1,0:T(8,128)} %convert_add_fusion.6.dkv_ref, f32[8,512]{1,0:T(8,128)} %copy-done.21, ...), custom_call_target="tpu_custom_call" | custom-call | flops 1409286144 | bytes 8388608 | tf_op jit(solution)/shard_map/tail/pallas_call | solution.py:335
  211.2 1.7 fusion.21
  215.7 1.7 convert_add_fusion.2
  218.2 1.4 copy-done.4
  220.7 1.8 convert_add_fusion
  222.7 1.6 convert_add_fusion.1
  224.5 1.3 copy-done.3
  229.1 5.1 %collective-permute-done.49 = bf16[2,4,48,768]{3,2,1,0:T(8,128)(2,1)S(1)} collective-permute-done((bf16[2,4,48,768]{3,2,1,0:T(8,128)(2,1)S(1)}, bf16[2,4,48,768]{3,2,1,0:T(8,128)(2,1)S(1)}, u32[]{:S(2)}, u32[]{:S(2)}) %collective-permute-start.49) | collective-permute-done | bytes 589856 | tf_op jit(solution)/shard_map/ppermute | solution.py:33
  236.0 17.1 %collective-permute-done.38 = bf16[4,2,24,768]{3,2,1,0:T(8,128)(2,1)S(1)} collective-permute-done((bf16[4,2,24,768]{3,2,1,0:T(8,128)(2,1)S(1)}, bf16[4,2,24,768]{3,2,1,0:T(8,128)(2,1)S(1)}, u32[]{:S(2)}, u32[]{:S(2)}) %collective-permute-start.38) | collective-permute-done | bytes 294944 | tf_op jit(solution)/shard_map/ppermute | solution.py:33
  256.8 8.0 %collective-permute-done.39 = bf16[4,24,768]{2,1,0:T(8,128)(2,1)S(1)} collective-permute-done((bf16[4,24,768]{2,1,0:T(8,128)(2,1)S(1)}, bf16[4,24,768]{2,1,0:T(8,128)(2,1)S(1)}, u32[]{:S(2)}, u32[]{:S(2)}) %collective-permute-start.39) | collective-permute-done | bytes 147488 | tf_op jit(solution)/shard_map/ppermute | solution.py:33
  266.1 4.9 %collective-permute-done.37 = bf16[4,32,768]{2,1,0:T(8,128)(2,1)S(1)} collective-permute-done((bf16[4,32,768]{2,1,0:T(8,128)(2,1)S(1)}, bf16[4,32,768]{2,1,0:T(8,128)(2,1)S(1)}, u32[]{:S(2)}, u32[]{:S(2)}) %collective-permute-start.37) | collective-permute-done | bytes 196640 | tf_op jit(solution)/shard_map/ppermute | solution.py:33
  272.4 1.4 collective-permute-start.42
  274.5 1.6 collective-permute-start.51
  276.8 1.7 collective-permute-done.42
  278.6 2.9 collective-permute-done.51
  282.2 3.4 collective-permute-done.52
  285.6 8.1 %collective-permute-done.53 = bf16[96,768]{1,0:T(8,128)(2,1)S(1)} collective-permute-done((bf16[96,768]{1,0:T(8,128)(2,1)S(1)}, bf16[96,768]{1,0:T(8,128)(2,1)S(1)}, u32[]{:S(2)}, u32[]{:S(2)}) %collective-permute-start.53) | collective-permute-done | bytes 147488 | tf_op jit(solution)/shard_map/ppermute | solution.py:47
  294.1 1.5 collective-permute-start.61
  296.8 1.3 collective-permute-done.60
  298.1 2.1 collective-permute-done.61
  300.1 9.5 %collective-permute-done.62 = bf16[96,768]{1,0:T(8,128)(2,1)S(1)} collective-permute-done((bf16[96,768]{1,0:T(8,128)(2,1)S(1)}, bf16[96,768]{1,0:T(8,128)(2,1)S(1)}, u32[]{:S(2)}, u32[]{:S(2)}) %collective-permute-start.62) | collective-permute-done | bytes 147488 | tf_op jit(solution)/shard_map/ppermute | solution.py:47
  310.5 1.7 collective-permute-start.44
  312.3 4.7 %collective-permute-done.63 = bf16[192,768]{1,0:T(8,128)(2,1)S(1)} collective-permute-done((bf16[192,768]{1,0:T(8,128)(2,1)S(1)}, bf16[192,768]{1,0:T(8,128)(2,1)S(1)}, u32[]{:S(2)}, u32[]{:S(2)}) %collective-permute-start.63) | collective-permute-done | bytes 294944 | tf_op jit(solution)/shard_map/ppermute | solution.py:33
  317.1 2.4 collective-permute-start.64
  321.0 4.4 %update.5 = (f32[96,768]{1,0:T(8,128)}, f32[96,768]{1,0:T(8,128)}, f32[96,768]{1,0:T(8,128)}, f32[96,768]{1,0:T(8,128)}) custom-call(bf16[96,768]{1,0:T(8,128)(2,1)} %bitcast.362, f32[4,768,768]{2,1,0:T(8,128)} %basis_ref.7, f32[96,768]{1,0:T(8,128)} %w_ref.5, f32[96,768]{1,0:T(8,128)} %first_ref.5, f32[96,768]{1,0:T(8,128)} %second_ref.5), custom_call_target="tpu_custom_call" | custom-call | flops 566231040 | bytes 8388608 | tf_op jit(solution)/shard_map/update/pallas_call | solution.py:385
  325.5 4.6 %update.4 = (f32[112,768]{1,0:T(8,128)}, f32[112,768]{1,0:T(8,128)}, f32[112,768]{1,0:T(8,128)}, f32[112,768]{1,0:T(8,128)}) custom-call(bf16[112,768]{1,0:T(8,128)(2,1)} %slice.358.g_ref, f32[4,768,768]{2,1,0:T(8,128)} %basis_ref.7, f32[112,768]{1,0:T(8,128)} %w_ref.4, f32[112,768]{1,0:T(8,128)} %first_ref.4, f32[112,768]{1,0:T(8,128)} %second_ref.4), custom_call_target="tpu_custom_call" | custom-call | flops 660602880 | bytes 8388608 | tf_op jit(solution)/shard_map/update/pallas_call | solution.py:385
  332.3 9.1 %update.6 = (f32[384,768]{1,0:T(8,128)}, f32[384,768]{1,0:T(8,128)}, f32[384,768]{1,0:T(8,128)}, f32[384,768]{1,0:T(8,128)}) custom-call(bf16[384,768]{1,0:T(8,128)(2,1)} %bitcast.337, f32[4,768,768]{2,1,0:T(8,128)} %basis_ref.7, f32[384,768]{1,0:T(8,128)} %w_ref.6, f32[384,768]{1,0:T(8,128)} %first_ref.6, f32[384,768]{1,0:T(8,128)} %second_ref.6), custom_call_target="tpu_custom_call" | custom-call | flops 2264924160 | bytes 8388608 | tf_op jit(solution)/shard_map/update/pallas_call | solution.py:385
  341.4 8.8 %update.7 = (f32[768,384]{1,0:T(8,128)}, f32[768,384]{1,0:T(8,128)}, f32[768,384]{1,0:T(8,128)}, f32[768,384]{1,0:T(8,128)}) custom-call(bf16[384,768]{1,0:T(8,128)(2,1)} %bitcast.336, f32[4,768,768]{2,1,0:T(8,128)} %basis_ref.7, f32[768,384]{1,0:T(8,128)} %w_ref.7, f32[768,384]{1,0:T(8,128)} %first_ref.7, f32[768,384]{1,0:T(8,128)} %second_ref.7), custom_call_target="tpu_custom_call" | custom-call | flops 2264924160 | bytes 8388608 | tf_op jit(solution)/shard_map/update/pallas_call | solution.py:385
  (312 shorter events, 67.6 us)
Async XLA Ops:
  3.5 7.8 %collective-permute-start.2 = (bf16[56,768]{1,0:T(8,128)(2,1)S(1)}, bf16[56,768]{1,0:T(8,128)(2,1)S(1)}, u32[]{:S(2)}, u32[]{:S(2)}) collective-permute-start(bf16[56,768]{1,0:T(8,128)(2,1)S(1)} %pad_maximum_fusion.29), channel_id=1, source_target_pairs={{0,8},{4,12},{8,0},{12,4},{16,24},{20,28},{24,16},{28,20},{1,9},{5... | collective-permute-start | bytes 258056 | tf_op jit(solution)/shard_map/ppermute | solution.py:47
  3.6 10.4 %collective-permute-start = (bf16[56,768]{1,0:T(8,128)(2,1)S(1)}, bf16[56,768]{1,0:T(8,128)(2,1)S(1)}, u32[]{:S(2)}, u32[]{:S(2)}) collective-permute-start(bf16[56,768]{1,0:T(8,128)(2,1)S(1)} %pad_maximum_fusion.29), channel_id=1, source_target_pairs={{0,24},{4,28},{8,16},{12,20},{16,8},{20,12},{24,0},{28,4},{1,25},{... | collective-permute-start | bytes 258056 | tf_op jit(solution)/shard_map/ppermute | solution.py:47
  6.2 7.8 %collective-permute-start.1 = (bf16[56,768]{1,0:T(8,128)(2,1)S(1)}, bf16[56,768]{1,0:T(8,128)(2,1)S(1)}, u32[]{:S(2)}, u32[]{:S(2)}) collective-permute-start(bf16[56,768]{1,0:T(8,128)(2,1)S(1)} %pad_maximum_fusion.29), channel_id=1, source_target_pairs={{0,16},{4,20},{8,24},{12,28},{16,0},{20,4},{24,8},{28,12},{1,17},{... | collective-permute-start | bytes 258056 | tf_op jit(solution)/shard_map/ppermute | solution.py:47
  11.3 7.2 %collective-permute-start.13 = (bf16[96,768]{1,0:T(8,128)(2,1)S(1)}, bf16[96,768]{1,0:T(8,128)(2,1)S(1)}, u32[]{:S(2)}, u32[]{:S(2)}) collective-permute-start(bf16[96,768]{1,0:T(8,128)(2,1)S(1)} %pad_maximum_fusion.27), channel_id=1, source_target_pairs={{0,8},{4,12},{8,0},{12,4},{16,24},{20,28},{24,16},{28,20},{1,9},{5... | collective-permute-start | bytes 442376 | tf_op jit(solution)/shard_map/ppermute | solution.py:47
  11.6 10.1 %collective-permute-start.23 = (bf16[96,768]{1,0:T(8,128)(2,1)S(1)}, bf16[96,768]{1,0:T(8,128)(2,1)S(1)}, u32[]{:S(2)}, u32[]{:S(2)}) collective-permute-start(bf16[96,768]{1,0:T(8,128)(2,1)S(1)} %pad_maximum_fusion.27), channel_id=1, source_target_pairs={{0,16},{4,20},{8,24},{12,28},{16,0},{20,4},{24,8},{28,12},{1,17},{... | collective-permute-start | bytes 442376 | tf_op jit(solution)/shard_map/ppermute | solution.py:47
  13.9 12.4 %collective-permute-start.24 = (bf16[96,768]{1,0:T(8,128)(2,1)S(1)}, bf16[96,768]{1,0:T(8,128)(2,1)S(1)}, u32[]{:S(2)}, u32[]{:S(2)}) collective-permute-start(bf16[96,768]{1,0:T(8,128)(2,1)S(1)} %pad_maximum_fusion.27), channel_id=1, source_target_pairs={{0,24},{4,28},{8,16},{12,20},{16,8},{20,12},{24,0},{28,4},{1,25},{... | collective-permute-start | bytes 442376 | tf_op jit(solution)/shard_map/ppermute | solution.py:47
  14.2 20.6 %collective-permute-start.3 = (bf16[4,32,768]{2,1,0:T(8,128)(2,1)S(1)}, bf16[4,32,768]{2,1,0:T(8,128)(2,1)S(1)}, u32[]{:S(2)}, u32[]{:S(2)}) collective-permute-start(bf16[4,32,768]{2,1,0:T(8,128)(2,1)S(1)} %slice.325), channel_id=1, source_target_pairs={{0,4},{4,0},{8,12},{12,8},{16,20},{20,16},{24,28},{28,24},{1,5},{5... | collective-permute-start | bytes 589832 | tf_op jit(solution)/shard_map/ppermute | solution.py:33
  15.5 19.1 %collective-permute-start.6 = (bf16[4,24,768]{2,1,0:T(8,128)(2,1)S(1)}, bf16[4,24,768]{2,1,0:T(8,128)(2,1)S(1)}, u32[]{:S(2)}, u32[]{:S(2)}) collective-permute-start(bf16[4,24,768]{2,1,0:T(8,128)(2,1)S(1)} %pad_maximum_fusion.25), channel_id=1, source_target_pairs={{0,2},{1,3},{2,0},{3,1},{4,6},{5,7},{6,4},{7,5},{8,10},{9,11},{10,... | collective-permute-start | bytes 442376 | tf_op jit(solution)/shard_map/ppermute | solution.py:33
  18.5 17.7 %collective-permute-start.14 = (bf16[96,768]{1,0:T(8,128)(2,1)S(1)}, bf16[96,768]{1,0:T(8,128)(2,1)S(1)}, u32[]{:S(2)}, u32[]{:S(2)}) collective-permute-start(bf16[96,768]{1,0:T(8,128)(2,1)S(1)} %pad_maximum_fusion.26), channel_id=1, source_target_pairs={{0,8},{4,12},{8,0},{12,4},{16,24},{20,28},{24,16},{28,20},{1,9},{5... | collective-permute-start | bytes 442376 | tf_op jit(solution)/shard_map/ppermute | solution.py:47
  21.7 14.8 %collective-permute-start.15 = (bf16[96,768]{1,0:T(8,128)(2,1)S(1)}, bf16[96,768]{1,0:T(8,128)(2,1)S(1)}, u32[]{:S(2)}, u32[]{:S(2)}) collective-permute-start(bf16[96,768]{1,0:T(8,128)(2,1)S(1)} %pad_maximum_fusion.26), channel_id=1, source_target_pairs={{0,16},{4,20},{8,24},{12,28},{16,0},{20,4},{24,8},{28,12},{1,17},{... | collective-permute-start | bytes 442376 | tf_op jit(solution)/shard_map/ppermute | solution.py:47
  26.2 12.3 %collective-permute-start.16 = (bf16[96,768]{1,0:T(8,128)(2,1)S(1)}, bf16[96,768]{1,0:T(8,128)(2,1)S(1)}, u32[]{:S(2)}, u32[]{:S(2)}) collective-permute-start(bf16[96,768]{1,0:T(8,128)(2,1)S(1)} %pad_maximum_fusion.26), channel_id=1, source_target_pairs={{0,24},{4,28},{8,16},{12,20},{16,8},{20,12},{24,0},{28,4},{1,25},{... | collective-permute-start | bytes 442376 | tf_op jit(solution)/shard_map/ppermute | solution.py:47
  34.6 5.9 %collective-permute-start.27 = (bf16[4,48,768]{2,1,0:T(8,128)(2,1)S(1)}, bf16[4,48,768]{2,1,0:T(8,128)(2,1)S(1)}, u32[]{:S(2)}, u32[]{:S(2)}) collective-permute-start(bf16[4,48,768]{2,1,0:T(8,128)(2,1)S(1)} %get-tuple-element.145), channel_id=1, source_target_pairs={{0,2},{1,3},{2,0},{3,1},{4,6},{5,7},{6,4},{7,5},{8,10},{9,11},{10,... | collective-permute-start | bytes 884744 | tf_op jit(solution)/shard_map/ppermute | solution.py:33
  34.8 7.1 %collective-permute-start.25 = (bf16[4,48,768]{2,1,0:T(8,128)(2,1)S(1)}, bf16[4,48,768]{2,1,0:T(8,128)(2,1)S(1)}, u32[]{:S(2)}, u32[]{:S(2)}) collective-permute-start(bf16[4,48,768]{2,1,0:T(8,128)(2,1)S(1)} %get-tuple-element.146), channel_id=1, source_target_pairs={{0,4},{4,0},{8,12},{12,8},{16,20},{20,16},{24,28},{28,24},{1,5},{5... | collective-permute-start | bytes 884744 | tf_op jit(solution)/shard_map/ppermute | solution.py:33
  36.2 9.2 %collective-permute-start.7 = (bf16[4,2,24,768]{3,2,1,0:T(8,128)(2,1)S(1)}, bf16[4,2,24,768]{3,2,1,0:T(8,128)(2,1)S(1)}, u32[]{:S(2)}, u32[]{:S(2)}) collective-permute-start(bf16[4,2,24,768]{3,2,1,0:T(8,128)(2,1)S(1)} %pad_maximum_fusion.22), channel_id=1, source_target_pairs={{0,4},{4,0},{8,12},{12,8},{16,20},{20,16},{24,28},{28,24},{1,5},{5... | collective-permute-start | bytes 884744 | tf_op jit(solution)/shard_map/ppermute | solution.py:33
  36.5 12.2 %collective-permute-start.4 = (bf16[4,2,32,768]{3,2,0,1:T(8,128)(2,1)S(1)}, bf16[4,2,32,768]{3,2,0,1:T(8,128)(2,1)S(1)}, u32[]{:S(2)}, u32[]{:S(2)}) collective-permute-start(bf16[4,2,32,768]{3,2,0,1:T(8,128)(2,1)S(1)} %pad_maximum_fusion.19), channel_id=1, source_target_pairs={{0,2},{1,3},{2,0},{3,1},{4,6},{5,7},{6,4},{7,5},{8,10},{9,11},{10,... | collective-permute-start | bytes 1179656 | tf_op jit(solution)/shard_map/ppermute | solution.py:33
  38.8 17.6 %collective-permute-start.19 = (bf16[4,48,768]{2,1,0:T(8,128)(2,1)S(1)}, bf16[4,48,768]{2,1,0:T(8,128)(2,1)S(1)}, u32[]{:S(2)}, u32[]{:S(2)}) collective-permute-start(bf16[4,48,768]{2,1,0:T(8,128)(2,1)S(1)} %get-tuple-element.153), channel_id=1, source_target_pairs={{0,2},{1,3},{2,0},{3,1},{4,6},{5,7},{6,4},{7,5},{8,10},{9,11},{10,... | collective-permute-start | bytes 884744 | tf_op jit(solution)/shard_map/ppermute | solution.py:33
  40.5 21.8 %collective-permute-start.17 = (bf16[4,48,768]{2,1,0:T(8,128)(2,1)S(1)}, bf16[4,48,768]{2,1,0:T(8,128)(2,1)S(1)}, u32[]{:S(2)}, u32[]{:S(2)}) collective-permute-start(bf16[4,48,768]{2,1,0:T(8,128)(2,1)S(1)} %get-tuple-element.154), channel_id=1, source_target_pairs={{0,4},{4,0},{8,12},{12,8},{16,20},{20,16},{24,28},{28,24},{1,5},{5... | collective-permute-start | bytes 884744 | tf_op jit(solution)/shard_map/ppermute | solution.py:33
  41.9 22.5 %collective-permute-start.28 = (bf16[2,4,48,768]{3,2,1,0:T(8,128)(2,1)S(1)}, bf16[2,4,48,768]{3,2,1,0:T(8,128)(2,1)S(1)}, u32[]{:S(2)}, u32[]{:S(2)}) collective-permute-start(bf16[2,4,48,768]{3,2,1,0:T(8,128)(2,1)S(1)} %get-tuple-element.142), channel_id=1, source_target_pairs={{0,4},{4,0},{8,12},{12,8},{16,20},{20,16},{24,28},{28,24},{1,5},{5... | collective-permute-start | bytes 1769480 | tf_op jit(solution)/shard_map/ppermute | solution.py:33
  45.4 30.8 %collective-permute-start.26 = (bf16[2,4,48,768]{3,2,1,0:T(8,128)(2,1)S(1)}, bf16[2,4,48,768]{3,2,1,0:T(8,128)(2,1)S(1)}, u32[]{:S(2)}, u32[]{:S(2)}) collective-permute-start(bf16[2,4,48,768]{3,2,1,0:T(8,128)(2,1)S(1)} %get-tuple-element.148), channel_id=1, source_target_pairs={{0,2},{1,3},{2,0},{3,1},{4,6},{5,7},{6,4},{7,5},{8,10},{9,11},{10,... | collective-permute-start | bytes 1769480 | tf_op jit(solution)/shard_map/ppermute | solution.py:33
  48.7 19.3 %collective-permute-start.8 = (bf16[4,2,2,24,768]{4,3,2,1,0:T(8,128)(2,1)S(1)}, bf16[4,2,2,24,768]{4,3,2,1,0:T(8,128)(2,1)S(1)}, u32[]{:S(2)}, u32[]{:S(2)}) collective-permute-start(bf16[4,2,2,24,768]{4,3,2,1,0:T(8,128)(2,1)S(1)} %pad_maximum_fusion.11), channel_id=1, source_target_pairs={{0,1},{1,0},{2,3},{3,2},{4,5},{5,4},{6,7},{7,6},{8,9},{9,8},{10,11... | collective-permute-start | bytes 1769480 | tf_op jit(solution)/shard_map/ppermute | solution.py:33
  56.4 26.3 %collective-permute-start.5 = (bf16[4,2,2,32,768]{4,3,0,1,2:T(8,128)(2,1)S(1)}, bf16[4,2,2,32,768]{4,3,0,1,2:T(8,128)(2,1)S(1)}, u32[]{:S(2)}, u32[]{:S(2)}) collective-permute-start(bf16[4,2,2,32,768]{4,3,0,1,2:T(8,128)(2,1)S(1)} %pad_maximum_fusion.10), channel_id=1, source_target_pairs={{0,1},{1,0},{2,3},{3,2},{4,5},{5,4},{6,7},{7,6},{8,9},{9,8},{10,11... | collective-permute-start | bytes 2359304 | tf_op jit(solution)/shard_map/ppermute | solution.py:33
  62.3 18.1 %collective-permute-start.20 = (bf16[2,4,48,768]{3,2,1,0:T(8,128)(2,1)S(1)}, bf16[2,4,48,768]{3,2,1,0:T(8,128)(2,1)S(1)}, u32[]{:S(2)}, u32[]{:S(2)}) collective-permute-start(bf16[2,4,48,768]{3,2,1,0:T(8,128)(2,1)S(1)} %get-tuple-element.150), channel_id=1, source_target_pairs={{0,4},{4,0},{8,12},{12,8},{16,20},{20,16},{24,28},{28,24},{1,5},{5... | collective-permute-start | bytes 1769480 | tf_op jit(solution)/shard_map/ppermute | solution.py:33
  64.4 17.2 %collective-permute-start.18 = (bf16[2,4,48,768]{3,2,1,0:T(8,128)(2,1)S(1)}, bf16[2,4,48,768]{3,2,1,0:T(8,128)(2,1)S(1)}, u32[]{:S(2)}, u32[]{:S(2)}) collective-permute-start(bf16[2,4,48,768]{3,2,1,0:T(8,128)(2,1)S(1)} %get-tuple-element.156), channel_id=1, source_target_pairs={{0,2},{1,3},{2,0},{3,1},{4,6},{5,7},{6,4},{7,5},{8,10},{9,11},{10,... | collective-permute-start | bytes 1769480 | tf_op jit(solution)/shard_map/ppermute | solution.py:33
  68.0 83.5 %collective-permute-start.30 = (bf16[768,768]{1,0:T(8,128)(2,1)}, bf16[768,768]{1,0:T(8,128)(2,1)}, u32[]{:S(2)}, u32[]{:S(2)}) collective-permute-start(bf16[768,768]{1,0:T(8,128)(2,1)} %bitcast.71.down_ref), channel_id=1, source_target_pairs={{0,1},{1,0},{2,3},{3,2},{4,5},{5,4},{6,7},{7,6},{8,9},{9,8},{10,11... | collective-permute-start | bytes 3538952 | tf_op jit(solution)/shard_map/ppermute | solution.py:33
  85.0 13.8 %collective-permute-start.10 = (bf16[128,512]{1,0:T(8,128)(2,1)S(1)}, bf16[128,512]{1,0:T(8,128)(2,1)S(1)}, u32[]{:S(2)}, u32[]{:S(2)}) collective-permute-start(bf16[128,512]{1,0:T(8,128)(2,1)S(1)} %pad_maximum_fusion.28.refs_0_), channel_id=1, source_target_pairs={{0,8},{4,12},{8,16},{12,20},{16,24},{20,28},{1,9},{5,13},{9,17},{1... | collective-permute-start | bytes 393224 | tf_op jit(solution)/shard_map/ppermute | solution.py:522
  87.0 15.1 %collective-permute-start.11 = (bf16[128,512]{1,0:T(8,128)(2,1)S(1)}, bf16[128,512]{1,0:T(8,128)(2,1)S(1)}, u32[]{:S(2)}, u32[]{:S(2)}) collective-permute-start(bf16[128,512]{1,0:T(8,128)(2,1)S(1)} %pad_maximum_fusion.28.refs_0_), channel_id=1, source_target_pairs={{0,12},{4,16},{8,20},{12,24},{16,28},{1,13},{5,17},{9,21},{13,25},... | collective-permute-start | bytes 393224 | tf_op jit(solution)/shard_map/ppermute | solution.py:522
  89.8 12.3 %collective-permute-start.12 = (bf16[128,512]{1,0:T(8,128)(2,1)S(1)}, bf16[128,512]{1,0:T(8,128)(2,1)S(1)}, u32[]{:S(2)}, u32[]{:S(2)}) collective-permute-start(bf16[128,512]{1,0:T(8,128)(2,1)S(1)} %pad_maximum_fusion.28.refs_0_), channel_id=1, source_target_pairs={{0,16},{4,20},{8,24},{12,28},{1,17},{5,21},{9,25},{13,29},{2,18},{... | collective-permute-start | bytes 393224 | tf_op jit(solution)/shard_map/ppermute | solution.py:522
  91.1 11.0 %collective-permute-start.9 = (bf16[128,512]{1,0:T(8,128)(2,1)S(1)}, bf16[128,512]{1,0:T(8,128)(2,1)S(1)}, u32[]{:S(2)}, u32[]{:S(2)}) collective-permute-start(bf16[128,512]{1,0:T(8,128)(2,1)S(1)} %pad_maximum_fusion.28.refs_0_), channel_id=1, source_target_pairs={{0,4},{4,8},{8,12},{12,16},{16,20},{20,24},{24,28},{1,5},{5,9},{9,... | collective-permute-start | bytes 393224 | tf_op jit(solution)/shard_map/ppermute | solution.py:522
  98.8 52.7 %collective-permute-start.29 = (bf16[768,768]{1,0:T(8,128)(2,1)S(1)}, bf16[768,768]{1,0:T(8,128)(2,1)}, u32[]{:S(2)}, u32[]{:S(2)}) collective-permute-start(bf16[768,768]{1,0:T(8,128)(2,1)S(1)} %bitcast.345), channel_id=1, source_target_pairs={{0,1},{1,0},{2,3},{3,2},{4,5},{5,4},{6,7},{7,6},{8,9},{9,8},{10,11... | collective-permute-start | bytes 3538952 | tf_op jit(solution)/shard_map/ppermute | solution.py:33
  125.3 9.4 %collective-permute-start.31 = (bf16[128,512]{1,0:T(8,128)(2,1)S(1)}, bf16[128,512]{1,0:T(8,128)(2,1)S(1)}, u32[]{:S(2)}, u32[]{:S(2)}) collective-permute-start(bf16[128,512]{1,0:T(8,128)(2,1)S(1)} %get-tuple-element.159), channel_id=1, source_target_pairs={{4,0},{8,4},{12,8},{16,12},{20,16},{24,20},{28,24},{5,1},{9,5},{13... | collective-permute-start | bytes 393224 | tf_op jit(solution)/shard_map/ppermute | solution.py:528
  129.3 6.2 %collective-permute-start.32 = (bf16[128,512]{1,0:T(8,128)(2,1)S(1)}, bf16[128,512]{1,0:T(8,128)(2,1)S(1)}, u32[]{:S(2)}, u32[]{:S(2)}) collective-permute-start(bf16[128,512]{1,0:T(8,128)(2,1)S(1)} %get-tuple-element.162), channel_id=1, source_target_pairs={{8,0},{12,4},{16,8},{20,12},{24,16},{28,20},{9,1},{13,5},{17,9},{2... | collective-permute-start | bytes 393224 | tf_op jit(solution)/shard_map/ppermute | solution.py:528
  131.2 11.5 %collective-permute-start.33 = (bf16[128,512]{1,0:T(8,128)(2,1)S(1)}, bf16[128,512]{1,0:T(8,128)(2,1)S(1)}, u32[]{:S(2)}, u32[]{:S(2)}) collective-permute-start(bf16[128,512]{1,0:T(8,128)(2,1)S(1)} %get-tuple-element.161), channel_id=1, source_target_pairs={{12,0},{16,4},{20,8},{24,12},{28,16},{13,1},{17,5},{21,9},{25,13},... | collective-permute-start | bytes 393224 | tf_op jit(solution)/shard_map/ppermute | solution.py:528
  134.7 37.5 %collective-permute-start.22 = (bf16[768,768]{1,0:T(8,128)(2,1)S(1)}, bf16[768,768]{1,0:T(8,128)(2,1)}, u32[]{:S(2)}, u32[]{:S(2)}) collective-permute-start(bf16[768,768]{1,0:T(8,128)(2,1)S(1)} %bitcast.341), channel_id=1, source_target_pairs={{0,1},{1,0},{2,3},{3,2},{4,5},{5,4},{6,7},{7,6},{8,9},{9,8},{10,11... | collective-permute-start | bytes 3538952 | tf_op jit(solution)/shard_map/ppermute | solution.py:33
  135.5 36.7 %collective-permute-start.21 = (bf16[768,768]{1,0:T(8,128)(2,1)S(1)}, bf16[768,768]{1,0:T(8,128)(2,1)}, u32[]{:S(2)}, u32[]{:S(2)}) collective-permute-start(bf16[768,768]{1,0:T(8,128)(2,1)S(1)} %bitcast.343), channel_id=1, source_target_pairs={{0,1},{1,0},{2,3},{3,2},{4,5},{5,4},{6,7},{7,6},{8,9},{9,8},{10,11... | collective-permute-start | bytes 3538952 | tf_op jit(solution)/shard_map/ppermute | solution.py:33
  142.8 8.0 %collective-permute-start.34 = (bf16[128,512]{1,0:T(8,128)(2,1)S(1)}, bf16[128,512]{1,0:T(8,128)(2,1)S(1)}, u32[]{:S(2)}, u32[]{:S(2)}) collective-permute-start(bf16[128,512]{1,0:T(8,128)(2,1)S(1)} %get-tuple-element.160), channel_id=1, source_target_pairs={{16,0},{20,4},{24,8},{28,12},{17,1},{21,5},{25,9},{29,13},{18,2},{... | collective-permute-start | bytes 393224 | tf_op jit(solution)/shard_map/ppermute | solution.py:528
  160.7 54.2 %collective-permute-start.48 = (bf16[768,768]{1,0:T(8,128)(2,1)}, bf16[768,768]{1,0:T(8,128)(2,1)}, u32[]{:S(2)}, u32[]{:S(2)}) collective-permute-start(bf16[768,768]{1,0:T(8,128)(2,1)} %get-tuple-element.91), channel_id=1, source_target_pairs={{0,1},{1,0},{2,3},{3,2},{4,5},{5,4},{6,7},{7,6},{8,9},{9,8},{10,11... | collective-permute-start | bytes 3538952 | tf_op jit(solution)/shard_map/ppermute | solution.py:33
  161.6 55.9 %collective-permute-start.45 = (bf16[768,768]{1,0:T(8,128)(2,1)}, bf16[768,768]{1,0:T(8,128)(2,1)S(1)}, u32[]{:S(2)}, u32[]{:S(2)}) collective-permute-start(bf16[768,768]{1,0:T(8,128)(2,1)} %get-tuple-element.89), channel_id=1, source_target_pairs={{0,1},{1,0},{2,3},{3,2},{4,5},{5,4},{6,7},{7,6},{8,9},{9,8},{10,11... | collective-permute-start | bytes 3538952 | tf_op jit(solution)/shard_map/ppermute | solution.py:33
  182.5 37.9 %collective-permute-start.57 = (bf16[768,768]{1,0:T(8,128)(2,1)}, bf16[768,768]{1,0:T(8,128)(2,1)}, u32[]{:S(2)}, u32[]{:S(2)}) collective-permute-start(bf16[768,768]{1,0:T(8,128)(2,1)} %get-tuple-element.95), channel_id=1, source_target_pairs={{0,1},{1,0},{2,3},{3,2},{4,5},{5,4},{6,7},{7,6},{8,9},{9,8},{10,11... | collective-permute-start | bytes 3538952 | tf_op jit(solution)/shard_map/ppermute | solution.py:33
  183.0 39.5 %collective-permute-start.54 = (bf16[768,768]{1,0:T(8,128)(2,1)}, bf16[768,768]{1,0:T(8,128)(2,1)}, u32[]{:S(2)}, u32[]{:S(2)}) collective-permute-start(bf16[768,768]{1,0:T(8,128)(2,1)} %get-tuple-element.93), channel_id=1, source_target_pairs={{0,1},{1,0},{2,3},{3,2},{4,5},{5,4},{6,7},{7,6},{8,9},{9,8},{10,11... | collective-permute-start | bytes 3538952 | tf_op jit(solution)/shard_map/ppermute | solution.py:33
  212.9 14.8 %collective-permute-start.35 = (bf16[4,2,2,56,768]{4,3,2,1,0:T(8,128)(2,1)S(1)}, bf16[4,2,2,56,768]{4,3,2,1,0:T(8,128)(2,1)S(1)}, u32[]{:S(2)}, u32[]{:S(2)}) collective-permute-start(bf16[4,2,2,56,768]{4,3,2,1,0:T(8,128)(2,1)S(1)} %fusion.21), channel_id=1, source_target_pairs={{0,1},{1,0},{2,3},{3,2},{4,5},{5,4},{6,7},{7,6},{8,9},{9,8},{10,11... | collective-permute-start | bytes 4128776 | tf_op jit(solution)/shard_map/ppermute | solution.py:33
  219.6 14.5 %collective-permute-start.49 = (bf16[2,4,48,768]{3,2,1,0:T(8,128)(2,1)S(1)}, bf16[2,4,48,768]{3,2,1,0:T(8,128)(2,1)S(1)}, u32[]{:S(2)}, u32[]{:S(2)}) collective-permute-start(bf16[2,4,48,768]{3,2,1,0:T(8,128)(2,1)S(1)} %fusion.27), channel_id=1, source_target_pairs={{0,4},{4,0},{8,12},{12,8},{16,20},{20,16},{24,28},{28,24},{1,5},{5... | collective-permute-start | bytes 1769480 | tf_op jit(solution)/shard_map/ppermute | solution.py:33
  219.7 15.3 %collective-permute-start.46 = (bf16[2,4,48,768]{3,2,1,0:T(8,128)(2,1)S(1)}, bf16[2,4,48,768]{3,2,1,0:T(8,128)(2,1)S(1)}, u32[]{:S(2)}, u32[]{:S(2)}) collective-permute-start(bf16[2,4,48,768]{3,2,1,0:T(8,128)(2,1)S(1)} %bitcast.356), channel_id=1, source_target_pairs={{0,2},{1,3},{2,0},{3,1},{4,6},{5,7},{6,4},{7,5},{8,10},{9,11},{10,... | collective-permute-start | bytes 1769480 | tf_op jit(solution)/shard_map/ppermute | solution.py:33
  225.8 27.8 %collective-permute-start.58 = (bf16[2,4,48,768]{3,2,1,0:T(8,128)(2,1)S(1)}, bf16[2,4,48,768]{3,2,1,0:T(8,128)(2,1)S(1)}, u32[]{:S(2)}, u32[]{:S(2)}) collective-permute-start(bf16[2,4,48,768]{3,2,1,0:T(8,128)(2,1)S(1)} %fusion.26), channel_id=1, source_target_pairs={{0,4},{4,0},{8,12},{12,8},{16,20},{20,16},{24,28},{28,24},{1,5},{5... | collective-permute-start | bytes 1769480 | tf_op jit(solution)/shard_map/ppermute | solution.py:33
  227.0 27.5 %collective-permute-start.55 = (bf16[2,4,48,768]{3,2,1,0:T(8,128)(2,1)S(1)}, bf16[2,4,48,768]{3,2,1,0:T(8,128)(2,1)S(1)}, u32[]{:S(2)}, u32[]{:S(2)}) collective-permute-start(bf16[2,4,48,768]{3,2,1,0:T(8,128)(2,1)S(1)} %bitcast.355), channel_id=1, source_target_pairs={{0,2},{1,3},{2,0},{3,1},{4,6},{5,7},{6,4},{7,5},{8,10},{9,11},{10,... | collective-permute-start | bytes 1769480 | tf_op jit(solution)/shard_map/ppermute | solution.py:33
  228.5 24.6 %collective-permute-start.38 = (bf16[4,2,24,768]{3,2,1,0:T(8,128)(2,1)S(1)}, bf16[4,2,24,768]{3,2,1,0:T(8,128)(2,1)S(1)}, u32[]{:S(2)}, u32[]{:S(2)}) collective-permute-start(bf16[4,2,24,768]{3,2,1,0:T(8,128)(2,1)S(1)} %fusion.33), channel_id=1, source_target_pairs={{0,4},{4,0},{8,12},{12,8},{16,20},{20,16},{24,28},{28,24},{1,5},{5... | collective-permute-start | bytes 884744 | tf_op jit(solution)/shard_map/ppermute | solution.py:33
  234.2 21.3 %collective-permute-start.36 = (bf16[4,2,32,768]{3,2,1,0:T(8,128)(2,1)S(1)}, bf16[4,2,32,768]{3,2,1,0:T(8,128)(2,1)S(1)}, u32[]{:S(2)}, u32[]{:S(2)}) collective-permute-start(bf16[4,2,32,768]{3,2,1,0:T(8,128)(2,1)S(1)} %fusion.32), channel_id=1, source_target_pairs={{0,2},{1,3},{2,0},{3,1},{4,6},{5,7},{6,4},{7,5},{8,10},{9,11},{10,... | collective-permute-start | bytes 1179656 | tf_op jit(solution)/shard_map/ppermute | solution.py:33
  235.0 30.9 %collective-permute-start.50 = (bf16[4,48,768]{2,1,0:T(8,128)(2,1)S(1)}, bf16[4,48,768]{2,1,0:T(8,128)(2,1)S(1)}, u32[]{:S(2)}, u32[]{:S(2)}) collective-permute-start(bf16[4,48,768]{2,1,0:T(8,128)(2,1)S(1)} %fusion.35), channel_id=1, source_target_pairs={{0,2},{1,3},{2,0},{3,1},{4,6},{5,7},{6,4},{7,5},{8,10},{9,11},{10,... | collective-permute-start | bytes 884744 | tf_op jit(solution)/shard_map/ppermute | solution.py:33
  253.1 12.8 %collective-permute-start.47 = (bf16[4,48,768]{2,1,0:T(8,128)(2,1)S(1)}, bf16[4,48,768]{2,1,0:T(8,128)(2,1)S(1)}, u32[]{:S(2)}, u32[]{:S(2)}) collective-permute-start(bf16[4,48,768]{2,1,0:T(8,128)(2,1)S(1)} %fusion.34), channel_id=1, source_target_pairs={{0,4},{4,0},{8,12},{12,8},{16,20},{20,16},{24,28},{28,24},{1,5},{5... | collective-permute-start | bytes 884744 | tf_op jit(solution)/shard_map/ppermute | solution.py:33
  253.6 11.2 %collective-permute-start.39 = (bf16[4,24,768]{2,1,0:T(8,128)(2,1)S(1)}, bf16[4,24,768]{2,1,0:T(8,128)(2,1)S(1)}, u32[]{:S(2)}, u32[]{:S(2)}) collective-permute-start(bf16[4,24,768]{2,1,0:T(8,128)(2,1)S(1)} %fusion.63), channel_id=1, source_target_pairs={{0,2},{1,3},{2,0},{3,1},{4,6},{5,7},{6,4},{7,5},{8,10},{9,11},{10,... | collective-permute-start | bytes 442376 | tf_op jit(solution)/shard_map/ppermute | solution.py:33
  254.5 39.3 %collective-permute-start.59 = (bf16[4,48,768]{2,1,0:T(8,128)(2,1)S(1)}, bf16[4,48,768]{2,1,0:T(8,128)(2,1)S(1)}, u32[]{:S(2)}, u32[]{:S(2)}) collective-permute-start(bf16[4,48,768]{2,1,0:T(8,128)(2,1)S(1)} %fusion.37), channel_id=1, source_target_pairs={{0,2},{1,3},{2,0},{3,1},{4,6},{5,7},{6,4},{7,5},{8,10},{9,11},{10,... | collective-permute-start | bytes 884744 | tf_op jit(solution)/shard_map/ppermute | solution.py:33
  255.5 38.3 %collective-permute-start.56 = (bf16[4,48,768]{2,1,0:T(8,128)(2,1)S(1)}, bf16[4,48,768]{2,1,0:T(8,128)(2,1)S(1)}, u32[]{:S(2)}, u32[]{:S(2)}) collective-permute-start(bf16[4,48,768]{2,1,0:T(8,128)(2,1)S(1)} %fusion.36), channel_id=1, source_target_pairs={{0,4},{4,0},{8,12},{12,8},{16,20},{20,16},{24,28},{28,24},{1,5},{5... | collective-permute-start | bytes 884744 | tf_op jit(solution)/shard_map/ppermute | solution.py:33
  264.8 6.2 %collective-permute-start.37 = (bf16[4,32,768]{2,1,0:T(8,128)(2,1)S(1)}, bf16[4,32,768]{2,1,0:T(8,128)(2,1)S(1)}, u32[]{:S(2)}, u32[]{:S(2)}) collective-permute-start(bf16[4,32,768]{2,1,0:T(8,128)(2,1)S(1)} %fusion.50), channel_id=1, source_target_pairs={{0,4},{4,0},{8,12},{12,8},{16,20},{20,16},{24,28},{28,24},{1,5},{5... | collective-permute-start | bytes 589832 | tf_op jit(solution)/shard_map/ppermute | solution.py:33
  272.4 4.4 %collective-permute-start.41 = (bf16[56,768]{1,0:T(8,128)(2,1)S(1)}, bf16[56,768]{1,0:T(8,128)(2,1)S(1)}, u32[]{:S(2)}, u32[]{:S(2)}) collective-permute-start(bf16[56,768]{1,0:T(8,128)(2,1)S(1)} %get-tuple-element.129), channel_id=1, source_target_pairs={{0,16},{4,20},{8,24},{12,28},{16,0},{20,4},{24,8},{28,12},{1,17},{... | collective-permute-start | bytes 258056 | tf_op jit(solution)/shard_map/ppermute | solution.py:47
  272.4 6.1 %collective-permute-start.42 = (bf16[56,768]{1,0:T(8,128)(2,1)S(1)}, bf16[56,768]{1,0:T(8,128)(2,1)S(1)}, u32[]{:S(2)}, u32[]{:S(2)}) collective-permute-start(bf16[56,768]{1,0:T(8,128)(2,1)S(1)} %get-tuple-element.130), channel_id=1, source_target_pairs={{0,24},{4,28},{8,16},{12,20},{16,8},{20,12},{24,0},{28,4},{1,25},{... | collective-permute-start | bytes 258056 | tf_op jit(solution)/shard_map/ppermute | solution.py:47
  274.5 7.0 %collective-permute-start.51 = (bf16[96,768]{1,0:T(8,128)(2,1)S(1)}, bf16[96,768]{1,0:T(8,128)(2,1)S(1)}, u32[]{:S(2)}, u32[]{:S(2)}) collective-permute-start(bf16[96,768]{1,0:T(8,128)(2,1)S(1)} %get-tuple-element.133), channel_id=1, source_target_pairs={{0,8},{4,12},{8,0},{12,4},{16,24},{20,28},{24,16},{28,20},{1,9},{5... | collective-permute-start | bytes 442376 | tf_op jit(solution)/shard_map/ppermute | solution.py:47
  276.8 8.8 %collective-permute-start.52 = (bf16[96,768]{1,0:T(8,128)(2,1)S(1)}, bf16[96,768]{1,0:T(8,128)(2,1)S(1)}, u32[]{:S(2)}, u32[]{:S(2)}) collective-permute-start(bf16[96,768]{1,0:T(8,128)(2,1)S(1)} %get-tuple-element.135), channel_id=1, source_target_pairs={{0,16},{4,20},{8,24},{12,28},{16,0},{20,4},{24,8},{28,12},{1,17},{... | collective-permute-start | bytes 442376 | tf_op jit(solution)/shard_map/ppermute | solution.py:47
  278.5 15.2 %collective-permute-start.53 = (bf16[96,768]{1,0:T(8,128)(2,1)S(1)}, bf16[96,768]{1,0:T(8,128)(2,1)S(1)}, u32[]{:S(2)}, u32[]{:S(2)}) collective-permute-start(bf16[96,768]{1,0:T(8,128)(2,1)S(1)} %get-tuple-element.134), channel_id=1, source_target_pairs={{0,24},{4,28},{8,16},{12,20},{16,8},{20,12},{24,0},{28,4},{1,25},{... | collective-permute-start | bytes 442376 | tf_op jit(solution)/shard_map/ppermute | solution.py:47
  281.5 29.0 %collective-permute-start.43 = (bf16[56,768]{1,0:T(8,128)(2,1)S(1)}, bf16[56,768]{1,0:T(8,128)(2,1)S(1)}, u32[]{:S(2)}, u32[]{:S(2)}) collective-permute-start(bf16[56,768]{1,0:T(8,128)(2,1)S(1)} %fusion.58), channel_id=1, source_target_pairs={{0,2},{1,3},{2,0},{3,1},{4,6},{5,7},{6,4},{7,5},{8,10},{9,11},{10,... | collective-permute-start | bytes 258056 | tf_op jit(solution)/shard_map/ppermute | solution.py:33
  294.0 4.1 %collective-permute-start.60 = (bf16[96,768]{1,0:T(8,128)(2,1)S(1)}, bf16[96,768]{1,0:T(8,128)(2,1)S(1)}, u32[]{:S(2)}, u32[]{:S(2)}) collective-permute-start(bf16[96,768]{1,0:T(8,128)(2,1)S(1)} %get-tuple-element.136), channel_id=1, source_target_pairs={{0,8},{4,12},{8,0},{12,4},{16,24},{20,28},{24,16},{28,20},{1,9},{5... | collective-permute-start | bytes 442376 | tf_op jit(solution)/shard_map/ppermute | solution.py:47
  294.1 6.0 %collective-permute-start.61 = (bf16[96,768]{1,0:T(8,128)(2,1)S(1)}, bf16[96,768]{1,0:T(8,128)(2,1)S(1)}, u32[]{:S(2)}, u32[]{:S(2)}) collective-permute-start(bf16[96,768]{1,0:T(8,128)(2,1)S(1)} %get-tuple-element.138), channel_id=1, source_target_pairs={{0,16},{4,20},{8,24},{12,28},{16,0},{20,4},{24,8},{28,12},{1,17},{... | collective-permute-start | bytes 442376 | tf_op jit(solution)/shard_map/ppermute | solution.py:47
  295.6 14.1 %collective-permute-start.62 = (bf16[96,768]{1,0:T(8,128)(2,1)S(1)}, bf16[96,768]{1,0:T(8,128)(2,1)S(1)}, u32[]{:S(2)}, u32[]{:S(2)}) collective-permute-start(bf16[96,768]{1,0:T(8,128)(2,1)S(1)} %get-tuple-element.137), channel_id=1, source_target_pairs={{0,24},{4,28},{8,16},{12,20},{16,8},{20,12},{24,0},{28,4},{1,25},{... | collective-permute-start | bytes 442376 | tf_op jit(solution)/shard_map/ppermute | solution.py:47
  309.8 7.2 %collective-permute-start.63 = (bf16[192,768]{1,0:T(8,128)(2,1)S(1)}, bf16[192,768]{1,0:T(8,128)(2,1)S(1)}, u32[]{:S(2)}, u32[]{:S(2)}) collective-permute-start(bf16[192,768]{1,0:T(8,128)(2,1)S(1)} %pad_maximum_fusion.23), channel_id=1, source_target_pairs={{0,2},{1,3},{2,0},{3,1},{4,6},{5,7},{6,4},{7,5},{8,10},{9,11},{10,... | collective-permute-start | bytes 884744 | tf_op jit(solution)/shard_map/ppermute | solution.py:33
  310.5 9.0 %collective-permute-start.44 = (bf16[2,56,768]{2,1,0:T(8,128)(2,1)S(1)}, bf16[2,56,768]{2,1,0:T(8,128)(2,1)S(1)}, u32[]{:S(2)}, u32[]{:S(2)}) collective-permute-start(bf16[2,56,768]{2,1,0:T(8,128)(2,1)S(1)} %pad_maximum_fusion.24), channel_id=1, source_target_pairs={{0,1},{1,0},{2,3},{3,2},{4,5},{5,4},{6,7},{7,6},{8,9},{9,8},{10,11... | collective-permute-start | bytes 516104 | tf_op jit(solution)/shard_map/ppermute | solution.py:33
  317.1 13.6 %collective-permute-start.64 = (bf16[2,192,768]{2,1,0:T(8,128)(2,1)S(1)}, bf16[2,192,768]{2,1,0:T(8,128)(2,1)S(1)}, u32[]{:S(2)}, u32[]{:S(2)}) collective-permute-start(bf16[2,192,768]{2,1,0:T(8,128)(2,1)S(1)} %pad_maximum_fusion.18), channel_id=1, source_target_pairs={{0,1},{1,0},{2,3},{3,2},{4,5},{5,4},{6,7},{7,6},{8,9},{9,8},{10,11... | collective-permute-start | bytes 1769480 | tf_op jit(solution)/shard_map/ppermute | solution.py:33
  (38 other events, 373.2 us)
